TPU v7x, 256 devices: a whole 4x4x8 slice. The times are simulated.
256 devices in a mesh: ctx: 32 (over y, z), head: 8 (over x, core).
Axes of the slice: x: 4, y: 4, z: 8, core: 2. Of those that a mesh axis runs over, the one named last changes fastest.
Arguments:
- hidden: bfloat16 [512, 4096], P('head', 'ctx'), may hold values from -60 to 60
- norm_gain: float32 [4096], P('ctx'), may hold values from 0.1 to 1.9
- w_qkv: bfloat16 [4096, 6144], P('ctx'), may hold values from -0.09375 to 0.09375
- positions: int32 [512], replicated, may hold values from 0 to 1022, as said below
- cache_keys: bfloat16 [131072, 1024], P('ctx', 'head'), may hold values from -450 to 450
- cache_values: bfloat16 [131072, 1024], P('ctx', 'head'), may hold values from -6 to 6
- key_counts: int32 [32], P('ctx'), may hold values from 2048 to 4096, as said below
- w_out: bfloat16 [4096, 4096], P('head', 'ctx'), may hold values from -6 to 6
Outputs:
- attn_proj: bfloat16 [512, 4096], P('head', 'ctx')
Inputs may be any that keep to these rules, and one draw needn't show every extreme that they name: Rows of the question have positions that start at 0 and rise by 1 to 3 from one row to the next; the last row stands at position 1022; cached keys were rotated at positions relative to the same anchor. In context block c only the first key_counts[c] of its 4096 rows are valid; in every draw some block is full.
All inputs are finite; a program needn't handle non-finite values.
Results may differ from a plain program's by a relative error of at most 0.0055.
The roundings to bfloat16 on the way count: a program that leaves them out, or rounds other values in their place, can miss the bound.
Values may be sent and summed in bfloat16 or wider, within the bound.
No kernel may reach another device: no remote copies, remote signals or barrier semaphores. Data moves between devices by JAX's collectives and lax.ppermute only.
A program may use at most 64 MiB of HBM per device.

v0:
```python
import math

import jax
import jax.numpy as jnp
from jax import lax
from jax.sharding import PartitionSpec as P

D = 4096
HEADS = 32
KV_HEADS = 8
HEAD_DIM = 128


NEG_FILL = -1e30


def copy_for_each(array, axis):
    copies = jnp.broadcast_to(array, (lax.axis_size(axis), *array.shape))
    return lax.all_to_all(copies, axis, split_axis=0, concat_axis=0, tiled=True)


def taken_together(array, axis):
    everything = copy_for_each(array, axis)
    return jnp.sum(everything, axis=0)


def cut_along(array, dim, length):
    before, after = (array.shape[:dim], array.shape[dim + 1 :])
    return jnp.moveaxis(array.reshape(*before, length, -1, *after), dim, 0)


def sent_and_summed(array, axis, dim):
    length = lax.axis_size(axis)
    tiles = lax.all_to_all(cut_along(array, dim, length), axis, 0, 0, tiled=True)
    return jnp.sum(tiles, axis=0)


def laid_out(tiles, dim):
    lengths = list(tiles.shape[1:])
    lengths[dim] *= tiles.shape[0]
    return jnp.moveaxis(tiles, 0, dim).reshape(lengths)


def collect(array, axis, dim):
    tiles = copy_for_each(array, axis)
    return laid_out(tiles, dim)


def over_copies(array, axis):
    everything = copy_for_each(array, axis)
    return jnp.max(everything, axis=0)


def side_by_side(arrays, axis, dim, along):
    widths = [math.prod(a.shape[along:]) for a in arrays]
    both = jnp.concatenate(
        [a.reshape(*a.shape[:along], w) for a, w in zip(arrays, widths)], axis=along
    )
    filled = sent_and_summed(both, axis, dim)
    tiles = jnp.split(filled, [sum(widths[:k]) for k in range(1, len(widths))], axis=along)
    return tuple(
        (b.reshape(*filled.shape[:along], *a.shape[along:]) for a, b in zip(arrays, tiles))
    )


def rotate(values_in, positions_in):
    half_dim = values_in.shape[-1] // 2
    frequency = 500000.0 ** (-(jnp.arange(half_dim, dtype=jnp.float32) * 2.0 / values_in.shape[-1]))
    angles = positions_in.astype(jnp.float32)[:, None] * frequency[None, :]
    angles = angles.reshape((angles.shape[0],) + (1,) * (values_in.ndim - 2) + (half_dim,))
    cosine = jnp.cos(angles)
    sine_val = jnp.sin(angles)
    first_half = values_in[..., :half_dim]
    second = values_in[..., half_dim:]
    return jnp.concatenate(
        [first_half * cosine - second * sine_val, second * cosine + first_half * sine_val], axis=-1
    )


def rotate_slots(mixed_cols, positions_in, group_size):
    turned = rotate(mixed_cols[:, :, : group_size + 1], positions_in)
    return jnp.concatenate([turned, mixed_cols[:, :, group_size + 1 :]], axis=2)


def attend(query_block, key_block, value_block, new_keys, new_values, cache_mask, self_mask):
    score_scale = 1.0 / math.sqrt(query_block.shape[-1])
    score_cache = (
        jnp.einsum("tagh,kah->tagk", query_block, key_block, preferred_element_type=jnp.float32)
        * score_scale
    )
    score_self = (
        jnp.einsum("tagh,uah->tagu", query_block, new_keys, preferred_element_type=jnp.float32)
        * score_scale
    )
    score_cache = jnp.where(cache_mask[None, None, None, :], score_cache, NEG_FILL)
    score_self = jnp.where(self_mask[:, None, None, :], score_self, NEG_FILL)
    row_max = jnp.maximum(jnp.max(score_cache, axis=-1), jnp.max(score_self, axis=-1))
    exp_cache = jnp.exp(score_cache - row_max[..., None]).astype(jnp.bfloat16)
    exp_self = jnp.exp(score_self - row_max[..., None]).astype(jnp.bfloat16)
    totals = jnp.sum(exp_cache, axis=-1, dtype=jnp.float32) + jnp.sum(
        exp_self, axis=-1, dtype=jnp.float32
    )
    weighted = jnp.einsum(
        "tagk,kah->tagh", exp_cache, value_block, preferred_element_type=jnp.float32
    )
    weighted = weighted + jnp.einsum(
        "tagu,uah->tagh", exp_self, new_values, preferred_element_type=jnp.float32
    )
    return (row_max, totals, weighted)


def per_device(hidden, norm_gain, w_qkv, positions, cache_keys, cache_values, key_counts, w_out):
    row_count = hidden.shape[0]
    head_count = lax.axis_size("head")
    total_rows = row_count * head_count
    group_size = HEADS // KV_HEADS
    slot_count = group_size + 2
    local_groups = KV_HEADS // head_count
    hidden_f = hidden.astype(jnp.float32)
    square_total = taken_together(jnp.sum(hidden_f * hidden_f, axis=1), "ctx")
    inv_rms = lax.rsqrt(square_total / D + 1e-05)
    scaled = (hidden_f * norm_gain[None, :]).astype(jnp.bfloat16)
    partial_mix = jnp.dot(scaled, w_qkv, preferred_element_type=jnp.float32)
    scaled_mix = partial_mix * inv_rms[:, None]
    moved = lax.all_to_all(scaled_mix, "head", split_axis=1, concat_axis=0, tiled=True)
    share = sent_and_summed(moved, "ctx", 0)
    share_rows = share.shape[0]
    share_positions = lax.dynamic_slice_in_dim(
        positions, lax.axis_index("ctx") * share_rows, share_rows
    )
    share = share.reshape(share_rows, local_groups, slot_count, HEAD_DIM)
    turned_share = rotate_slots(share, share_positions, group_size).astype(jnp.bfloat16)
    turned_share = turned_share.reshape(share_rows, local_groups * slot_count * HEAD_DIM)
    grouped = collect(turned_share, "ctx", 0)
    grouped = grouped.reshape(total_rows, local_groups, slot_count, HEAD_DIM)
    queries = grouped[:, :, :group_size]
    new_keys = grouped[:, :, group_size]
    new_values = grouped[:, :, group_size + 1]
    key_rows = cache_keys.shape[0]
    key_block = cache_keys.reshape(key_rows, local_groups, HEAD_DIM)
    value_block = cache_values.reshape(key_rows, local_groups, HEAD_DIM)
    cache_mask = jnp.arange(key_rows, dtype=jnp.int32) < key_counts[0]
    first_group = lax.axis_index("ctx") == 0
    block_rows = math.gcd(total_rows, 128)
    block_count = total_rows // block_rows
    query_blocks = queries.reshape(block_count, block_rows, local_groups, group_size, HEAD_DIM)
    block_starts = jnp.arange(block_count, dtype=jnp.int32) * block_rows

    def one_block(block_args):
        query_block, row_start = block_args
        rows_here = row_start + jnp.arange(block_rows, dtype=jnp.int32)
        self_mask = (
            jnp.arange(total_rows, dtype=jnp.int32)[None, :] <= rows_here[:, None]
        ) & first_group
        return attend(
            query_block, key_block, value_block, new_keys, new_values, cache_mask, self_mask
        )

    part_max, part_sum, part_out = lax.map(one_block, (query_blocks, block_starts))
    part_max = part_max.reshape(total_rows, local_groups, group_size)
    part_sum = part_sum.reshape(total_rows, local_groups, group_size)
    part_out = part_out.reshape(total_rows, local_groups, group_size, HEAD_DIM)
    flat_width = local_groups * group_size * HEAD_DIM
    final_max = over_copies(part_max, "ctx")
    factor = jnp.exp(part_max - final_max)
    sum_share, out_share = side_by_side(
        (part_sum * factor, part_out * factor[..., None]), "ctx", 0, 3
    )
    attended_share = (out_share / sum_share[..., None]).astype(jnp.bfloat16)
    attended_share = attended_share.reshape(sum_share.shape[0], flat_width)
    attended = lax.all_gather(attended_share, "ctx", axis=0, tiled=True)
    result = lax.psum_scatter(
        jnp.dot(attended, w_out, preferred_element_type=jnp.float32),
        "head",
        scatter_dimension=0,
        tiled=True,
    )
    return result.astype(jnp.bfloat16)


def solution(mesh):
    return jax.shard_map(
        per_device,
        mesh=mesh,
        in_specs=(
            P("head", "ctx"),
            P("ctx"),
            P("ctx", None),
            P(),
            P("ctx", "head"),
            P("ctx", "head"),
            P("ctx"),
            P("head", "ctx"),
        ),
        out_specs=P("head", "ctx"),
        check_vma=False,
    )
```

profile of v0, /device:TPU:1, one launch (start us, length us, event | category | flops | bytes accessed | tf_op | source)
XLA Modules:
  0.0 354.3 jit_solution(3599179839066834852)
XLA Ops:
  6.5 0.9 fusion.20
  7.5 20.5 %all_to_all.42 = f32[32,1,64]{2,1,0:T(1,128)S(1)} all-to-all(f32[32,1,64]{2,1,0:T(1,128)S(1)} %broadcast_in_dim.55), channel_id=1, replica_groups=mesh['ctx'=32,'head'=8] {'ctx'}, dimensions={0} | all-to-all | bytes 16384 | tf_op jit(solution)/shard_map/all_to_all | solution.py:19
  28.0 1.1 convolution_multiply_fusion.1
  29.2 27.1 %all_to_all.43 = f32[64,8,768]{2,0,1:T(8,128)} all-to-all(f32[64,8,768]{2,0,1:T(8,128)S(1)} %bitcast.168), channel_id=1, replica_groups=mesh['ctx'=32,'head'=8] {'head'}, dimensions={1} | all-to-all | bytes 3145728 | tf_op jit(solution)/shard_map/all_to_all | solution.py:125
  56.3 4.0 %all-to-all-start.2 = ((f32[32,16,768]{2,1,0:T(8,128)}), f32[32,16,768]{2,1,0:T(8,128)S(1)}, u32[]{:S(2)}, u32[]{:S(2)}) async-start(f32[32,16,768]{2,1,0:T(8,128)} %bitcast.166), calls=%async_computation.2 | async-start | bytes 3145728 | tf_op jit(solution)/shard_map/all_to_all | solution.py:34
  60.3 0.8 dynamic-slice_convert_fusion
  61.2 35.8 %all-to-all-done.2 = f32[32,16,768]{2,1,0:T(8,128)S(1)} async-done(((f32[32,16,768]{2,1,0:T(8,128)}), f32[32,16,768]{2,1,0:T(8,128)S(1)}, u32[]{:S(2)}, u32[]{:S(2)}) %all-to-all-start.2) | async-done | bytes 1572896 | tf_op jit(solution)/shard_map/all_to_all | solution.py:34
  97.3 0.9 broadcast_in_dim.56
  98.3 7.7 %all-to-all-start.3 = ((bf16[32,16,768]{2,1,0:T(8,128)(2,1)}), bf16[32,16,768]{2,1,0:T(8,128)(2,1)S(1)}, u32[]{:S(2)}, u32[]{:S(2)}) async-start(bf16[32,16,768]{2,1,0:T(8,128)(2,1)} %broadcast_in_dim.56), calls=%async_computation.3 | async-start | bytes 1572864 | tf_op jit(solution)/shard_map/all_to_all | solution.py:19
  106.0 19.7 %all-to-all-done.3 = bf16[32,16,768]{2,1,0:T(8,128)(2,1)S(1)} async-done(((bf16[32,16,768]{2,1,0:T(8,128)(2,1)}), bf16[32,16,768]{2,1,0:T(8,128)(2,1)S(1)}, u32[]{:S(2)}, u32[]{:S(2)}) %all-to-all-start.3) | async-done | bytes 786464 | tf_op jit(solution)/shard_map/all_to_all | solution.py:19
  125.8 0.9 reshape_reshape.3
  127.4 62.1 %while.15 = (s32[]{:T(128)}, f32[4,128,1,4]{1,3,2,0:T(4,128)S(1)}, f32[4,128,1,4]{1,0,3,2:T(4,128)S(1)}, f32[4,128,1,4,128]{4,1,0,3,2:T(8,128)}, bf16[4,128,1,4,...) while((s32[]{:T(128)}, f32[4,128,1,4]{1,3,2,0:T(4,128)S(1)}, ...), condition=%wide.region_8.9_spmd.clone, body=%wide.region_3.8_spmd.clone.sunk | while | flops 1237781632 | bytes 65719500 | solution.py:159
  128.1 2.7 fusion.43
  130.9 0.7 dynamic_slice.19
  132.8 1.2 copy-done.1
  134.1 2.0 convert_reduce_fusion.4
  136.5 5.4 %fusion.46 = f32[128,4,128]{2,0,1:T(8,128)S(1)} fusion(bf16[4096,1,128]{2,0,1:T(8,128)(2,1)} %get-tuple-element.331, f32[128,4,4096]{2,0,1:T(8,128)} %copy-done.1, f32[128,4]{0,1:T(4,128)S(1)} %get-tuple-element.291, pred[4096]{0:T(1024)(128)(4,1)S(1)} %iota_compare_fusion.3), kind=kOutput, calls=%fused_computation.6.clone.1 | convolution fusion | flops 545259520 | bytes 9705472 | tf_op jit(solution)/shard_map/while/body/eval_jaxpr/tagk,kah->tagh/dot_general | solution.py:103
  141.8 1.1 fusion.47
  143.6 2.7 fusion.43
  146.4 0.7 dynamic_slice.19
  148.4 1.2 copy-done.1
  149.6 2.0 convert_reduce_fusion.4
  152.0 5.4 %fusion.46 = f32[128,4,128]{2,0,1:T(8,128)S(1)} fusion(bf16[4096,1,128]{2,0,1:T(8,128)(2,1)} %get-tuple-element.331, f32[128,4,4096]{2,0,1:T(8,128)} %copy-done.1, f32[128,4]{0,1:T(4,128)S(1)} %get-tuple-element.291, pred[4096]{0:T(1024)(128)(4,1)S(1)} %iota_compare_fusion.3), kind=kOutput, calls=%fused_computation.6.clone.1 | convolution fusion | flops 545259520 | bytes 9705472 | tf_op jit(solution)/shard_map/while/body/eval_jaxpr/tagk,kah->tagh/dot_general | solution.py:103
  157.4 1.1 fusion.47
  159.2 2.7 fusion.43
  161.9 0.7 dynamic_slice.19
  163.9 1.2 copy-done.1
  165.1 2.0 convert_reduce_fusion.4
  167.5 5.4 %fusion.46 = f32[128,4,128]{2,0,1:T(8,128)S(1)} fusion(bf16[4096,1,128]{2,0,1:T(8,128)(2,1)} %get-tuple-element.331, f32[128,4,4096]{2,0,1:T(8,128)} %copy-done.1, f32[128,4]{0,1:T(4,128)S(1)} %get-tuple-element.291, pred[4096]{0:T(1024)(128)(4,1)S(1)} %iota_compare_fusion.3), kind=kOutput, calls=%fused_computation.6.clone.1 | convolution fusion | flops 545259520 | bytes 9705472 | tf_op jit(solution)/shard_map/while/body/eval_jaxpr/tagk,kah->tagh/dot_general | solution.py:103
  172.9 1.1 fusion.47
  174.7 2.7 fusion.43
  177.4 0.7 dynamic_slice.19
  178.2 0.7 iota_add_fusion.2
  179.4 1.2 copy-done.1
  180.7 2.0 convert_reduce_fusion.4
  183.1 5.4 %fusion.46 = f32[128,4,128]{2,0,1:T(8,128)S(1)} fusion(bf16[4096,1,128]{2,0,1:T(8,128)(2,1)} %get-tuple-element.331, f32[128,4,4096]{2,0,1:T(8,128)} %copy-done.1, f32[128,4]{0,1:T(4,128)S(1)} %get-tuple-element.291, pred[4096]{0:T(1024)(128)(4,1)S(1)} %iota_compare_fusion.3), kind=kOutput, calls=%fused_computation.6.clone.1 | convolution fusion | flops 545259520 | bytes 9705472 | tf_op jit(solution)/shard_map/while/body/eval_jaxpr/tagk,kah->tagh/dot_general | solution.py:103
  188.4 1.1 fusion.47
  189.5 0.7 broadcast_in_dim.57
  190.2 7.5 %all-to-all-start.4 = ((f32[32,512,1,4]{1,3,2,0:T(4,128)}), f32[32,512,1,4]{1,3,2,0:T(4,128)S(1)}, u32[]{:S(2)}, u32[]{:S(2)}) async-start(f32[32,512,1,4]{1,3,2,0:T(4,128)} %broadcast_in_dim.57), calls=%async_computation.4 | async-start | bytes 524288 | tf_op jit(solution)/shard_map/all_to_all | solution.py:19
  198.3 9.2 %all-to-all-done.4 = f32[32,512,1,4]{1,3,2,0:T(4,128)S(1)} async-done(((f32[32,512,1,4]{1,3,2,0:T(4,128)}), f32[32,512,1,4]{1,3,2,0:T(4,128)S(1)}, u32[]{:S(2)}, u32[]{:S(2)}) %all-to-all-start.4) | async-done | bytes 262176 | tf_op jit(solution)/shard_map/all_to_all | solution.py:19
  207.7 0.8 copy.72
  208.5 1.6 broadcast_multiply_fusion
  211.0 52.4 %all_to_all.44 = f32[32,16,1,4,129]{4,1,3,2,0:T(8,128)} all-to-all(f32[32,16,1,4,129]{4,1,3,2,0:T(8,128)S(1)} %copy.73), channel_id=1, replica_groups=mesh['ctx'=32,'head'=8] {'ctx'}, dimensions={0} | all-to-all | bytes 2113536 | tf_op jit(solution)/shard_map/all_to_all | solution.py:34
  263.5 1.8 reduce_sum.59
  265.4 37.5 %all_gather.3 = bf16[512,512]{1,0:T(8,128)(2,1)S(1)} all-gather(bf16[16,512]{1,0:T(8,128)(2,1)S(1)} %bitcast.176), channel_id=1, replica_groups=mesh['ctx'=32,'head'=8] {'ctx'}, dimensions={0}, use_global_device_ids=true | all-gather | bytes 540672 | tf_op jit(solution)/shard_map/all_gather | solution.py:171
  302.9 1.0 fusion.26
  303.9 42.2 %reduce-scatter.2.cloned.1.call-done = f32[64,128]{1,0:T(8,128)} async-done(((f32[512,128]{1,0:T(8,128)}), f32[64,128]{1,0:T(8,128)}) %reduce-scatter.2.cloned.1.call-update) | async-done | bytes 32784 | tf_op jit(solution)/shard_map/reduce_scatter | solution.py:172
  346.1 1.4 convert_element_type.39
  (79 shorter events, 11.7 us)
Async XLA Ops:
  6.5 21.5 %copy-start = (bf16[128,6144]{1,0:T(8,128)(2,1)S(1)}, bf16[128,6144]{1,0:T(8,128)(2,1)}, u32[]{:S(2)}) copy-start(bf16[128,6144]{1,0:T(8,128)(2,1)} %param.12) | copy-start | bytes 4718596
  56.3 40.7 %all-to-all-start.2 = ((f32[32,16,768]{2,1,0:T(8,128)}), f32[32,16,768]{2,1,0:T(8,128)S(1)}, u32[]{:S(2)}, u32[]{:S(2)}) async-start(f32[32,16,768]{2,1,0:T(8,128)} %bitcast.166), calls=%async_computation.2 | async-start | bytes 3145728 | tf_op jit(solution)/shard_map/all_to_all | solution.py:34
  98.3 27.5 %all-to-all-start.3 = ((bf16[32,16,768]{2,1,0:T(8,128)(2,1)}), bf16[32,16,768]{2,1,0:T(8,128)(2,1)S(1)}, u32[]{:S(2)}, u32[]{:S(2)}) async-start(bf16[32,16,768]{2,1,0:T(8,128)(2,1)} %broadcast_in_dim.56), calls=%async_computation.3 | async-start | bytes 1572864 | tf_op jit(solution)/shard_map/all_to_all | solution.py:19
  130.8 3.2 copy-start.1
  146.4 3.2 copy-start.1
  161.9 3.2 copy-start.1
  177.4 3.2 copy-start.1
  190.2 17.2 %all-to-all-start.4 = ((f32[32,512,1,4]{1,3,2,0:T(4,128)}), f32[32,512,1,4]{1,3,2,0:T(4,128)S(1)}, u32[]{:S(2)}, u32[]{:S(2)}) async-start(f32[32,512,1,4]{1,3,2,0:T(4,128)} %broadcast_in_dim.57), calls=%async_computation.4 | async-start | bytes 524288 | tf_op jit(solution)/shard_map/all_to_all | solution.py:19
  197.8 148.3 %reduce-scatter.2.cloned.1.call-start = ((), (), s32[]{:S(2)}) async-start(), calls=%async_computation.7 | async-start | bytes 294912 | tf_op jit(solution)/shard_map/reduce_scatter | solution.py:172
  208.5 94.4 %copy-start.2 = (bf16[512,128]{1,0:T(8,128)(2,1)S(1)}, bf16[512,128]{1,0:T(8,128)(2,1)}, u32[]{:S(2)}) copy-start(bf16[512,128]{1,0:T(8,128)(2,1)} %param.17) | copy-start | bytes 393220
Sparse Core Ops, SparseCore 0:
  304.1 41.9 reduce-scatter.1
where the time goes:
time: 357 us; the launch traced here: 354 us
  blocking collectives  137 us (38%)
  waiting for transfers between devices  107 us (30%)
  matrix products  40.3 us (11%)
  other arithmetic  23 us (6%)
  starting transfers between devices  19.4 us (5%)
  between operations  13.7 us (4%)
  local copies, waits for them, and re-layouts  13.3 us (4%)
    all_to_all x1, blocking collectives, sent_and_summed(): lax.all_to_all(cut_along(array, dim, length), axis, 0, 0, tiled=True)  52.4 us
    reduce_scatter x1, waiting for transfers between devices, per_device(): lax.psum_scatter(jnp.dot(attended, w_out, preferred_element_type=jnp.floa...  42.2 us
    all_gather x1, blocking collectives, per_device(): attended = lax.all_gather(attended_share, 'ctx', axis=0, tiled=True)  37.5 us
    all_to_all x1, waiting for transfers between devices, sent_and_summed(): lax.all_to_all(cut_along(array, dim, length), axis, 0, 0, tiled=True)  35.8 us
    all_to_all x2, waiting for transfers between devices, copy_for_each(): return lax.all_to_all(copies, axis, split_axis=0, concat_axis=0, tiled=True)  28.9 us
    all_to_all x1, blocking collectives, per_device(): lax.all_to_all(scaled_mix, 'head', split_axis=1, concat_axis=0, tiled=True)  27.1 us
    dot_general x4, matrix products, attend(): jnp.einsum('tagk,kah->tagh', exp_cache, value_block, preferred_element_ty...  21.4 us
    all_to_all x1, blocking collectives, copy_for_each(): return lax.all_to_all(copies, axis, split_axis=0, concat_axis=0, tiled=True)  20.5 us
  transfers between devices with their start and end apart: 4, of which 4 were waited for; matrix products, arithmetic and copies ran while one was open for 0% of the time, Pallas kernels for 0%

commit v1 on v0

v1 whole, which is shorter than its diff:
```python
import functools
import math

import jax
import jax.numpy as jnp
from jax import lax
from jax.experimental import pallas as pl
from jax.experimental.pallas import tpu as pltpu
from jax.sharding import Mesh
from jax.sharding import PartitionSpec as P

D = 4096
HEADS = 32
KV_HEADS = 8
HEAD_DIM = 128
GROUP = HEADS // KV_HEADS
SLOTS = GROUP + 2
TQ = 512
KEYS_DEV = 4096
NEG_FILL = -1e30
LOG2E = 1.4426950408889634

YN, ZN, XN, CN = 4, 8, 4, 2
HN = XN * CN
CTX = ("y", "z")
HEAD = ("x", "core")
OWN = 16
TAIL = 128
KTOT = KEYS_DEV + TAIL
OUT_W = 640
KEY_TILE = 512


def exchange(array, axes):
    return lax.all_to_all(array, axes, 0, 0, tiled=True)


def copies(array, count):
    return jnp.broadcast_to(array[None], (count, *array.shape))


def attend_kernel(info_ref, q_ref, k_ref, v_ref, new_ref, o_ref, kx, vx, scores, weights):
    count = info_ref[0]
    first_own = info_ref[1]
    rows = q_ref.shape[0]

    @pl.when(pl.program_id(0) == 0)
    def _():
        lane = lax.broadcasted_iota(jnp.int32, (KEYS_DEV, HEAD_DIM), 1)
        key_row = lax.broadcasted_iota(jnp.int32, (KEYS_DEV, HEAD_DIM), 0)
        kx[0:KEYS_DEV, 0:HEAD_DIM] = k_ref[...]
        kx[0:KEYS_DEV, HEAD_DIM:] = jnp.where((lane == 0) & (key_row >= count), NEG_FILL, 0.0).astype(jnp.bfloat16)
        vx[0:KEYS_DEV, 0:HEAD_DIM] = v_ref[...]
        vx[0:KEYS_DEV, HEAD_DIM:] = jnp.where(lane == 0, 1.0, 0.0).astype(jnp.bfloat16)
        kx[KEYS_DEV:, :] = jnp.zeros((TAIL, 2 * HEAD_DIM), jnp.bfloat16)
        vx[KEYS_DEV:, :] = jnp.zeros((TAIL, 2 * HEAD_DIM), jnp.bfloat16)
        kx[KEYS_DEV : KEYS_DEV + OWN, 0:HEAD_DIM] = new_ref[:, 0:HEAD_DIM]
        vx[KEYS_DEV : KEYS_DEV + OWN, 0:HEAD_DIM] = new_ref[:, HEAD_DIM:]
        vx[KEYS_DEV : KEYS_DEV + OWN, HEAD_DIM:] = jnp.where(lane[:OWN] == 0, 1.0, 0.0).astype(jnp.bfloat16)

    scale = 1.0 / math.sqrt(HEAD_DIM)
    one = jnp.where(lax.broadcasted_iota(jnp.int32, (rows, HEAD_DIM), 1) == 0, 1.0, 0.0).astype(jnp.bfloat16)
    qx = jnp.concatenate([q_ref[...], one], axis=1)
    row = lax.broadcasted_iota(jnp.int32, (rows, TAIL), 0)
    asked = ((row // OWN) % ZN) * (OWN * YN) + (row // (OWN * ZN)) * OWN + row % OWN
    own = lax.broadcasted_iota(jnp.int32, (rows, TAIL), 1)
    seen = (own < OWN) & (own + first_own <= asked)

    def product(a, b):
        return lax.dot_general(a, b, (((1,), (1,)), ((), ())), preferred_element_type=jnp.float32)

    top = jnp.where(seen, product(qx, kx[KEYS_DEV:, :]), NEG_FILL)
    scores[:, KEYS_DEV:] = top
    for start in range(0, KEYS_DEV, KEY_TILE):
        part = product(qx, kx[start : start + KEY_TILE, :])
        scores[:, start : start + KEY_TILE] = part
        for j in range(0, KEY_TILE, 128):
            top = jnp.maximum(top, part[:, j : j + 128])
    best = jnp.max(top, axis=1, keepdims=True)
    shift = best * (scale * LOG2E)
    for start in range(0, KTOT, 128):
        weights[:, start : start + 128] = jnp.exp2(
            scores[:, start : start + 128] * (scale * LOG2E) - shift
        ).astype(jnp.bfloat16)
    out = jnp.dot(weights[...], vx[...], preferred_element_type=jnp.float32)
    total = out[:, HEAD_DIM : HEAD_DIM + 1]
    o_ref[:, 0:HEAD_DIM] = (out[:, 0:HEAD_DIM] / total).astype(jnp.bfloat16)
    level = best * scale + jnp.log(total)
    high = level.astype(jnp.bfloat16)
    rest = level - high.astype(jnp.float32)
    mid = rest.astype(jnp.bfloat16)
    low = (rest - mid.astype(jnp.float32)).astype(jnp.bfloat16)
    lane = lax.broadcasted_iota(jnp.int32, (rows, HEAD_DIM), 1)
    packed = jnp.where(
        lane == 0,
        high.astype(jnp.float32),
        jnp.where(lane == 1, mid.astype(jnp.float32), jnp.where(lane == 2, low.astype(jnp.float32), 0.0)),
    )
    o_ref[:, HEAD_DIM:] = packed.astype(jnp.bfloat16)


def attend(info, queries, key_block, value_block, new_rows):
    rows = TQ
    return pl.pallas_call(
        attend_kernel,
        grid_spec=pltpu.PrefetchScalarGridSpec(
            num_scalar_prefetch=1,
            grid=(GROUP,),
            in_specs=[
                pl.BlockSpec((rows, HEAD_DIM), lambda s, info: (0, s)),
                pl.BlockSpec((KEYS_DEV, HEAD_DIM), lambda s, info: (0, 0)),
                pl.BlockSpec((KEYS_DEV, HEAD_DIM), lambda s, info: (0, 0)),
                pl.BlockSpec((OWN, 2 * HEAD_DIM), lambda s, info: (0, 0)),
            ],
            out_specs=pl.BlockSpec((rows, 2 * HEAD_DIM), lambda s, info: (0, s)),
            scratch_shapes=[
                pltpu.VMEM((KTOT, 2 * HEAD_DIM), jnp.bfloat16),
                pltpu.VMEM((KTOT, 2 * HEAD_DIM), jnp.bfloat16),
                pltpu.VMEM((rows, KTOT), jnp.float32),
                pltpu.VMEM((rows, KTOT), jnp.bfloat16),
            ],
        ),
        out_shape=jax.ShapeDtypeStruct((rows, GROUP * 2 * HEAD_DIM), jnp.bfloat16),
        compiler_params=pltpu.CompilerParams(vmem_limit_bytes=48 * 1024 * 1024),
        name="attend",
    )(info, queries, key_block, value_block, new_rows)


def rotate(values_in, positions_in):
    half = HEAD_DIM // 2
    frequency = 500000.0 ** (-(jnp.arange(half, dtype=jnp.float32) * 2.0 / HEAD_DIM))
    angles = positions_in.astype(jnp.float32)[:, None] * frequency[None, :]
    cosine = jnp.cos(angles)[:, None, :]
    sine = jnp.sin(angles)[:, None, :]
    first, second = values_in[..., :half], values_in[..., half:]
    return jnp.concatenate([first * cosine - second * sine, second * cosine + first * sine], axis=-1)


def per_device(hidden, norm_gain, w_qkv, positions, cache_keys, cache_values, key_counts, w_out):
    y, z = lax.axis_index("y"), lax.axis_index("z")
    head = lax.axis_index(HEAD)
    width = SLOTS * HEAD_DIM
    scaled = (hidden.astype(jnp.float32) * norm_gain[None, :]).astype(jnp.bfloat16)
    both = jnp.concatenate([hidden, scaled], axis=1).reshape(YN, 1, OWN, 256)
    sent = jnp.broadcast_to(both, (YN, HN, OWN, 256)).reshape(YN * HN, OWN, 256)
    own_columns = lax.dynamic_slice_in_dim(w_qkv, head * width, width, axis=1)
    w_all = exchange(copies(own_columns, YN), "y")
    got = exchange(sent, ("y", "x", "core")).reshape(YN, HN * OWN, 256)
    plain = got[:, :, :128].astype(jnp.float32)
    square = jnp.sum(plain * plain, axis=(0, 2))
    turned = jnp.moveaxis(got[:, :, 128:], 0, 1).reshape(HN * OWN, YN * 128)
    mix = jnp.dot(turned, w_all.reshape(YN * 128, width), preferred_element_type=jnp.float32)
    mix = jnp.concatenate([mix, jnp.broadcast_to(square[:, None], (HN * OWN, 128))], axis=1)
    share = jnp.sum(exchange(mix.reshape(ZN, OWN, width + 128), "z"), axis=0)
    inv_rms = lax.rsqrt(share[:, width] / D + 1e-05)
    share = (share[:, :width] * inv_rms[:, None]).reshape(OWN, SLOTS, HEAD_DIM)
    first_own = z * (OWN * YN) + y * OWN
    here = lax.dynamic_slice_in_dim(positions, first_own, OWN)
    turned = rotate(share[:, : GROUP + 1], here).astype(jnp.bfloat16)
    queries = turned[:, :GROUP].reshape(OWN, GROUP * HEAD_DIM)
    new_rows = jnp.concatenate([turned[:, GROUP], share[:, GROUP + 1].astype(jnp.bfloat16)], axis=1)
    queries = exchange(copies(queries, YN * ZN), CTX).reshape(TQ, GROUP * HEAD_DIM)
    info = jnp.stack([key_counts[0], first_own.astype(jnp.int32)])
    w_full = exchange(copies(w_out, HN), HEAD).reshape(HEADS * HEAD_DIM, 128)
    part = attend(info, queries, cache_keys, cache_values, new_rows)
    part = part.reshape(TQ, GROUP, 2, HEAD_DIM)
    levels = part[:, :, 1, :32].reshape(TQ, GROUP * 32)
    message = jnp.concatenate([part[:, :, 0].reshape(TQ, GROUP * HEAD_DIM), levels], axis=1)
    message = message.reshape(256, 2, OUT_W)
    back = exchange(message, ("y", "x", "core", "z"))
    back = back.reshape(YN, HN, ZN, 2, OUT_W).astype(jnp.float32)
    levels = back[..., GROUP * HEAD_DIM :].reshape(YN, HN, ZN, 2, GROUP, 32)
    level = levels[..., 0] + levels[..., 1] + levels[..., 2]
    outs = back[..., : GROUP * HEAD_DIM].reshape(YN, HN, ZN, 2, GROUP, HEAD_DIM)
    most = jnp.max(level, axis=(0, 2), keepdims=True)
    factor = jnp.exp(level - most)
    summed = jnp.sum(outs * factor[..., None], axis=(0, 2))
    total = jnp.sum(factor, axis=(0, 2))
    attended = (summed / total[..., None]).astype(jnp.bfloat16)
    attended = jnp.moveaxis(attended, 0, 1).reshape(2, HEADS * HEAD_DIM)
    rows = exchange(copies(attended, YN * ZN), CTX).reshape(64, HEADS * HEAD_DIM)
    return jnp.dot(rows, w_full, preferred_element_type=jnp.float32).astype(jnp.bfloat16)


def solution(mesh):
    fine = Mesh(mesh.devices.reshape(YN, ZN, XN, CN), ("y", "z", "x", "core"))
    return jax.shard_map(
        per_device,
        mesh=fine,
        in_specs=(
            P(HEAD, CTX),
            P(CTX),
            P(CTX, None),
            P(),
            P(CTX, HEAD),
            P(CTX, HEAD),
            P(CTX),
            P(HEAD, CTX),
        ),
        out_specs=P(HEAD, CTX),
        check_vma=False,
    )
```

time: 357 us -> 210 us (0.59)
  blocking collectives: 137 us -> 56.2 us
  waiting for transfers between devices: 107 us -> 60.7 us
  matrix products: 40.3 us -> 1.19 us
  Pallas kernels: 0 us -> 25.8 us
  other arithmetic: 23 us -> 8.3 us
  between operations: 13.7 us -> 0.86 us
  local copies, waits for them, and re-layouts: 13.3 us -> 26 us
  starting transfers between devices: 19.4 us -> 30.5 us
    all_to_all x3 -> x2, blocking collectives: 100 us -> 56.2 us  [exchange(): return lax.all_to_all(array, axes, 0, 0, tiled=True)]
    reduce_scatter x1 -> x0, waiting for transfers between devices: 42.2 us -> none  [per_device(): lax.psum_scatter(jnp.dot(attended, w_out, preferred_element_type=jnp.floa...]
    dot_general x18 -> x2, matrix products: 40.3 us -> 1.19 us  [the longest x1 0.92 us: per_device(): jnp.dot(rows, w_full, preferred_element_type=jnp.float32)]
    all_gather x1 -> x0, blocking collectives: 37.5 us -> none  [per_device(): attended = lax.all_gather(attended_share, 'ctx', axis=0, tiled=True)]
    pallas_call x0 -> x1, Pallas kernels: none -> 25.8 us  [attend(): pl.pallas_call(attend_kernel, grid_spec=pltpu.PrefetchScalarGridSpec(num_...]
    all_to_all x3 -> x5, starting transfers between devices: 19.2 us -> 30.5 us  [exchange(): return lax.all_to_all(array, axes, 0, 0, tiled=True)]
    slice x3 -> x6, local copies, waits for them, and re-layouts: 0.67 us -> 10.8 us  [the longest x1 4.48 us: per_device(): part[:, :, 0].reshape(TQ, GROUP * HEAD_DIM)]
    reduce_sum x12 -> x4, other arithmetic: 12.2 us -> 2.16 us  [the longest x1 1.84 us: per_device(): summed = jnp.sum(outs * factor[..., None], axis=(0, 2))]
  transfers between devices with their start and end apart: 4 -> 5, of which waited for: 4 -> 5; matrix products, arithmetic and copies ran while one was open for 0% -> 1% of each run, Pallas kernels for 0% -> 0%
where the time goes in v1:
time: 210 us
  waiting for transfers between devices  60.7 us (29%)
  blocking collectives  56.2 us (27%)
  starting transfers between devices  30.5 us (15%)
  local copies, waits for them, and re-layouts  26 us (12%)
  Pallas kernels  25.8 us (12%)
  other arithmetic  8.3 us (4%)
    all_to_all x5, waiting for transfers between devices, exchange(): return lax.all_to_all(array, axes, 0, 0, tiled=True)  60.7 us
    all_to_all x2, blocking collectives, exchange(): return lax.all_to_all(array, axes, 0, 0, tiled=True)  56.2 us
    all_to_all x5, starting transfers between devices, exchange(): return lax.all_to_all(array, axes, 0, 0, tiled=True)  30.5 us
    pallas_call x1, Pallas kernels, attend(): pl.pallas_call(attend_kernel, grid_spec=pltpu.PrefetchScalarGridSpec(num_...  25.8 us
    mul x3, local copies, waits for them, and re-layouts, per_device(): summed = jnp.sum(outs * factor[..., None], axis=(0, 2))  5.08 us
    slice x1, local copies, waits for them, and re-layouts, per_device(): part[:, :, 0].reshape(TQ, GROUP * HEAD_DIM)  4.48 us
  transfers between devices with their start and end apart: 5, of which 5 were waited for; matrix products, arithmetic and copies ran while one was open for 1% of the time, Pallas kernels for 0%

profile of v1, /device:TPU:1, one launch (start us, length us, event | category | flops | bytes accessed | tf_op | source)
XLA Modules:
  0.0 209.5 jit_solution(507300992570868443)
XLA Ops:
  0.0 0.8 multiply_convert_fusion
  0.8 0.7 pad_maximum_fusion.2
  1.6 0.7 broadcast_in_dim.19
  2.3 8.6 %all-to-all-start = ((bf16[32,16,256]{2,1,0:T(8,128)(2,1)}), bf16[32,16,256]{2,1,0:T(8,128)(2,1)S(1)}, u32[]{:S(2)}, u32[]{:S(2)}) async-start(bf16[32,16,256]{2,1,0:T(8,128)(2,1)} %bitcast.2), calls=%async_computation | async-start | bytes 524288 | tf_op jit(solution)/shard_map/all_to_all | solution.py:35
  10.9 8.9 %all-to-all-done = bf16[32,16,256]{2,1,0:T(8,128)(2,1)S(1)} async-done(((bf16[32,16,256]{2,1,0:T(8,128)(2,1)}), bf16[32,16,256]{2,1,0:T(8,128)(2,1)S(1)}, u32[]{:S(2)}, u32[]{:S(2)}) %all-to-all-start) | async-done | bytes 262176 | tf_op jit(solution)/shard_map/all_to_all | solution.py:35
  19.8 0.9 broadcast_in_dim.20
  20.7 3.5 %all-to-all-start.1 = ((bf16[4,128,768]{2,1,0:T(8,128)(2,1)}), bf16[4,128,768]{2,1,0:T(8,128)(2,1)S(1)}, u32[]{:S(2)}, u32[]{:S(2)}) async-start(bf16[4,128,768]{2,1,0:T(8,128)(2,1)} %broadcast_in_dim.20), calls=%async_computation.1 | async-start | bytes 1572864 | tf_op jit(solution)/shard_map/all_to_all | solution.py:35
  24.2 0.1 multiply_reduce_fusion
  24.3 12.0 %all-to-all-done.1 = bf16[4,128,768]{2,1,0:T(8,128)(2,1)S(1)} async-done(((bf16[4,128,768]{2,1,0:T(8,128)(2,1)}), bf16[4,128,768]{2,1,0:T(8,128)(2,1)S(1)}, u32[]{:S(2)}, u32[]{:S(2)}) %all-to-all-start.1) | async-done | bytes 786464 | tf_op jit(solution)/shard_map/all_to_all | solution.py:35
  36.4 0.3 convolution_bitcast_fusion
  36.7 0.8 pad_maximum_fusion.1
  37.5 8.2 %all-to-all-start.2 = ((f32[8,16,896]{2,1,0:T(8,128)}), f32[8,16,896]{2,1,0:T(8,128)S(1)}, u32[]{:S(2)}, u32[]{:S(2)}) async-start(f32[8,16,896]{2,1,0:T(8,128)} %bitcast.6), calls=%async_computation.2 | async-start | bytes 917504 | tf_op jit(solution)/shard_map/all_to_all | solution.py:35
  45.7 0.8 dynamic-slice_convert_fusion
  46.5 0.1 multiply_cosine_fusion
  46.6 13.9 %all-to-all-done.2 = f32[8,16,896]{2,1,0:T(8,128)S(1)} async-done(((f32[8,16,896]{2,1,0:T(8,128)}), f32[8,16,896]{2,1,0:T(8,128)S(1)}, u32[]{:S(2)}, u32[]{:S(2)}) %all-to-all-start.2) | async-done | bytes 458784 | tf_op jit(solution)/shard_map/all_to_all | solution.py:35
  60.6 0.1 fusion.8
  61.0 0.9 broadcast_in_dim.23
  61.8 3.9 %all-to-all-start.3 = ((bf16[32,16,512]{2,1,0:T(8,128)(2,1)}), bf16[32,16,512]{2,1,0:T(8,128)(2,1)S(1)}, u32[]{:S(2)}, u32[]{:S(2)}) async-start(bf16[32,16,512]{2,1,0:T(8,128)(2,1)} %broadcast_in_dim.23), calls=%async_computation.3 | async-start | bytes 1048576 | tf_op jit(solution)/shard_map/all_to_all | solution.py:35
  66.6 11.9 %all-to-all-done.3 = bf16[32,16,512]{2,1,0:T(8,128)(2,1)S(1)} async-done(((bf16[32,16,512]{2,1,0:T(8,128)(2,1)}), bf16[32,16,512]{2,1,0:T(8,128)(2,1)S(1)}, u32[]{:S(2)}, u32[]{:S(2)}) %all-to-all-start.3) | async-done | bytes 524320 | tf_op jit(solution)/shard_map/all_to_all | solution.py:35
  78.5 1.2 copy-done.1
  79.7 1.2 copy-done.2
  81.0 25.8 %attend.1 = bf16[512,1024]{1,0:T(8,128)(2,1)S(1)} custom-call(s32[2]{0:T(128)S(1)} %pad_add_fusion.info_ref, bf16[512,512]{1,0:T(8,128)(2,1)S(1)} %bitcast.43, bf16[4096,128]{1,0:T(8,128)(2,1)S(1)} %copy-done.1, bf16[4096,128]{1,0:T(8,128)(2,1)S(1)} %copy-done.2, bf16[16,256]{1,0:T(8,128)(2,1)S(1)} %pad_maximum_fusion.3.new_ref), custom_call_target="tpu_custom_call" | custom-call | tf_op jit(solution)/shard_map/attend/pallas_call | solution.py:104
  106.8 1.6 reshape.109
  108.4 4.5 %slice_reduce_fusion.1 = bf16[512,4,128]{2,1,0:T(4,128)(2,1)S(1)} fusion(bf16[512,4,2,128]{3,2,1,0:T(2,128)(2,1)} %reshape.109), kind=kLoop, calls=%fused_computation.5 | loop fusion | bytes 1048576 | tf_op jit(solution)/shard_map/slice | solution.py:168
  112.9 3.6 %slice_reduce_fusion = bf16[512,4,32]{2,1,0:T(4,128)(2,1)S(1)} fusion(bf16[512,4,2,128]{3,2,1,0:T(2,128)(2,1)S(1)} %copy-done.3), kind=kLoop, calls=%fused_computation.4 | loop fusion | bytes 262144 | tf_op jit(solution)/shard_map/slice | solution.py:167
  116.4 0.2 concatenate.25
  116.6 0.3 concatenate.26
  116.9 0.6 pad_maximum_fusion
  117.6 37.7 %all_to_all.35 = bf16[256,2,640]{2,1,0:T(2,128)(2,1)S(1)} all-to-all(bf16[256,2,640]{2,1,0:T(2,128)(2,1)S(1)} %pad_maximum_fusion), channel_id=1, replica_groups=mesh['y'=4,'z'=8,'x'=4,'core'=2] {'y','x','core','z'}, dimensions={0} | all-to-all | bytes 1310720 | tf_op jit(solution)/shard_map/all_to_all | solution.py:35
  155.3 0.5 bitcast_convert_fusion
  155.8 0.1 slice.80
  155.9 2.6 %copy.31 = f32[4,8,8,2,128]{2,1,4,3,0:T(8,128)} copy(f32[4,8,8,2,128]{4,3,2,1,0:T(2,128)S(1)} %slice.80) | data formatting | bytes 524288 | tf_op jit(solution)/shard_map/slice | solution.py:172
  158.4 1.1 fusion.11
  159.6 0.2 fusion.2
  159.8 0.1 exponential_bitcast_fusion
  159.9 0.1 copy.34
  160.0 0.5 copy.32
  160.4 1.6 mul.117
  162.0 3.0 %mul.118 = f32[4,8,8,2,512]{4,3,2,1,0:T(2,128)} reshape(f32[4,8,8,2,4,128]{5,4,3,2,1,0:T(4,128)} %mul.117) | data formatting | bytes 2097152 | tf_op jit(solution)/shard_map/mul | solution.py:177
  165.0 1.8 fusion
  166.9 0.1 fusion.3
  167.1 0.5 broadcast_in_dim.25
  167.5 18.5 %all_to_all.36 = bf16[32,2,4096]{2,1,0:T(2,128)(2,1)} all-to-all(bf16[32,2,4096]{2,1,0:T(2,128)(2,1)S(1)} %broadcast_in_dim.25), channel_id=1, replica_groups=mesh['y'=4,'z'=8,'x'=4,'core'=2] {'y','z'}, dimensions={0} | all-to-all | bytes 1048576 | tf_op jit(solution)/shard_map/all_to_all | solution.py:35
  186.0 1.1 broadcast_in_dim.26
  187.1 6.3 %all-to-all-start.6 = ((bf16[8,512,128]{2,1,0:T(8,128)(2,1)}), bf16[8,512,128]{2,1,0:T(8,128)(2,1)S(1)}, u32[]{:S(2)}, u32[]{:S(2)}) async-start(bf16[8,512,128]{2,1,0:T(8,128)(2,1)} %broadcast_in_dim.26), calls=%async_computation.6 | async-start | bytes 2097152 | tf_op jit(solution)/shard_map/all_to_all | solution.py:35
  193.5 1.2 reshape.111
  194.7 13.9 %all-to-all-done.6 = bf16[8,512,128]{2,1,0:T(8,128)(2,1)S(1)} async-done(((bf16[8,512,128]{2,1,0:T(8,128)(2,1)}), bf16[8,512,128]{2,1,0:T(8,128)(2,1)S(1)}, u32[]{:S(2)}, u32[]{:S(2)}) %all-to-all-start.6) | async-done | bytes 1048608 | tf_op jit(solution)/shard_map/all_to_all | solution.py:35
  208.6 0.9 convolution_convert_fusion
  (23 shorter events, 0.6 us)
Async XLA Ops:
  0.0 10.9 %copy-start = (bf16[128,6144]{1,0:T(8,128)(2,1)S(1)}, bf16[128,6144]{1,0:T(8,128)(2,1)}, u32[]{:S(2)}) copy-start(bf16[128,6144]{1,0:T(8,128)(2,1)} %param.10) | copy-start | bytes 4718596
  2.3 17.5 %all-to-all-start = ((bf16[32,16,256]{2,1,0:T(8,128)(2,1)}), bf16[32,16,256]{2,1,0:T(8,128)(2,1)S(1)}, u32[]{:S(2)}, u32[]{:S(2)}) async-start(bf16[32,16,256]{2,1,0:T(8,128)(2,1)} %bitcast.2), calls=%async_computation | async-start | bytes 524288 | tf_op jit(solution)/shard_map/all_to_all | solution.py:35
  20.7 15.7 %all-to-all-start.1 = ((bf16[4,128,768]{2,1,0:T(8,128)(2,1)}), bf16[4,128,768]{2,1,0:T(8,128)(2,1)S(1)}, u32[]{:S(2)}, u32[]{:S(2)}) async-start(bf16[4,128,768]{2,1,0:T(8,128)(2,1)} %broadcast_in_dim.20), calls=%async_computation.1 | async-start | bytes 1572864 | tf_op jit(solution)/shard_map/all_to_all | solution.py:35
  37.5 23.0 %all-to-all-start.2 = ((f32[8,16,896]{2,1,0:T(8,128)}), f32[8,16,896]{2,1,0:T(8,128)S(1)}, u32[]{:S(2)}, u32[]{:S(2)}) async-start(f32[8,16,896]{2,1,0:T(8,128)} %bitcast.6), calls=%async_computation.2 | async-start | bytes 917504 | tf_op jit(solution)/shard_map/all_to_all | solution.py:35
  61.8 16.7 %all-to-all-start.3 = ((bf16[32,16,512]{2,1,0:T(8,128)(2,1)}), bf16[32,16,512]{2,1,0:T(8,128)(2,1)S(1)}, u32[]{:S(2)}, u32[]{:S(2)}) async-start(bf16[32,16,512]{2,1,0:T(8,128)(2,1)} %broadcast_in_dim.23), calls=%async_computation.3 | async-start | bytes 1048576 | tf_op jit(solution)/shard_map/all_to_all | solution.py:35
  78.5 1.2 copy-start.1
  79.7 1.2 copy-start.2
  108.4 4.5 %copy-start.3 = (bf16[512,4,2,128]{3,2,1,0:T(2,128)(2,1)S(1)}, bf16[512,4,2,128]{3,2,1,0:T(2,128)(2,1)}, u32[]{:S(2)}) copy-start(bf16[512,4,2,128]{3,2,1,0:T(2,128)(2,1)} %reshape.109) | copy-start | bytes 3145732
  166.9 19.1 %copy-start.4 = (bf16[512,128]{1,0:T(8,128)(2,1)S(1)}, bf16[512,128]{1,0:T(8,128)(2,1)}, u32[]{:S(2)}) copy-start(bf16[512,128]{1,0:T(8,128)(2,1)} %param.15) | copy-start | bytes 393220
  187.1 21.4 %all-to-all-start.6 = ((bf16[8,512,128]{2,1,0:T(8,128)(2,1)}), bf16[8,512,128]{2,1,0:T(8,128)(2,1)S(1)}, u32[]{:S(2)}, u32[]{:S(2)}) async-start(bf16[8,512,128]{2,1,0:T(8,128)(2,1)} %broadcast_in_dim.26), calls=%async_computation.6 | async-start | bytes 2097152 | tf_op jit(solution)/shard_map/all_to_all | solution.py:35

commit v2 on v1

v2 whole, which is shorter than its diff:
```python
import math

import jax
import jax.numpy as jnp
from jax import lax
from jax.experimental import pallas as pl
from jax.experimental.pallas import tpu as pltpu
from jax.sharding import Mesh
from jax.sharding import PartitionSpec as P

D = 4096
HEADS = 32
KV_HEADS = 8
HEAD_DIM = 128
GROUP = HEADS // KV_HEADS
SLOTS = GROUP + 2
WIDTH = SLOTS * HEAD_DIM
FLAT = GROUP * HEAD_DIM
TQ = 512
KEYS_DEV = 4096
NEG_FILL = -1e30
SCALE = 1.0 / math.sqrt(HEAD_DIM)
SCALE2 = SCALE * 1.4426950408889634

YN, ZN, XN, CN = 4, 8, 4, 2
HN = XN * CN
CTXN = YN * ZN
CTX = ("y", "z")
HEAD = ("x", "core")
OWN = TQ // CTXN
TAIL = 128
KEY_TILE = 512
PAIR = 2

VMEM = pl.BlockSpec(memory_space=pltpu.VMEM)
SMEM = pl.BlockSpec(memory_space=pltpu.SMEM)
ANY = pl.BlockSpec(memory_space=pl.ANY)


def shape(dims, kind):
    return jax.ShapeDtypeStruct(dims, kind)


def params(mib):
    return pltpu.CompilerParams(vmem_limit_bytes=mib * 1024 * 1024)


def exchange(array, axes):
    return lax.all_to_all(array, axes, 0, 0, tiled=True)


def split_kernel(head_ref, hidden_ref, gain_ref, w_ref, sent_ref, own_ref, sem):
    first = pl.multiple_of(head_ref[0] * WIDTH, 128)
    copy = pltpu.make_async_copy(w_ref.at[:, pl.ds(first, WIDTH)], own_ref, sem)
    copy.start()
    hidden = hidden_ref[...]
    scaled = (hidden.astype(jnp.float32) * gain_ref[...]).astype(jnp.bfloat16)
    both = jnp.concatenate([hidden, scaled], axis=1)
    for y in range(YN):
        for h in range(HN):
            sent_ref[y * HN + h] = both[y * OWN : (y + 1) * OWN]
    copy.wait()


def project_kernel(info_ref, got_ref, w0, w1, w2, w3, table_ref, k_ref, v_ref, mix_ref):
    y = info_ref[2]
    total = None
    square = None
    for shift, w in enumerate((w0, w1, w2, w3)):
        source = lax.rem(y + YN - shift, YN)
        part = got_ref[pl.ds(source * HN, HN)].reshape(HN * OWN, 2 * HEAD_DIM)
        term = jnp.dot(part[:, HEAD_DIM:], w[...], preferred_element_type=jnp.float32)
        plain = part[:, :HEAD_DIM].astype(jnp.float32)
        own = jnp.sum(plain * plain, axis=1, keepdims=True)
        total = term if total is None else total + term
        square = own if square is None else square + own
    mix_ref[:, :, :WIDTH] = total.reshape(ZN, OWN, WIDTH)
    mix_ref[:, :, WIDTH:] = jnp.broadcast_to(square, (HN * OWN, HEAD_DIM)).reshape(ZN, OWN, HEAD_DIM)


def turn_kernel(mix_ref, table_ref, queries_ref, new_ref):
    share = mix_ref[0]
    for z in range(1, ZN):
        share = share + mix_ref[z]
    inv_rms = lax.rsqrt(share[:, WIDTH : WIDTH + 1] / D + 1e-05)
    cosine, sine = table_ref[:, :HEAD_DIM], table_ref[:, HEAD_DIM:]
    slots = []
    for s in range(SLOTS):
        value = share[:, s * HEAD_DIM : (s + 1) * HEAD_DIM] * inv_rms
        if s <= GROUP:
            value = value * cosine + pltpu.roll(value, HEAD_DIM // 2, 1) * sine
        slots.append(value.astype(jnp.bfloat16))
    queries = jnp.concatenate(slots[:GROUP], axis=1)
    for c in range(CTXN):
        queries_ref[c] = queries
    new_ref[...] = jnp.concatenate(slots[GROUP:], axis=1)


def attend_kernel(info_ref, q_ref, k_ref, v_ref, new_ref, o_ref):
    count = info_ref[0]
    first_own = info_ref[1]
    rows = PAIR * TQ

    def lane(n):
        return lax.broadcasted_iota(jnp.int32, (n, HEAD_DIM), 1)

    def first_lane(n):
        return jnp.where(lane(n) == 0, 1.0, 0.0).astype(jnp.bfloat16)

    def product(a, b):
        return lax.dot_general(a, b, (((1,), (1,)), ((), ())), preferred_element_type=jnp.float32)

    asked = lax.broadcasted_iota(jnp.int32, (rows, TAIL), 0) % TQ
    own = lax.broadcasted_iota(jnp.int32, (rows, TAIL), 1)
    seen = (own < OWN) & (own + first_own <= asked)
    blank = jnp.zeros((TAIL - OWN, HEAD_DIM), jnp.bfloat16)
    tail_keys = jnp.concatenate([new_ref[:, :HEAD_DIM], blank], axis=0)
    tail_values = jnp.concatenate([new_ref[:, HEAD_DIM:], blank], axis=0)
    spot = lane(TQ)
    packed = jnp.zeros((TQ, HEAD_DIM), jnp.float32)
    for pair in range(GROUP // PAIR):
        slots = range(pair * PAIR, (pair + 1) * PAIR)
        queries = jnp.concatenate(
            [q_ref[:, :, s * HEAD_DIM : (s + 1) * HEAD_DIM].reshape(TQ, HEAD_DIM) for s in slots], axis=0
        )
        wide = jnp.concatenate([queries, first_lane(rows)], axis=1)
        best = jnp.full((rows, 1), NEG_FILL, jnp.float32)
        sums = jnp.zeros((rows, 2 * HEAD_DIM), jnp.float32)
        for start in range(0, KEYS_DEV + TAIL, KEY_TILE):
            if start < KEYS_DEV:
                index = lax.broadcasted_iota(jnp.int32, (KEY_TILE, HEAD_DIM), 0) + start
                hide = jnp.where((lane(KEY_TILE) == 0) & (index >= count), NEG_FILL, 0.0).astype(jnp.bfloat16)
                keys = jnp.concatenate([k_ref[start : start + KEY_TILE, :], hide], axis=1)
                values = jnp.concatenate([v_ref[start : start + KEY_TILE, :], first_lane(KEY_TILE)], axis=1)
                scores = product(wide, keys)
            else:
                values = jnp.concatenate([tail_values, first_lane(TAIL)], axis=1)
                scores = jnp.where(seen, product(queries, tail_keys), NEG_FILL)
            higher = jnp.maximum(best, jnp.max(scores, axis=1, keepdims=True))
            weights = jnp.exp2(scores * SCALE2 - higher * SCALE2).astype(jnp.bfloat16)
            sums = sums * jnp.exp2((best - higher) * SCALE2) + jnp.dot(
                weights, values, preferred_element_type=jnp.float32
            )
            best = higher
        total = sums[:, HEAD_DIM : HEAD_DIM + 1]
        outs = (sums[:, :HEAD_DIM] * (1.0 / total)).astype(jnp.bfloat16)
        level = best * SCALE + jnp.log(total)
        high = level.astype(jnp.bfloat16).astype(jnp.float32)
        mid = (level - high).astype(jnp.bfloat16).astype(jnp.float32)
        low = (level - high) - mid
        for n, s in enumerate(slots):
            here = slice(n * TQ, (n + 1) * TQ)
            o_ref[:, :, s * HEAD_DIM : (s + 1) * HEAD_DIM] = outs[here].reshape(CTXN, OWN, HEAD_DIM)
            for step, piece in enumerate((high, mid, low)):
                packed = jnp.where(spot == step * GROUP + s, piece[here], packed)
    o_ref[:, :, FLAT:] = packed.astype(jnp.bfloat16).reshape(CTXN, OWN, HEAD_DIM)


def join_kernel(back_ref, rows_ref):
    parts = back_ref[:, :, FLAT:].astype(jnp.float32).reshape(CTXN * OWN, HEAD_DIM)
    level = parts + pltpu.roll(parts, HEAD_DIM - GROUP, 1) + pltpu.roll(parts, HEAD_DIM - 2 * GROUP, 1)
    spot = lax.broadcasted_iota(jnp.int32, parts.shape, 1)
    level = jnp.where(spot < GROUP, level, 0.0).reshape(CTXN, OWN, HEAD_DIM)
    factor = jnp.exp(level - jnp.max(level, axis=0, keepdims=True))
    factor = factor * (1.0 / jnp.sum(factor, axis=0, keepdims=True))
    joined = []
    for s in range(GROUP):
        total = jnp.zeros((OWN, HEAD_DIM), jnp.float32)
        for c in range(CTXN):
            outs = back_ref[c, :, s * HEAD_DIM : (s + 1) * HEAD_DIM].astype(jnp.float32)
            total = total + outs * factor[c, :, s : s + 1]
        joined.append(total.astype(jnp.bfloat16))
    attended = jnp.concatenate(joined, axis=1)
    for c in range(CTXN):
        rows_ref[c] = attended


def rotary_table(positions):
    half = HEAD_DIM // 2
    frequency = 500000.0 ** (-(jnp.arange(half, dtype=jnp.float32) * 2.0 / HEAD_DIM))
    angles = positions.astype(jnp.float32)[:, None] * frequency[None, :]
    cosine, sine = jnp.cos(angles), jnp.sin(angles)
    return jnp.concatenate([cosine, cosine, -sine, sine], axis=1)


def per_device(hidden, norm_gain, w_qkv, positions, cache_keys, cache_values, key_counts, w_out):
    bf16, f32 = jnp.bfloat16, jnp.float32
    y, z = lax.axis_index("y").astype(jnp.int32), lax.axis_index("z").astype(jnp.int32)
    head = lax.axis_index(HEAD).astype(jnp.int32)
    sent, own_columns = pl.pallas_call(
        split_kernel,
        in_specs=[SMEM, VMEM, VMEM, ANY],
        out_specs=[VMEM, VMEM],
        out_shape=[shape((YN * HN, OWN, 2 * HEAD_DIM), bf16), shape((HEAD_DIM, WIDTH), bf16)],
        scratch_shapes=[pltpu.SemaphoreType.DMA],
        name="split",
    )(head[None], hidden, norm_gain[None, :], w_qkv)
    columns = [own_columns] + [
        lax.ppermute(own_columns, "y", [(i, (i + k) % YN) for i in range(YN)]) for k in range(1, YN)
    ]
    got = exchange(sent, ("y", "x", "core"))
    first_own = z * (OWN * YN) + y * OWN
    info = jnp.stack([key_counts[0], first_own, y])
    table = rotary_table(lax.dynamic_slice_in_dim(positions, first_own, OWN))
    mix = pl.pallas_call(
        project_kernel,
        in_specs=[SMEM] + [VMEM] * 8,
        out_specs=VMEM,
        out_shape=shape((ZN, OWN, WIDTH + HEAD_DIM), f32),
        compiler_params=params(16),
        name="project",
    )(info, got, *columns, table, cache_keys, cache_values)
    mix = exchange(mix, "z")
    queries, new_rows = pl.pallas_call(
        turn_kernel,
        in_specs=[VMEM, VMEM],
        out_specs=[VMEM, VMEM],
        out_shape=[shape((CTXN, OWN, FLAT), bf16), shape((OWN, 2 * HEAD_DIM), bf16)],
        name="turn",
    )(mix, table)
    queries = exchange(queries, ("z", "y"))
    part = pl.pallas_call(
        attend_kernel,
        in_specs=[SMEM, VMEM, VMEM, VMEM, VMEM],
        out_specs=VMEM,
        out_shape=shape((CTXN, OWN, FLAT + HEAD_DIM), bf16),
        compiler_params=params(40),
        name="attend",
    )(info, queries, cache_keys, cache_values, new_rows)
    part = exchange(part, CTX)
    rows = pl.pallas_call(
        join_kernel,
        in_specs=[VMEM],
        out_specs=VMEM,
        out_shape=shape((CTXN, OWN, FLAT), bf16),
        name="join",
    )(part)
    rows = exchange(rows, CTX).reshape(TQ, FLAT)
    result = jnp.dot(rows, w_out, preferred_element_type=f32)
    result = exchange(result.reshape(HN, TQ // HN, HEAD_DIM), HEAD)
    return jnp.sum(result, axis=0).astype(bf16)


def solution(mesh):
    fine = Mesh(mesh.devices.reshape(YN, ZN, XN, CN), ("y", "z", "x", "core"))
    return jax.shard_map(
        per_device,
        mesh=fine,
        in_specs=(
            P(HEAD, CTX),
            P(CTX),
            P(CTX, None),
            P(),
            P(CTX, HEAD),
            P(CTX, HEAD),
            P(CTX),
            P(HEAD, CTX),
        ),
        out_specs=P(HEAD, CTX),
        check_vma=False,
    )
```

time: 210 us -> 148 us (0.70)
  waiting for transfers between devices: 60.7 us -> 7.17 us
  blocking collectives: 56.2 us -> 102 us
  local copies, waits for them, and re-layouts: 26 us -> 1.64 us
  starting transfers between devices: 30.5 us -> 12.3 us
  other arithmetic: 8.3 us -> 1.67 us
  Pallas kernels: 25.8 us -> 21.2 us
    all_to_all x5 -> x1, waiting for transfers between devices: 60.7 us -> 4.87 us  [exchange(): return lax.all_to_all(array, axes, 0, 0, tiled=True)]
    all_to_all x2 -> x5, blocking collectives: 56.2 us -> 102 us  [exchange(): return lax.all_to_all(array, axes, 0, 0, tiled=True)]
    all_to_all x5 -> x1, starting transfers between devices: 30.5 us -> 7.67 us  [exchange(): return lax.all_to_all(array, axes, 0, 0, tiled=True)]
    slice x6 -> x0, local copies, waits for them, and re-layouts: 10.8 us -> none  [the longest x1 4.48 us: per_device(): part[:, :, 0].reshape(TQ, GROUP * HEAD_DIM)]
    mul x3 -> x0, local copies, waits for them, and re-layouts: 5.08 us -> none  [per_device(): summed = jnp.sum(outs * factor[..., None], axis=(0, 2))]
    ppermute x0 -> x3, starting transfers between devices: none -> 4.68 us  [per_device(): lax.ppermute(own_columns, 'y', [(i, (i + k) % YN) for i in range(YN)])]
    pallas_call x1 -> x5, Pallas kernels: 25.8 us -> 21.2 us  [the longest x1 13.3 us: per_device(): pl.pallas_call(attend_kernel, in_specs=[SMEM, VMEM, VMEM, VMEM, VMEM], ou...]
    broadcast_in_dim x7 -> x0, local copies, waits for them, and re-layouts: 4.17 us -> none  [the longest x5 3.38 us: copies(): return jnp.broadcast_to(array[None], (count, *array.shape))]
  transfers between devices with their start and end apart: 5 -> 4, of which waited for: 5 -> 2; matrix products, arithmetic and copies ran while one was open for 1% -> 1% of each run, Pallas kernels for 0% -> 0%
where the time goes in v2:
time: 148 us; the launch traced here: 147 us
  blocking collectives  102 us (69%)
  Pallas kernels  21.2 us (14%)
  starting transfers between devices  12.3 us (8%)
  waiting for transfers between devices  7.17 us (5%)
  other arithmetic  1.67 us (1%)
  local copies, waits for them, and re-layouts  1.64 us (1%)
    all_to_all x5, blocking collectives, exchange(): return lax.all_to_all(array, axes, 0, 0, tiled=True)  102 us
    pallas_call x1, Pallas kernels, per_device(): pl.pallas_call(attend_kernel, in_specs=[SMEM, VMEM, VMEM, VMEM, VMEM], ou...  13.3 us
    all_to_all x1, starting transfers between devices, exchange(): return lax.all_to_all(array, axes, 0, 0, tiled=True)  7.67 us
    all_to_all x1, waiting for transfers between devices, exchange(): return lax.all_to_all(array, axes, 0, 0, tiled=True)  4.87 us
    ppermute x3, starting transfers between devices, per_device(): lax.ppermute(own_columns, 'y', [(i, (i + k) % YN) for i in range(YN)])  4.68 us
  transfers between devices with their start and end apart: 4, of which 2 were waited for; matrix products, arithmetic and copies ran while one was open for 1% of the time, Pallas kernels for 0%

profile of v2, /device:TPU:1, one launch (start us, length us, event | category | flops | bytes accessed | tf_op | source)
XLA Modules:
  0.0 147.1 jit_solution(16423712979320280207)
XLA Ops:
  0.0 0.0 copy-start
  0.0 0.0 copy-start.2
  0.0 0.0 copy-start.1
  0.0 2.6 %split.1 = (bf16[32,16,256]{2,1,0:T(8,128)(2,1)}, bf16[128,768]{1,0:T(8,128)(2,1)}) custom-call(s32[1]{0:T(128)} %bitcast.2.head_ref, bf16[64,128]{1,0:T(8,128)(2,1)} %hidden_ref.1, f32[1,128]{1,0:T(1,128)} %bitcast.10, bf16[128,6144]{1,0:T(8,128)(2,1)} %w_ref.1), custom_call_target="tpu_custom_call" | custom-call | tf_op jit(solution)/shard_map/split/pallas_call | solution.py:190
  2.6 3.6 %collective-permute-start.2 = (bf16[128,768]{1,0:T(8,128)(2,1)}, bf16[128,768]{1,0:T(8,128)(2,1)S(1)}, u32[]{:S(2)}, u32[]{:S(2)}) collective-permute-start(bf16[128,768]{1,0:T(8,128)(2,1)} %get-tuple-element.10.w0), channel_id=1, source_target_pairs={{0,192},{64,0},{128,64},{192,128},{1,193},{65,1},{129,65},{193,129... | collective-permute-start | bytes 589832 | tf_op jit(solution)/shard_map/ppermute | solution.py:199
  6.2 0.3 collective-permute-start.1
  6.6 0.7 collective-permute-start
  7.3 7.7 %all-to-all-start = ((bf16[32,16,256]{2,1,0:T(8,128)(2,1)}), bf16[32,16,256]{2,1,0:T(8,128)(2,1)S(1)}, u32[]{:S(2)}, u32[]{:S(2)}) async-start(bf16[32,16,256]{2,1,0:T(8,128)(2,1)} %get-tuple-element.9), calls=%async_computation | async-start | bytes 524288 | tf_op jit(solution)/shard_map/all_to_all | solution.py:49
  15.0 0.8 dynamic-slice_convert_fusion
  15.7 0.1 multiply_cosine_fusion
  16.5 0.1 pad_add_fusion.info_ref
  16.6 0.1 pad_maximum_fusion.table_ref
  16.7 0.0 copy-start.4
  16.7 0.0 collective-permute-done.2.w3
  16.7 0.0 collective-permute-done.1.w2
  16.7 2.3 %collective-permute-done.w1 = bf16[128,768]{1,0:T(8,128)(2,1)S(1)} collective-permute-done((bf16[128,768]{1,0:T(8,128)(2,1)}, bf16[128,768]{1,0:T(8,128)(2,1)S(1)}, u32[]{:S(2)}, u32[]{:S(2)}) %collective-permute-start) | collective-permute-done | bytes 196640 | tf_op jit(solution)/shard_map/ppermute | solution.py:199
  19.0 4.9 %all-to-all-done.got_ref = bf16[32,16,256]{2,1,0:T(8,128)(2,1)S(1)} async-done(((bf16[32,16,256]{2,1,0:T(8,128)(2,1)}), bf16[32,16,256]{2,1,0:T(8,128)(2,1)S(1)}, u32[]{:S(2)}, u32[]{:S(2)}) %all-to-all-start) | async-done | bytes 262176 | tf_op jit(solution)/shard_map/all_to_all | solution.py:49
  23.9 0.0 copy-done.2
  23.9 0.0 copy-done.1
  23.9 0.0 copy-start.3
  23.9 0.9 copy-done.3
  24.8 0.9 project.1
  25.7 0.0 copy-done.4
  25.7 24.5 %all_to_all.30.mix_ref = f32[8,16,896]{2,1,0:T(8,128)} all-to-all(f32[8,16,896]{2,1,0:T(8,128)S(1)} %project.1), channel_id=1, replica_groups=mesh['y'=4,'z'=8,'x'=4,'core'=2] {'z'}, dimensions={0} | all-to-all | bytes 917504 | tf_op jit(solution)/shard_map/all_to_all | solution.py:49
  50.2 2.0 %turn.1 = (bf16[32,16,512]{2,1,0:T(8,128)(2,1)}, bf16[16,256]{1,0:T(8,128)(2,1)}) custom-call(f32[8,16,896]{2,1,0:T(8,128)} %all_to_all.30.mix_ref, f32[16,256]{1,0:T(8,128)} %copy-done.4), custom_call_target="tpu_custom_call" | custom-call | tf_op jit(solution)/shard_map/turn/pallas_call | solution.py:214
  52.3 20.5 %all_to_all.31.q_ref = bf16[32,16,512]{2,1,0:T(8,128)(2,1)S(1)} all-to-all(bf16[32,16,512]{2,1,0:T(8,128)(2,1)} %get-tuple-element.11), channel_id=1, replica_groups=mesh['y'=4,'z'=8,'x'=4,'core'=2] {'z','y'}, dimensions={0} | all-to-all | bytes 1048576 | tf_op jit(solution)/shard_map/all_to_all | solution.py:49
  72.7 0.0 copy-start.5
  72.7 0.7 copy-done.5
  73.4 13.3 %attend.1 = bf16[32,16,640]{2,1,0:T(8,128)(2,1)S(1)} custom-call(s32[3]{0:T(128)S(1)} %pad_add_fusion.info_ref, bf16[32,16,512]{2,1,0:T(8,128)(2,1)S(1)} %all_to_all.31.q_ref, bf16[4096,128]{1,0:T(8,128)(2,1)S(1)} %copy-done.1, bf16[4096,128]{1,0:T(8,128)(2,1)S(1)} %copy-done.2, bf16[16,256]{1,0:T(8,128)(2,1)S(1)} %copy-done.5), custom_call_target="tpu_custom_call" | custom-call | tf_op jit(solution)/shard_map/attend/pallas_call | solution.py:222
  86.7 20.9 %all_to_all.32.back_ref = bf16[32,16,640]{2,1,0:T(8,128)(2,1)} all-to-all(bf16[32,16,640]{2,1,0:T(8,128)(2,1)S(1)} %attend.1), channel_id=1, replica_groups=mesh['y'=4,'z'=8,'x'=4,'core'=2] {'y','z'}, dimensions={0} | all-to-all | bytes 1310720 | tf_op jit(solution)/shard_map/all_to_all | solution.py:49
  107.6 2.5 %join.1 = bf16[32,16,512]{2,1,0:T(8,128)(2,1)} custom-call(bf16[32,16,640]{2,1,0:T(8,128)(2,1)} %all_to_all.32.back_ref), custom_call_target="tpu_custom_call" | custom-call | tf_op jit(solution)/shard_map/join/pallas_call | solution.py:231
  110.1 21.3 %all_to_all.33 = bf16[32,16,512]{2,1,0:T(8,128)(2,1)S(1)} all-to-all(bf16[32,16,512]{2,1,0:T(8,128)(2,1)} %join.1), channel_id=1, replica_groups=mesh['y'=4,'z'=8,'x'=4,'core'=2] {'y','z'}, dimensions={0} | all-to-all | bytes 1048576 | tf_op jit(solution)/shard_map/all_to_all | solution.py:49
  131.4 0.0 copy-done
  131.4 0.3 fusion
  131.7 14.8 %all_to_all.34 = f32[8,64,128]{2,1,0:T(8,128)S(1)} all-to-all(f32[8,64,128]{2,1,0:T(8,128)S(1)} %fusion), channel_id=1, replica_groups=mesh['y'=4,'z'=8,'x'=4,'core'=2] {'x','core'}, dimensions={0} | all-to-all | bytes 524288 | tf_op jit(solution)/shard_map/all_to_all | solution.py:49
  146.5 0.6 reduce_sum.9
  (1 shorter events, 0.0 us)
Async XLA Ops:
  0.0 131.4 %copy-start = (bf16[512,128]{1,0:T(8,128)(2,1)S(1)}, bf16[512,128]{1,0:T(8,128)(2,1)}, u32[]{:S(2)}) copy-start(bf16[512,128]{1,0:T(8,128)(2,1)} %param.15) | copy-start | bytes 393220
  0.0 23.9 %copy-start.2 = (bf16[4096,128]{1,0:T(8,128)(2,1)S(1)}, bf16[4096,128]{1,0:T(8,128)(2,1)}, u32[]{:S(2)}) copy-start(bf16[4096,128]{1,0:T(8,128)(2,1)} %v_ref.3) | copy-start | bytes 3145732
  0.0 23.9 %copy-start.1 = (bf16[4096,128]{1,0:T(8,128)(2,1)S(1)}, bf16[4096,128]{1,0:T(8,128)(2,1)}, u32[]{:S(2)}) copy-start(bf16[4096,128]{1,0:T(8,128)(2,1)} %k_ref.3) | copy-start | bytes 3145732
  2.6 14.1 %collective-permute-start.2 = (bf16[128,768]{1,0:T(8,128)(2,1)}, bf16[128,768]{1,0:T(8,128)(2,1)S(1)}, u32[]{:S(2)}, u32[]{:S(2)}) collective-permute-start(bf16[128,768]{1,0:T(8,128)(2,1)} %get-tuple-element.10.w0), channel_id=1, source_target_pairs={{0,192},{64,0},{128,64},{192,128},{1,193},{65,1},{129,65},{193,129... | collective-permute-start | bytes 589832 | tf_op jit(solution)/shard_map/ppermute | solution.py:199
  6.2 10.4 %collective-permute-start.1 = (bf16[128,768]{1,0:T(8,128)(2,1)}, bf16[128,768]{1,0:T(8,128)(2,1)S(1)}, u32[]{:S(2)}, u32[]{:S(2)}) collective-permute-start(bf16[128,768]{1,0:T(8,128)(2,1)} %get-tuple-element.10.w0), channel_id=1, source_target_pairs={{0,128},{64,192},{128,0},{192,64},{1,129},{65,193},{129,1},{193,65... | collective-permute-start | bytes 589832 | tf_op jit(solution)/shard_map/ppermute | solution.py:199
  6.6 12.4 %collective-permute-start = (bf16[128,768]{1,0:T(8,128)(2,1)}, bf16[128,768]{1,0:T(8,128)(2,1)S(1)}, u32[]{:S(2)}, u32[]{:S(2)}) collective-permute-start(bf16[128,768]{1,0:T(8,128)(2,1)} %get-tuple-element.10.w0), channel_id=1, source_target_pairs={{0,64},{64,128},{128,192},{192,0},{1,65},{65,129},{129,193},{193,1... | collective-permute-start | bytes 589832 | tf_op jit(solution)/shard_map/ppermute | solution.py:199
  7.3 16.6 %all-to-all-start = ((bf16[32,16,256]{2,1,0:T(8,128)(2,1)}), bf16[32,16,256]{2,1,0:T(8,128)(2,1)S(1)}, u32[]{:S(2)}, u32[]{:S(2)}) async-start(bf16[32,16,256]{2,1,0:T(8,128)(2,1)} %get-tuple-element.9), calls=%async_computation | async-start | bytes 524288 | tf_op jit(solution)/shard_map/all_to_all | solution.py:49
  16.7 9.0 %copy-start.4 = (f32[16,256]{1,0:T(8,128)}, f32[16,256]{1,0:T(8,128)S(1)}, u32[]{:S(2)}) copy-start(f32[16,256]{1,0:T(8,128)S(1)} %pad_maximum_fusion.table_ref) | copy-start | bytes 49156
  23.9 0.9 copy-start.3
  72.7 0.7 copy-start.5

commit v3 on v2

--- a/solution.py
+++ b/solution.py
@@ -34,14 +34,13 @@
 
 VMEM = pl.BlockSpec(memory_space=pltpu.VMEM)
 SMEM = pl.BlockSpec(memory_space=pltpu.SMEM)
-ANY = pl.BlockSpec(memory_space=pl.ANY)
 
 
 def shape(dims, kind):
     return jax.ShapeDtypeStruct(dims, kind)
 
 
-def params(mib):
+def params(mib=8):
     return pltpu.CompilerParams(vmem_limit_bytes=mib * 1024 * 1024)
 
 
@@ -49,20 +48,16 @@
     return lax.all_to_all(array, axes, 0, 0, tiled=True)
 
 
-def split_kernel(head_ref, hidden_ref, gain_ref, w_ref, sent_ref, own_ref, sem):
-    first = pl.multiple_of(head_ref[0] * WIDTH, 128)
-    copy = pltpu.make_async_copy(w_ref.at[:, pl.ds(first, WIDTH)], own_ref, sem)
-    copy.start()
+def split_kernel(hidden_ref, gain_ref, sent_ref):
     hidden = hidden_ref[...]
     scaled = (hidden.astype(jnp.float32) * gain_ref[...]).astype(jnp.bfloat16)
     both = jnp.concatenate([hidden, scaled], axis=1)
     for y in range(YN):
         for h in range(HN):
             sent_ref[y * HN + h] = both[y * OWN : (y + 1) * OWN]
-    copy.wait()
-
-
-def project_kernel(info_ref, got_ref, w0, w1, w2, w3, table_ref, k_ref, v_ref, mix_ref):
+
+
+def project_kernel(info_ref, got_ref, w0, w1, w2, w3, table_ref, k_ref, mix_ref):
     y = info_ref[2]
     total = None
     square = None
@@ -187,14 +182,15 @@
     bf16, f32 = jnp.bfloat16, jnp.float32
     y, z = lax.axis_index("y").astype(jnp.int32), lax.axis_index("z").astype(jnp.int32)
     head = lax.axis_index(HEAD).astype(jnp.int32)
-    sent, own_columns = pl.pallas_call(
+    own_columns = lax.dynamic_slice_in_dim(w_qkv, head * WIDTH, WIDTH, axis=1)
+    sent = pl.pallas_call(
         split_kernel,
-        in_specs=[SMEM, VMEM, VMEM, ANY],
-        out_specs=[VMEM, VMEM],
-        out_shape=[shape((YN * HN, OWN, 2 * HEAD_DIM), bf16), shape((HEAD_DIM, WIDTH), bf16)],
-        scratch_shapes=[pltpu.SemaphoreType.DMA],
+        in_specs=[VMEM, VMEM],
+        out_specs=VMEM,
+        out_shape=shape((YN * HN, OWN, 2 * HEAD_DIM), bf16),
+        compiler_params=params(56),
         name="split",
-    )(head[None], hidden, norm_gain[None, :], w_qkv)
+    )(hidden, norm_gain[None, :])
     columns = [own_columns] + [
         lax.ppermute(own_columns, "y", [(i, (i + k) % YN) for i in range(YN)]) for k in range(1, YN)
     ]
@@ -204,18 +200,19 @@
     table = rotary_table(lax.dynamic_slice_in_dim(positions, first_own, OWN))
     mix = pl.pallas_call(
         project_kernel,
-        in_specs=[SMEM] + [VMEM] * 8,
+        in_specs=[SMEM] + [VMEM] * 7,
         out_specs=VMEM,
         out_shape=shape((ZN, OWN, WIDTH + HEAD_DIM), f32),
         compiler_params=params(16),
         name="project",
-    )(info, got, *columns, table, cache_keys, cache_values)
+    )(info, got, *columns, table, cache_keys)
     mix = exchange(mix, "z")
     queries, new_rows = pl.pallas_call(
         turn_kernel,
         in_specs=[VMEM, VMEM],
         out_specs=[VMEM, VMEM],
         out_shape=[shape((CTXN, OWN, FLAT), bf16), shape((OWN, 2 * HEAD_DIM), bf16)],
+        compiler_params=params(),
         name="turn",
     )(mix, table)
     queries = exchange(queries, ("z", "y"))
@@ -233,6 +230,7 @@
         in_specs=[VMEM],
         out_specs=VMEM,
         out_shape=shape((CTXN, OWN, FLAT), bf16),
+        compiler_params=params(),
         name="join",
     )(part)
     rows = exchange(rows, CTX).reshape(TQ, FLAT)

time: 148 us -> 142 us (0.959)
  Pallas kernels: 21.2 us -> 16.8 us
    pallas_call x1, Pallas kernels: 2.46 us -> 0.57 us  [per_device(): pl.pallas_call(join_kernel, in_specs=[VMEM], out_specs=VMEM, out_shape=sh...]
    pallas_call x1, Pallas kernels: 2.03 us -> 0.2 us  [per_device(): pl.pallas_call(turn_kernel, in_specs=[VMEM, VMEM], out_specs=[VMEM, VMEM]...]
    all_to_all x1, waiting for transfers between devices: 4.87 us -> 6.41 us  [exchange(): return lax.all_to_all(array, axes, 0, 0, tiled=True)]
    ppermute x3, waiting for transfers between devices: 2.31 us -> 0.77 us  [per_device(): lax.ppermute(own_columns, 'y', [(i, (i + k) % YN) for i in range(YN)])]
  transfers between devices with their start and end apart: 4 -> 4, of which waited for: 2 -> 2; matrix products, arithmetic and copies ran while one was open for 1% -> 1% of each run, Pallas kernels for 0% -> 1%
where the time goes in v3:
time: 142 us; the launch traced here: 141 us
  blocking collectives  101 us (71%)
  Pallas kernels  16.8 us (12%)
  starting transfers between devices  12.4 us (9%)
  waiting for transfers between devices  7.18 us (5%)
  other arithmetic  1.67 us (1%)
  local copies, waits for them, and re-layouts  1.44 us (1%)
    all_to_all x5, blocking collectives, exchange(): return lax.all_to_all(array, axes, 0, 0, tiled=True)  101 us
    pallas_call x1, Pallas kernels, per_device(): pl.pallas_call(attend_kernel, in_specs=[SMEM, VMEM, VMEM, VMEM, VMEM], ou...  13.3 us
    all_to_all x1, starting transfers between devices, exchange(): return lax.all_to_all(array, axes, 0, 0, tiled=True)  7.67 us
    all_to_all x1, waiting for transfers between devices, exchange(): return lax.all_to_all(array, axes, 0, 0, tiled=True)  6.41 us
    ppermute x3, starting transfers between devices, per_device(): lax.ppermute(own_columns, 'y', [(i, (i + k) % YN) for i in range(YN)])  4.68 us
  transfers between devices with their start and end apart: 4, of which 2 were waited for; matrix products, arithmetic and copies ran while one was open for 1% of the time, Pallas kernels for 1%

profile of v3, /device:TPU:1, one launch (start us, length us, event | category | flops | bytes accessed | tf_op | source)
XLA Modules:
  0.0 141.4 jit_solution(15603398215647857776)
XLA Ops:
  0.0 0.0 copy-start
  0.0 0.0 copy-start.1
  0.0 1.4 copy-done
  1.4 3.6 %collective-permute-start.2 = (bf16[128,768]{1,0:T(8,128)(2,1)S(1)}, bf16[128,768]{1,0:T(8,128)(2,1)S(1)}, u32[]{:S(2)}, u32[]{:S(2)}) collective-permute-start(bf16[128,768]{1,0:T(8,128)(2,1)S(1)} %constant_dynamic-slice_fusion.w0), channel_id=1, source_target_pairs={{0,192},{64,0},{128,64},{192,128},{1,193},{65,1},{129,65},{193,129... | collective-permute-start | bytes 589832 | tf_op jit(solution)/shard_map/ppermute | solution.py:195
  5.1 0.3 collective-permute-start.1
  5.4 0.7 collective-permute-start
  6.1 1.4 %split.1 = bf16[32,16,256]{2,1,0:T(8,128)(2,1)} custom-call(bf16[64,128]{1,0:T(8,128)(2,1)} %hidden_ref.1, f32[1,128]{1,0:T(1,128)} %bitcast.9), custom_call_target="tpu_custom_call" | custom-call | tf_op jit(solution)/shard_map/split/pallas_call | solution.py:186
  7.5 7.7 %all-to-all-start = ((bf16[32,16,256]{2,1,0:T(8,128)(2,1)}), bf16[32,16,256]{2,1,0:T(8,128)(2,1)S(1)}, u32[]{:S(2)}, u32[]{:S(2)}) async-start(bf16[32,16,256]{2,1,0:T(8,128)(2,1)} %split.1), calls=%async_computation | async-start | bytes 524288 | tf_op jit(solution)/shard_map/all_to_all | solution.py:48
  15.2 0.8 dynamic-slice_convert_fusion
  16.0 0.1 multiply_cosine_fusion
  16.8 0.1 pad_add_fusion.info_ref
  16.9 0.1 pad_maximum_fusion.table_ref
  16.9 0.0 collective-permute-done.2.w3
  16.9 0.0 collective-permute-done.1.w2
  16.9 0.8 collective-permute-done.w1
  17.7 6.4 %all-to-all-done.got_ref = bf16[32,16,256]{2,1,0:T(8,128)(2,1)S(1)} async-done(((bf16[32,16,256]{2,1,0:T(8,128)(2,1)}), bf16[32,16,256]{2,1,0:T(8,128)(2,1)S(1)}, u32[]{:S(2)}, u32[]{:S(2)}) %all-to-all-start) | async-done | bytes 262176 | tf_op jit(solution)/shard_map/all_to_all | solution.py:48
  24.1 0.0 copy-done.1
  24.1 1.3 project.1
  25.4 0.0 copy-start.2
  25.4 24.5 %all_to_all.30.mix_ref = f32[8,16,896]{2,1,0:T(8,128)S(1)} all-to-all(f32[8,16,896]{2,1,0:T(8,128)S(1)} %project.1), channel_id=1, replica_groups=mesh['y'=4,'z'=8,'x'=4,'core'=2] {'z'}, dimensions={0} | all-to-all | bytes 917504 | tf_op jit(solution)/shard_map/all_to_all | solution.py:48
  50.0 0.2 turn.1
  50.2 19.6 %all_to_all.31.q_ref = bf16[32,16,512]{2,1,0:T(8,128)(2,1)S(1)} all-to-all(bf16[32,16,512]{2,1,0:T(8,128)(2,1)S(1)} %get-tuple-element.7), channel_id=1, replica_groups=mesh['y'=4,'z'=8,'x'=4,'core'=2] {'z','y'}, dimensions={0} | all-to-all | bytes 1048576 | tf_op jit(solution)/shard_map/all_to_all | solution.py:48
  69.7 0.0 copy-done.2
  69.7 13.3 %attend.1 = bf16[32,16,640]{2,1,0:T(8,128)(2,1)S(1)} custom-call(s32[3]{0:T(128)S(1)} %pad_add_fusion.info_ref, bf16[32,16,512]{2,1,0:T(8,128)(2,1)S(1)} %all_to_all.31.q_ref, bf16[4096,128]{1,0:T(8,128)(2,1)S(1)} %copy-done.1, bf16[4096,128]{1,0:T(8,128)(2,1)S(1)} %copy-done.2, bf16[16,256]{1,0:T(8,128)(2,1)S(1)} %get-tuple-element.8.new_ref), custom_call_target="tpu_custom_call" | custom-call | tf_op jit(solution)/shard_map/attend/pallas_call | solution.py:219
  83.0 0.0 copy-start.3
  83.0 20.9 %all_to_all.32.back_ref = bf16[32,16,640]{2,1,0:T(8,128)(2,1)S(1)} all-to-all(bf16[32,16,640]{2,1,0:T(8,128)(2,1)S(1)} %attend.1), channel_id=1, replica_groups=mesh['y'=4,'z'=8,'x'=4,'core'=2] {'y','z'}, dimensions={0} | all-to-all | bytes 1310720 | tf_op jit(solution)/shard_map/all_to_all | solution.py:48
  104.0 0.6 join.1
  104.5 21.1 %all_to_all.33 = bf16[32,16,512]{2,1,0:T(8,128)(2,1)S(1)} all-to-all(bf16[32,16,512]{2,1,0:T(8,128)(2,1)S(1)} %join.1), channel_id=1, replica_groups=mesh['y'=4,'z'=8,'x'=4,'core'=2] {'y','z'}, dimensions={0} | all-to-all | bytes 1048576 | tf_op jit(solution)/shard_map/all_to_all | solution.py:48
  125.6 0.0 copy-done.3
  125.6 0.3 fusion
  125.9 14.9 %all_to_all.34 = f32[8,64,128]{2,1,0:T(8,128)S(1)} all-to-all(f32[8,64,128]{2,1,0:T(8,128)S(1)} %fusion), channel_id=1, replica_groups=mesh['y'=4,'z'=8,'x'=4,'core'=2] {'x','core'}, dimensions={0} | all-to-all | bytes 524288 | tf_op jit(solution)/shard_map/all_to_all | solution.py:48
  140.8 0.6 reduce_sum.9
  (2 shorter events, 0.0 us)
Async XLA Ops:
  0.0 1.4 copy-start
  0.0 24.1 %copy-start.1 = (bf16[4096,128]{1,0:T(8,128)(2,1)S(1)}, bf16[4096,128]{1,0:T(8,128)(2,1)}, u32[]{:S(2)}) copy-start(bf16[4096,128]{1,0:T(8,128)(2,1)} %k_ref.3) | copy-start | bytes 3145732
  1.4 15.5 %collective-permute-start.2 = (bf16[128,768]{1,0:T(8,128)(2,1)S(1)}, bf16[128,768]{1,0:T(8,128)(2,1)S(1)}, u32[]{:S(2)}, u32[]{:S(2)}) collective-permute-start(bf16[128,768]{1,0:T(8,128)(2,1)S(1)} %constant_dynamic-slice_fusion.w0), channel_id=1, source_target_pairs={{0,192},{64,0},{128,64},{192,128},{1,193},{65,1},{129,65},{193,129... | collective-permute-start | bytes 589832 | tf_op jit(solution)/shard_map/ppermute | solution.py:195
  5.1 11.9 %collective-permute-start.1 = (bf16[128,768]{1,0:T(8,128)(2,1)S(1)}, bf16[128,768]{1,0:T(8,128)(2,1)S(1)}, u32[]{:S(2)}, u32[]{:S(2)}) collective-permute-start(bf16[128,768]{1,0:T(8,128)(2,1)S(1)} %constant_dynamic-slice_fusion.w0), channel_id=1, source_target_pairs={{0,128},{64,192},{128,0},{192,64},{1,129},{65,193},{129,1},{193,65... | collective-permute-start | bytes 589832 | tf_op jit(solution)/shard_map/ppermute | solution.py:195
  5.4 12.3 %collective-permute-start = (bf16[128,768]{1,0:T(8,128)(2,1)S(1)}, bf16[128,768]{1,0:T(8,128)(2,1)}, u32[]{:S(2)}, u32[]{:S(2)}) collective-permute-start(bf16[128,768]{1,0:T(8,128)(2,1)S(1)} %constant_dynamic-slice_fusion.w0), channel_id=1, source_target_pairs={{0,64},{64,128},{128,192},{192,0},{1,65},{65,129},{129,193},{193,1... | collective-permute-start | bytes 589832 | tf_op jit(solution)/shard_map/ppermute | solution.py:195
  7.5 16.6 %all-to-all-start = ((bf16[32,16,256]{2,1,0:T(8,128)(2,1)}), bf16[32,16,256]{2,1,0:T(8,128)(2,1)S(1)}, u32[]{:S(2)}, u32[]{:S(2)}) async-start(bf16[32,16,256]{2,1,0:T(8,128)(2,1)} %split.1), calls=%async_computation | async-start | bytes 524288 | tf_op jit(solution)/shard_map/all_to_all | solution.py:48
  25.4 44.3 %copy-start.2 = (bf16[4096,128]{1,0:T(8,128)(2,1)S(1)}, bf16[4096,128]{1,0:T(8,128)(2,1)}, u32[]{:S(2)}) copy-start(bf16[4096,128]{1,0:T(8,128)(2,1)} %v_ref.1) | copy-start | bytes 3145732
  83.0 42.6 %copy-start.3 = (bf16[512,128]{1,0:T(8,128)(2,1)S(1)}, bf16[512,128]{1,0:T(8,128)(2,1)}, u32[]{:S(2)}) copy-start(bf16[512,128]{1,0:T(8,128)(2,1)} %param.15) | copy-start | bytes 393220

commit v4 on v3

v4 whole, which is shorter than its diff:
```python
import functools
import math

import jax
import jax.numpy as jnp
from jax import lax
from jax.experimental import pallas as pl
from jax.experimental.pallas import tpu as pltpu
from jax.sharding import Mesh
from jax.sharding import PartitionSpec as P

D = 4096
HEADS = 32
KV_HEADS = 8
HEAD_DIM = 128
GROUP = HEADS // KV_HEADS
SLOTS = GROUP + 2
WIDTH = SLOTS * HEAD_DIM
FLAT = GROUP * HEAD_DIM
TQ = 512
KEYS_DEV = 4096
NEG_FILL = -1e30
SCALE = 1.0 / math.sqrt(HEAD_DIM)
SCALE2 = SCALE * 1.4426950408889634

YN, ZN, XN, CN = 4, 8, 4, 2
HN = XN * CN
CTXN = YN * ZN
CTX = ("y", "z")
HEAD = ("x", "core")
OWN = TQ // CTXN
TAIL = 128
KEY_TILE = 512
SHARE = OWN * ZN

VMEM = pl.BlockSpec(memory_space=pltpu.VMEM)
SMEM = pl.BlockSpec(memory_space=pltpu.SMEM)


def shape(dims, kind):
    return jax.ShapeDtypeStruct(dims, kind)


def params(mib=8):
    return pltpu.CompilerParams(vmem_limit_bytes=mib * 1024 * 1024)


def exchange(array, axes):
    return lax.all_to_all(array, axes, 0, 0, tiled=True)


def along_y(array, shift):
    if shift == 0:
        return array
    return lax.ppermute(array, "y", [(i, (i + shift) % YN) for i in range(YN)])


def split_kernel(hidden_ref, gain_ref, sent_ref):
    hidden = hidden_ref[...]
    scaled = (hidden.astype(jnp.float32) * gain_ref[...]).astype(jnp.bfloat16)
    both = jnp.concatenate([hidden, scaled], axis=1)
    for y in range(YN):
        for h in range(HN):
            sent_ref[y * HN + h] = both[y * OWN : (y + 1) * OWN]


def project_kernel(info_ref, got_ref, w0, w1, w2, w3, table_ref, k_ref, mix_ref):
    y = info_ref[2]
    total = None
    square = None
    for shift, w in enumerate((w0, w1, w2, w3)):
        source = lax.rem(y + YN - shift, YN)
        part = got_ref[pl.ds(source * HN, HN)].reshape(HN * OWN, 2 * HEAD_DIM)
        term = jnp.dot(part[:, HEAD_DIM:], w[...], preferred_element_type=jnp.float32)
        plain = part[:, :HEAD_DIM].astype(jnp.float32)
        own = jnp.sum(plain * plain, axis=1, keepdims=True)
        total = term if total is None else total + term
        square = own if square is None else square + own
    mix_ref[:, :, :WIDTH] = total.reshape(ZN, OWN, WIDTH)
    mix_ref[:, :, WIDTH:] = jnp.broadcast_to(square, (HN * OWN, HEAD_DIM)).reshape(ZN, OWN, HEAD_DIM)


def turn_kernel(mix_ref, table_ref, queries_ref, new_ref):
    share = mix_ref[0]
    for z in range(1, ZN):
        share = share + mix_ref[z]
    inv_rms = lax.rsqrt(share[:, WIDTH : WIDTH + 1] / D + 1e-05)
    cosine, sine = table_ref[:, :HEAD_DIM], table_ref[:, HEAD_DIM:]
    slots = []
    for s in range(SLOTS):
        value = share[:, s * HEAD_DIM : (s + 1) * HEAD_DIM] * inv_rms
        if s <= GROUP:
            value = value * cosine + pltpu.roll(value, HEAD_DIM // 2, 1) * sine
        slots.append(value.astype(jnp.bfloat16))
    queries = jnp.concatenate(slots[:GROUP], axis=1)
    for z in range(ZN):
        queries_ref[z] = queries
    new_ref[...] = jnp.concatenate(slots[GROUP:], axis=1)


def packed_levels(level):
    high = level.astype(jnp.bfloat16).astype(jnp.float32)
    mid = (level - high).astype(jnp.bfloat16).astype(jnp.float32)
    low = (level - high) - mid
    return (high + pltpu.roll(mid, GROUP, 1) + pltpu.roll(low, 2 * GROUP, 1)).astype(jnp.bfloat16)


def levels_of(parts):
    parts = parts.astype(jnp.float32)
    level = parts + pltpu.roll(parts, HEAD_DIM - GROUP, 1) + pltpu.roll(parts, HEAD_DIM - 2 * GROUP, 1)
    spot = lax.broadcasted_iota(jnp.int32, parts.shape, 1)
    return jnp.where(spot < GROUP, level, 0.0)


def attend_kernel(shift, info_ref, q_ref, k_ref, v_ref, new_ref, o_ref):
    count = info_ref[0]
    first_own = info_ref[1]
    source = lax.rem(info_ref[2] + YN - shift, YN)
    rows = GROUP * SHARE

    def lane(n):
        return lax.broadcasted_iota(jnp.int32, (n, HEAD_DIM), 1)

    def first_lane(n):
        return jnp.where(lane(n) == 0, 1.0, 0.0).astype(jnp.bfloat16)

    def product(a, b):
        return lax.dot_general(a, b, (((1,), (1,)), ((), ())), preferred_element_type=jnp.float32)

    place = lax.broadcasted_iota(jnp.int32, (rows, TAIL), 0) % SHARE
    asked = (place // OWN) * (OWN * YN) + source * OWN + place % OWN
    own = lax.broadcasted_iota(jnp.int32, (rows, TAIL), 1)
    seen = (own < OWN) & (own + first_own <= asked)
    blank = jnp.zeros((TAIL - OWN, HEAD_DIM), jnp.bfloat16)
    tail_keys = jnp.concatenate([new_ref[:, :HEAD_DIM], blank], axis=0)
    tail_values = jnp.concatenate([new_ref[:, HEAD_DIM:], blank], axis=0)
    queries = jnp.concatenate(
        [q_ref[:, :, s * HEAD_DIM : (s + 1) * HEAD_DIM].reshape(SHARE, HEAD_DIM) for s in range(GROUP)], axis=0
    )
    wide = jnp.concatenate([queries, first_lane(rows)], axis=1)
    best = jnp.full((rows, 1), NEG_FILL, jnp.float32)
    sums = jnp.zeros((rows, 2 * HEAD_DIM), jnp.float32)
    for start in range(0, KEYS_DEV + TAIL, KEY_TILE):
        if start < KEYS_DEV:
            index = lax.broadcasted_iota(jnp.int32, (KEY_TILE, HEAD_DIM), 0) + start
            hide = jnp.where((lane(KEY_TILE) == 0) & (index >= count), NEG_FILL, 0.0).astype(jnp.bfloat16)
            keys = jnp.concatenate([k_ref[start : start + KEY_TILE, :], hide], axis=1)
            values = jnp.concatenate([v_ref[start : start + KEY_TILE, :], first_lane(KEY_TILE)], axis=1)
            scores = product(wide, keys)
        else:
            values = jnp.concatenate([tail_values, first_lane(TAIL)], axis=1)
            scores = jnp.where(seen, product(queries, tail_keys), NEG_FILL)
        higher = jnp.maximum(best, jnp.max(scores, axis=1, keepdims=True))
        weights = jnp.exp2(scores * SCALE2 - higher * SCALE2).astype(jnp.bfloat16)
        sums = sums * jnp.exp2((best - higher) * SCALE2) + jnp.dot(
            weights, values, preferred_element_type=jnp.float32
        )
        best = higher
    total = sums[:, HEAD_DIM : HEAD_DIM + 1]
    outs = (sums[:, :HEAD_DIM] * (1.0 / total)).astype(jnp.bfloat16)
    level = best * SCALE + jnp.log(total)
    spot = lane(SHARE)
    levels = jnp.zeros((SHARE, HEAD_DIM), jnp.float32)
    for s in range(GROUP):
        here = slice(s * SHARE, (s + 1) * SHARE)
        o_ref[:, :, s * HEAD_DIM : (s + 1) * HEAD_DIM] = outs[here].reshape(ZN, OWN, HEAD_DIM)
        levels = jnp.where(spot == s, level[here], levels)
    o_ref[:, :, FLAT:] = packed_levels(levels).reshape(ZN, OWN, HEAD_DIM)


def merge_kernel(own_ref, one_ref, two_ref, three_ref, w1, w2, w3, o_ref):
    refs = (own_ref, one_ref, two_ref, three_ref)
    levels = [levels_of(ref[:, :, FLAT:].reshape(SHARE, HEAD_DIM)) for ref in refs]
    most = levels[0]
    for level in levels[1:]:
        most = jnp.maximum(most, level)
    factors = [jnp.exp(level - most) for level in levels]
    total = factors[0] + factors[1] + factors[2] + factors[3]
    factors = [factor * (1.0 / total) for factor in factors]
    for s in range(GROUP):
        here = slice(s * HEAD_DIM, (s + 1) * HEAD_DIM)
        joined = jnp.zeros((SHARE, HEAD_DIM), jnp.float32)
        for ref, factor in zip(refs, factors):
            joined = joined + ref[:, :, here].reshape(SHARE, HEAD_DIM).astype(jnp.float32) * factor[:, s : s + 1]
        o_ref[:, :, here] = joined.astype(jnp.bfloat16).reshape(ZN, OWN, HEAD_DIM)
    spot = lax.broadcasted_iota(jnp.int32, most.shape, 1)
    level = jnp.where(spot < GROUP, most + jnp.log(total), 0.0)
    o_ref[:, :, FLAT:] = packed_levels(level).reshape(ZN, OWN, HEAD_DIM)


def join_kernel(back_ref, rows_ref):
    level = levels_of(back_ref[:, :, FLAT:].reshape(SHARE, HEAD_DIM)).reshape(ZN, OWN, HEAD_DIM)
    factor = jnp.exp(level - jnp.max(level, axis=0, keepdims=True))
    factor = factor * (1.0 / jnp.sum(factor, axis=0, keepdims=True))
    joined = []
    for s in range(GROUP):
        total = jnp.zeros((OWN, HEAD_DIM), jnp.float32)
        for z in range(ZN):
            outs = back_ref[z, :, s * HEAD_DIM : (s + 1) * HEAD_DIM].astype(jnp.float32)
            total = total + outs * factor[z, :, s : s + 1]
        joined.append(total.astype(jnp.bfloat16))
    attended = jnp.concatenate(joined, axis=1)
    for z in range(ZN):
        rows_ref[z] = attended


def finish_kernel(info_ref, rows_ref, w0, w1, w2, w3, o_ref):
    rows = rows_ref[...].reshape(SHARE, FLAT)
    for shift, w in enumerate((w0, w1, w2, w3)):
        source = lax.rem(info_ref[2] + YN - shift, YN)
        term = jnp.dot(rows, w[...], preferred_element_type=jnp.float32)
        o_ref[pl.ds(source * HN, HN)] = term.reshape(HN, OWN, HEAD_DIM)


def rotary_table(positions):
    half = HEAD_DIM // 2
    frequency = 500000.0 ** (-(jnp.arange(half, dtype=jnp.float32) * 2.0 / HEAD_DIM))
    angles = positions.astype(jnp.float32)[:, None] * frequency[None, :]
    cosine, sine = jnp.cos(angles), jnp.sin(angles)
    return jnp.concatenate([cosine, cosine, -sine, sine], axis=1)


def per_device(hidden, norm_gain, w_qkv, positions, cache_keys, cache_values, key_counts, w_out):
    bf16, f32 = jnp.bfloat16, jnp.float32
    y, z = lax.axis_index("y").astype(jnp.int32), lax.axis_index("z").astype(jnp.int32)
    head = lax.axis_index(HEAD).astype(jnp.int32)
    own_columns = lax.dynamic_slice_in_dim(w_qkv, head * WIDTH, WIDTH, axis=1)
    sent = pl.pallas_call(
        split_kernel,
        in_specs=[VMEM, VMEM],
        out_specs=VMEM,
        out_shape=shape((YN * HN, OWN, 2 * HEAD_DIM), bf16),
        compiler_params=params(56),
        name="split",
    )(hidden, norm_gain[None, :])
    columns = [along_y(own_columns, shift) for shift in range(YN)]
    got = exchange(sent, ("y", "x", "core"))
    first_own = z * (OWN * YN) + y * OWN
    info = jnp.stack([key_counts[0], first_own, y])
    table = rotary_table(lax.dynamic_slice_in_dim(positions, first_own, OWN))
    mix = pl.pallas_call(
        project_kernel,
        in_specs=[SMEM] + [VMEM] * 7,
        out_specs=VMEM,
        out_shape=shape((ZN, OWN, WIDTH + HEAD_DIM), f32),
        compiler_params=params(16),
        name="project",
    )(info, got, *columns, table, cache_keys)
    mix = exchange(mix, "z")
    queries, new_rows = pl.pallas_call(
        turn_kernel,
        in_specs=[VMEM, VMEM],
        out_specs=[VMEM, VMEM],
        out_shape=[shape((ZN, OWN, FLAT), bf16), shape((OWN, 2 * HEAD_DIM), bf16)],
        compiler_params=params(),
        name="turn",
    )(mix, table)
    queries = exchange(queries, "z")
    parts = []
    for shift in range(YN):
        part = pl.pallas_call(
            functools.partial(attend_kernel, shift),
            in_specs=[SMEM, VMEM, VMEM, VMEM, VMEM],
            out_specs=VMEM,
            out_shape=shape((ZN, OWN, FLAT + HEAD_DIM), bf16),
            compiler_params=params(24),
            cost_estimate=pl.CostEstimate(flops=4_000_000_000, bytes_accessed=0, transcendentals=0),
            name="attend",
        )(info, along_y(queries, shift), cache_keys, cache_values, new_rows)
        parts.append(along_y(part, -shift))
    w_outs = [along_y(w_out, shift) for shift in range(YN)]
    part = pl.pallas_call(
        merge_kernel,
        in_specs=[VMEM] * 7,
        out_specs=VMEM,
        out_shape=shape((ZN, OWN, FLAT + HEAD_DIM), bf16),
        compiler_params=params(),
        name="merge",
    )(*parts, *w_outs[1:])
    part = exchange(part, "z")
    rows = pl.pallas_call(
        join_kernel,
        in_specs=[VMEM],
        out_specs=VMEM,
        out_shape=shape((ZN, OWN, FLAT), bf16),
        compiler_params=params(),
        name="join",
    )(part)
    rows = exchange(rows, "z")
    result = pl.pallas_call(
        finish_kernel,
        in_specs=[SMEM] + [VMEM] * 5,
        out_specs=VMEM,
        out_shape=shape((YN * HN, OWN, HEAD_DIM), f32),
        compiler_params=params(),
        name="finish",
    )(info, rows, *w_outs)
    result = exchange(result, ("y", "x", "core")).reshape(YN, HN, OWN, HEAD_DIM)
    return jnp.sum(result, axis=1).reshape(YN * OWN, HEAD_DIM).astype(bf16)


def solution(mesh):
    fine = Mesh(mesh.devices.reshape(YN, ZN, XN, CN), ("y", "z", "x", "core"))
    return jax.shard_map(
        per_device,
        mesh=fine,
        in_specs=(
            P(HEAD, CTX),
            P(CTX),
            P(CTX, None),
            P(),
            P(CTX, HEAD),
            P(CTX, HEAD),
            P(CTX),
            P(HEAD, CTX),
        ),
        out_specs=P(HEAD, CTX),
        check_vma=False,
    )
```

time: 142 us -> 134 us (0.944)
  blocking collectives: 101 us -> 77.3 us
  starting transfers between devices: 12.4 us -> 24 us
  Pallas kernels: 16.8 us -> 21.4 us
    all_to_all x5, blocking collectives: 101 us -> 77.3 us  [exchange(): return lax.all_to_all(array, axes, 0, 0, tiled=True)]
    ppermute x3 -> x12, starting transfers between devices: 4.68 us -> 17.9 us  [along_y(): return lax.ppermute(array, 'y', [(i, (i + shift) % YN) for i in range(YN)])]
    pallas_call x1 -> x6, Pallas kernels: 13.3 us -> 18.2 us  [the longest x4 16.8 us: per_device(): pl.pallas_call(functools.partial(attend_kernel, shift), in_specs=[SMEM, V...]
    all_to_all x1, starting transfers between devices: 7.67 us -> 6.08 us  [exchange(): return lax.all_to_all(array, axes, 0, 0, tiled=True)]
  transfers between devices with their start and end apart: 4 -> 13, of which waited for: 2 -> 1; matrix products, arithmetic and copies ran while one was open for 1% -> 1% of each run, Pallas kernels for 1% -> 14%
where the time goes in v4:
time: 134 us
  blocking collectives  77.3 us (58%)
  starting transfers between devices  24 us (18%)
  Pallas kernels  21.4 us (16%)
  waiting for transfers between devices  7.2 us (5%)
  other arithmetic  1.66 us (1%)
  local copies, waits for them, and re-layouts  1.43 us (1%)
    all_to_all x5, blocking collectives, exchange(): return lax.all_to_all(array, axes, 0, 0, tiled=True)  77.3 us
    ppermute x12, starting transfers between devices, along_y(): return lax.ppermute(array, 'y', [(i, (i + shift) % YN) for i in range(YN)])  17.9 us
    pallas_call x4, Pallas kernels, per_device(): pl.pallas_call(functools.partial(attend_kernel, shift), in_specs=[SMEM, V...  16.8 us
    all_to_all x1, waiting for transfers between devices, exchange(): return lax.all_to_all(array, axes, 0, 0, tiled=True)  7.17 us
    all_to_all x1, starting transfers between devices, exchange(): return lax.all_to_all(array, axes, 0, 0, tiled=True)  6.08 us
  transfers between devices with their start and end apart: 13, of which 1 were waited for; matrix products, arithmetic and copies ran while one was open for 1% of the time, Pallas kernels for 14%

profile of v4, /device:TPU:1, one launch (start us, length us, event | category | flops | bytes accessed | tf_op | source)
XLA Modules:
  0.0 133.9 jit_solution(7311256889780580978)
XLA Ops:
  0.0 1.4 %copy-done = bf16[128,6144]{1,0:T(8,128)(2,1)S(1)} copy-done((bf16[128,6144]{1,0:T(8,128)(2,1)S(1)}, bf16[128,6144]{1,0:T(8,128)(2,1)}, u32[]{:S(2)}) %copy-start) | copy-done | bytes 1572888
  1.4 2.2 %collective-permute-start = (bf16[128,768]{1,0:T(8,128)(2,1)S(1)}, bf16[128,768]{1,0:T(8,128)(2,1)S(1)}, u32[]{:S(2)}, u32[]{:S(2)}) collective-permute-start(bf16[128,768]{1,0:T(8,128)(2,1)S(1)} %constant_dynamic-slice_fusion.w0), channel_id=1, source_target_pairs={{0,64},{64,128},{128,192},{192,0},{1,65},{65,129},{129,193},{193,1... | collective-permute-start | bytes 589832 | tf_op jit(solution)/shard_map/ppermute | solution.py:55
  3.6 2.6 %collective-permute-start.1 = (bf16[128,768]{1,0:T(8,128)(2,1)S(1)}, bf16[128,768]{1,0:T(8,128)(2,1)S(1)}, u32[]{:S(2)}, u32[]{:S(2)}) collective-permute-start(bf16[128,768]{1,0:T(8,128)(2,1)S(1)} %constant_dynamic-slice_fusion.w0), channel_id=1, source_target_pairs={{0,128},{64,192},{128,0},{192,64},{1,129},{65,193},{129,1},{193,65... | collective-permute-start | bytes 589832 | tf_op jit(solution)/shard_map/ppermute | solution.py:55
  6.3 1.1 collective-permute-start.2
  7.3 1.4 %split.1 = bf16[32,16,256]{2,1,0:T(8,128)(2,1)} custom-call(bf16[64,128]{1,0:T(8,128)(2,1)} %hidden_ref.1, f32[1,128]{1,0:T(1,128)} %bitcast.6), custom_call_target="tpu_custom_call" | custom-call | tf_op jit(solution)/shard_map/split/pallas_call | solution.py:228
  8.8 6.1 %all-to-all-start = ((bf16[32,16,256]{2,1,0:T(8,128)(2,1)}), bf16[32,16,256]{2,1,0:T(8,128)(2,1)S(1)}, u32[]{:S(2)}, u32[]{:S(2)}) async-start(bf16[32,16,256]{2,1,0:T(8,128)(2,1)} %split.1), calls=%async_computation | async-start | bytes 524288 | tf_op jit(solution)/shard_map/all_to_all | solution.py:49
  14.9 0.8 dynamic-slice_convert_fusion
  15.6 0.1 multiply_cosine_fusion
  16.4 0.1 pad_add_fusion.info_ref
  16.5 0.1 pad_maximum_fusion.table_ref
  16.6 0.0 collective-permute-done.w1
  16.6 0.0 collective-permute-done.1.w2
  16.6 0.0 collective-permute-done.2.w3
  16.6 7.2 %all-to-all-done.got_ref = bf16[32,16,256]{2,1,0:T(8,128)(2,1)S(1)} async-done(((bf16[32,16,256]{2,1,0:T(8,128)(2,1)}), bf16[32,16,256]{2,1,0:T(8,128)(2,1)S(1)}, u32[]{:S(2)}, u32[]{:S(2)}) %all-to-all-start) | async-done | bytes 262176 | tf_op jit(solution)/shard_map/all_to_all | solution.py:49
  23.8 1.4 %project.1 = f32[8,16,896]{2,1,0:T(8,128)S(1)} custom-call(s32[3]{0:T(128)S(1)} %pad_add_fusion.info_ref, bf16[32,16,256]{2,1,0:T(8,128)(2,1)S(1)} %all-to-all-done.got_ref, bf16[128,768]{1,0:T(8,128)(2,1)S(1)} %constant_dynamic-slice_fusion.w0, bf16[128,768]{1,0:T(8,128)(2,1)S(1)} %collective-permute-done.w1, ...), custom_call_target="tpu_custom_call" | custom-call | tf_op jit(solution)/shard_map/project/pallas_call | solution.py:241
  25.1 24.4 %all_to_all.30.mix_ref = f32[8,16,896]{2,1,0:T(8,128)S(1)} all-to-all(f32[8,16,896]{2,1,0:T(8,128)S(1)} %project.1), channel_id=1, replica_groups=mesh['y'=4,'z'=8,'x'=4,'core'=2] {'z'}, dimensions={0} | all-to-all | bytes 917504 | tf_op jit(solution)/shard_map/all_to_all | solution.py:49
  49.5 0.2 turn.1
  49.7 10.3 %all_to_all.31.q_ref = bf16[8,16,512]{2,1,0:T(8,128)(2,1)S(1)} all-to-all(bf16[8,16,512]{2,1,0:T(8,128)(2,1)S(1)} %get-tuple-element.7), channel_id=1, replica_groups=mesh['y'=4,'z'=8,'x'=4,'core'=2] {'z'}, dimensions={0} | all-to-all | bytes 262144 | tf_op jit(solution)/shard_map/all_to_all | solution.py:49
  60.0 1.4 %collective-permute-start.7 = (bf16[8,16,512]{2,1,0:T(8,128)(2,1)S(1)}, bf16[8,16,512]{2,1,0:T(8,128)(2,1)S(1)}, u32[]{:S(2)}, u32[]{:S(2)}) collective-permute-start(bf16[8,16,512]{2,1,0:T(8,128)(2,1)S(1)} %all_to_all.31.q_ref), channel_id=1, source_target_pairs={{0,192},{64,0},{128,64},{192,128},{1,193},{65,1},{129,65},{193,129... | collective-permute-start | bytes 393224 | tf_op jit(solution)/shard_map/ppermute | solution.py:55
  61.3 0.0 copy-done.2
  61.3 1.3 collective-permute-start.10
  62.6 1.2 collective-permute-start.11
  63.8 0.2 collective-permute-start.9
  64.1 1.7 %collective-permute-start.5 = (bf16[8,16,512]{2,1,0:T(8,128)(2,1)S(1)}, bf16[8,16,512]{2,1,0:T(8,128)(2,1)S(1)}, u32[]{:S(2)}, u32[]{:S(2)}) collective-permute-start(bf16[8,16,512]{2,1,0:T(8,128)(2,1)S(1)} %all_to_all.31.q_ref), channel_id=1, source_target_pairs={{0,128},{64,192},{128,0},{192,64},{1,129},{65,193},{129,1},{193,65... | collective-permute-start | bytes 393224 | tf_op jit(solution)/shard_map/ppermute | solution.py:55
  65.8 0.0 collective-permute-done.7.q_ref
  65.8 1.3 collective-permute-start.3
  67.1 4.2 %attend.7 = bf16[8,16,640]{2,1,0:T(8,128)(2,1)S(1)} custom-call(s32[3]{0:T(128)S(1)} %pad_add_fusion.info_ref, bf16[8,16,512]{2,1,0:T(8,128)(2,1)S(1)} %collective-permute-done.7.q_ref, bf16[4096,128]{1,0:T(8,128)(2,1)S(1)} %copy-done.1, bf16[4096,128]{1,0:T(8,128)(2,1)S(1)} %copy-done.3, bf16[16,256]{1,0:T(8,128)(2,1)S(1)} %get-tuple-element.8.new_ref), custom_call_target="tpu_custom_call" | custom-call | flops 4000000000 | tf_op jit(solution)/shard_map/attend/pallas_call | solution.py:261
  71.3 0.0 collective-permute-done.5.q_ref
  71.3 2.2 %collective-permute-start.8 = (bf16[8,16,640]{2,1,0:T(8,128)(2,1)S(1)}, bf16[8,16,640]{2,1,0:T(8,128)(2,1)S(1)}, u32[]{:S(2)}, u32[]{:S(2)}) collective-permute-start(bf16[8,16,640]{2,1,0:T(8,128)(2,1)S(1)} %attend.7), channel_id=1, source_target_pairs={{0,64},{64,128},{128,192},{192,0},{1,65},{65,129},{129,193},{193,1... | collective-permute-start | bytes 491528 | tf_op jit(solution)/shard_map/ppermute | solution.py:55
  73.5 4.2 %attend.6 = bf16[8,16,640]{2,1,0:T(8,128)(2,1)S(1)} custom-call(s32[3]{0:T(128)S(1)} %pad_add_fusion.info_ref, bf16[8,16,512]{2,1,0:T(8,128)(2,1)S(1)} %collective-permute-done.5.q_ref, bf16[4096,128]{1,0:T(8,128)(2,1)S(1)} %copy-done.1, bf16[4096,128]{1,0:T(8,128)(2,1)S(1)} %copy-done.3, bf16[16,256]{1,0:T(8,128)(2,1)S(1)} %get-tuple-element.8.new_ref), custom_call_target="tpu_custom_call" | custom-call | flops 4000000000 | tf_op jit(solution)/shard_map/attend/pallas_call | solution.py:261
  77.7 0.0 collective-permute-done.3.q_ref
  77.7 1.3 collective-permute-start.6
  79.0 4.2 %attend.5 = bf16[8,16,640]{2,1,0:T(8,128)(2,1)S(1)} custom-call(s32[3]{0:T(128)S(1)} %pad_add_fusion.info_ref, bf16[8,16,512]{2,1,0:T(8,128)(2,1)S(1)} %collective-permute-done.3.q_ref, bf16[4096,128]{1,0:T(8,128)(2,1)S(1)} %copy-done.1, bf16[4096,128]{1,0:T(8,128)(2,1)S(1)} %copy-done.3, bf16[16,256]{1,0:T(8,128)(2,1)S(1)} %get-tuple-element.8.new_ref), custom_call_target="tpu_custom_call" | custom-call | flops 4000000000 | tf_op jit(solution)/shard_map/attend/pallas_call | solution.py:261
  83.2 0.0 collective-permute-done.10.w2
  83.2 1.5 %collective-permute-start.4 = (bf16[8,16,640]{2,1,0:T(8,128)(2,1)S(1)}, bf16[8,16,640]{2,1,0:T(8,128)(2,1)S(1)}, u32[]{:S(2)}, u32[]{:S(2)}) collective-permute-start(bf16[8,16,640]{2,1,0:T(8,128)(2,1)S(1)} %attend.5), channel_id=1, source_target_pairs={{0,192},{64,0},{128,64},{192,128},{1,193},{65,1},{129,65},{193,129... | collective-permute-start | bytes 491528 | tf_op jit(solution)/shard_map/ppermute | solution.py:55
  84.7 4.2 %attend.4.own_ref = bf16[8,16,640]{2,1,0:T(8,128)(2,1)S(1)} custom-call(s32[3]{0:T(128)S(1)} %pad_add_fusion.info_ref, bf16[8,16,512]{2,1,0:T(8,128)(2,1)S(1)} %all_to_all.31.q_ref, bf16[4096,128]{1,0:T(8,128)(2,1)S(1)} %copy-done.1, bf16[4096,128]{1,0:T(8,128)(2,1)S(1)} %copy-done.3, bf16[16,256]{1,0:T(8,128)(2,1)S(1)} %get-tuple-element.8.new_ref), custom_call_target="tpu_custom_call" | custom-call | flops 4000000000 | tf_op jit(solution)/shard_map/attend/pallas_call | solution.py:261
  88.9 0.0 collective-permute-done.11.w3
  88.9 0.0 collective-permute-done.9.w1
  88.9 0.0 collective-permute-done.8.three_ref
  88.9 0.0 collective-permute-done.6.two_ref
  88.9 0.0 collective-permute-done.4.one_ref
  88.9 0.6 merge.1
  89.5 10.8 %all_to_all.32.back_ref = bf16[8,16,640]{2,1,0:T(8,128)(2,1)S(1)} all-to-all(bf16[8,16,640]{2,1,0:T(8,128)(2,1)S(1)} %merge.1), channel_id=1, replica_groups=mesh['y'=4,'z'=8,'x'=4,'core'=2] {'z'}, dimensions={0} | all-to-all | bytes 327680 | tf_op jit(solution)/shard_map/all_to_all | solution.py:49
  100.3 0.3 join.1
  100.5 10.3 %all_to_all.33.rows_ref = bf16[8,16,512]{2,1,0:T(8,128)(2,1)S(1)} all-to-all(bf16[8,16,512]{2,1,0:T(8,128)(2,1)S(1)} %join.1), channel_id=1, replica_groups=mesh['y'=4,'z'=8,'x'=4,'core'=2] {'z'}, dimensions={0} | all-to-all | bytes 262144 | tf_op jit(solution)/shard_map/all_to_all | solution.py:49
  110.8 0.8 finish.1
  111.7 21.6 %all_to_all.34 = f32[32,16,128]{2,1,0:T(8,128)S(1)} all-to-all(f32[32,16,128]{2,1,0:T(8,128)S(1)} %finish.1), channel_id=1, replica_groups=mesh['y'=4,'z'=8,'x'=4,'core'=2] {'y','x','core'}, dimensions={0} | all-to-all | bytes 524288 | tf_op jit(solution)/shard_map/all_to_all | solution.py:49
  133.3 0.6 bitcast_reduce_fusion
  (8 shorter events, 0.0 us)
Async XLA Ops:
  0.0 1.4 %copy-start = (bf16[128,6144]{1,0:T(8,128)(2,1)S(1)}, bf16[128,6144]{1,0:T(8,128)(2,1)}, u32[]{:S(2)}) copy-start(bf16[128,6144]{1,0:T(8,128)(2,1)} %param.10) | copy-start | bytes 4718596
  0.0 23.7 %copy-start.1 = (bf16[4096,128]{1,0:T(8,128)(2,1)S(1)}, bf16[4096,128]{1,0:T(8,128)(2,1)}, u32[]{:S(2)}) copy-start(bf16[4096,128]{1,0:T(8,128)(2,1)} %k_ref.9) | copy-start | bytes 3145732
  1.4 15.1 %collective-permute-start = (bf16[128,768]{1,0:T(8,128)(2,1)S(1)}, bf16[128,768]{1,0:T(8,128)(2,1)S(1)}, u32[]{:S(2)}, u32[]{:S(2)}) collective-permute-start(bf16[128,768]{1,0:T(8,128)(2,1)S(1)} %constant_dynamic-slice_fusion.w0), channel_id=1, source_target_pairs={{0,64},{64,128},{128,192},{192,0},{1,65},{65,129},{129,193},{193,1... | collective-permute-start | bytes 589832 | tf_op jit(solution)/shard_map/ppermute | solution.py:55
  3.6 12.9 %collective-permute-start.1 = (bf16[128,768]{1,0:T(8,128)(2,1)S(1)}, bf16[128,768]{1,0:T(8,128)(2,1)S(1)}, u32[]{:S(2)}, u32[]{:S(2)}) collective-permute-start(bf16[128,768]{1,0:T(8,128)(2,1)S(1)} %constant_dynamic-slice_fusion.w0), channel_id=1, source_target_pairs={{0,128},{64,192},{128,0},{192,64},{1,129},{65,193},{129,1},{193,65... | collective-permute-start | bytes 589832 | tf_op jit(solution)/shard_map/ppermute | solution.py:55
  6.3 10.3 %collective-permute-start.2 = (bf16[128,768]{1,0:T(8,128)(2,1)S(1)}, bf16[128,768]{1,0:T(8,128)(2,1)}, u32[]{:S(2)}, u32[]{:S(2)}) collective-permute-start(bf16[128,768]{1,0:T(8,128)(2,1)S(1)} %constant_dynamic-slice_fusion.w0), channel_id=1, source_target_pairs={{0,192},{64,0},{128,64},{192,128},{1,193},{65,1},{129,65},{193,129... | collective-permute-start | bytes 589832 | tf_op jit(solution)/shard_map/ppermute | solution.py:55
  8.8 15.0 %all-to-all-start = ((bf16[32,16,256]{2,1,0:T(8,128)(2,1)}), bf16[32,16,256]{2,1,0:T(8,128)(2,1)S(1)}, u32[]{:S(2)}, u32[]{:S(2)}) async-start(bf16[32,16,256]{2,1,0:T(8,128)(2,1)} %split.1), calls=%async_computation | async-start | bytes 524288 | tf_op jit(solution)/shard_map/all_to_all | solution.py:49
  23.7 37.6 %copy-start.2 = (bf16[512,128]{1,0:T(8,128)(2,1)S(1)}, bf16[512,128]{1,0:T(8,128)(2,1)}, u32[]{:S(2)}) copy-start(bf16[512,128]{1,0:T(8,128)(2,1)} %w0.1) | copy-start | bytes 393220
  23.7 43.3 %copy-start.3 = (bf16[4096,128]{1,0:T(8,128)(2,1)S(1)}, bf16[4096,128]{1,0:T(8,128)(2,1)}, u32[]{:S(2)}) copy-start(bf16[4096,128]{1,0:T(8,128)(2,1)} %v_ref.7) | copy-start | bytes 3145732
  60.0 5.8 %collective-permute-start.7 = (bf16[8,16,512]{2,1,0:T(8,128)(2,1)S(1)}, bf16[8,16,512]{2,1,0:T(8,128)(2,1)S(1)}, u32[]{:S(2)}, u32[]{:S(2)}) collective-permute-start(bf16[8,16,512]{2,1,0:T(8,128)(2,1)S(1)} %all_to_all.31.q_ref), channel_id=1, source_target_pairs={{0,192},{64,0},{128,64},{192,128},{1,193},{65,1},{129,65},{193,129... | collective-permute-start | bytes 393224 | tf_op jit(solution)/shard_map/ppermute | solution.py:55
  61.3 21.8 %collective-permute-start.10 = (bf16[512,128]{1,0:T(8,128)(2,1)S(1)}, bf16[512,128]{1,0:T(8,128)(2,1)S(1)}, u32[]{:S(2)}, u32[]{:S(2)}) collective-permute-start(bf16[512,128]{1,0:T(8,128)(2,1)S(1)} %copy-done.2), channel_id=1, source_target_pairs={{0,128},{64,192},{128,0},{192,64},{1,129},{65,193},{129,1},{193,65... | collective-permute-start | bytes 393224 | tf_op jit(solution)/shard_map/ppermute | solution.py:55
  62.6 26.3 %collective-permute-start.11 = (bf16[512,128]{1,0:T(8,128)(2,1)S(1)}, bf16[512,128]{1,0:T(8,128)(2,1)S(1)}, u32[]{:S(2)}, u32[]{:S(2)}) collective-permute-start(bf16[512,128]{1,0:T(8,128)(2,1)S(1)} %copy-done.2), channel_id=1, source_target_pairs={{0,192},{64,0},{128,64},{192,128},{1,193},{65,1},{129,65},{193,129... | collective-permute-start | bytes 393224 | tf_op jit(solution)/shard_map/ppermute | solution.py:55
  63.8 25.1 %collective-permute-start.9 = (bf16[512,128]{1,0:T(8,128)(2,1)S(1)}, bf16[512,128]{1,0:T(8,128)(2,1)S(1)}, u32[]{:S(2)}, u32[]{:S(2)}) collective-permute-start(bf16[512,128]{1,0:T(8,128)(2,1)S(1)} %copy-done.2), channel_id=1, source_target_pairs={{0,64},{64,128},{128,192},{192,0},{1,65},{65,129},{129,193},{193,1... | collective-permute-start | bytes 393224 | tf_op jit(solution)/shard_map/ppermute | solution.py:55
  64.1 7.2 %collective-permute-start.5 = (bf16[8,16,512]{2,1,0:T(8,128)(2,1)S(1)}, bf16[8,16,512]{2,1,0:T(8,128)(2,1)S(1)}, u32[]{:S(2)}, u32[]{:S(2)}) collective-permute-start(bf16[8,16,512]{2,1,0:T(8,128)(2,1)S(1)} %all_to_all.31.q_ref), channel_id=1, source_target_pairs={{0,128},{64,192},{128,0},{192,64},{1,129},{65,193},{129,1},{193,65... | collective-permute-start | bytes 393224 | tf_op jit(solution)/shard_map/ppermute | solution.py:55
  65.8 11.9 %collective-permute-start.3 = (bf16[8,16,512]{2,1,0:T(8,128)(2,1)S(1)}, bf16[8,16,512]{2,1,0:T(8,128)(2,1)S(1)}, u32[]{:S(2)}, u32[]{:S(2)}) collective-permute-start(bf16[8,16,512]{2,1,0:T(8,128)(2,1)S(1)} %all_to_all.31.q_ref), channel_id=1, source_target_pairs={{0,64},{64,128},{128,192},{192,0},{1,65},{65,129},{129,193},{193,1... | collective-permute-start | bytes 393224 | tf_op jit(solution)/shard_map/ppermute | solution.py:55
  71.3 17.6 %collective-permute-start.8 = (bf16[8,16,640]{2,1,0:T(8,128)(2,1)S(1)}, bf16[8,16,640]{2,1,0:T(8,128)(2,1)S(1)}, u32[]{:S(2)}, u32[]{:S(2)}) collective-permute-start(bf16[8,16,640]{2,1,0:T(8,128)(2,1)S(1)} %attend.7), channel_id=1, source_target_pairs={{0,64},{64,128},{128,192},{192,0},{1,65},{65,129},{129,193},{193,1... | collective-permute-start | bytes 491528 | tf_op jit(solution)/shard_map/ppermute | solution.py:55
  77.7 11.2 %collective-permute-start.6 = (bf16[8,16,640]{2,1,0:T(8,128)(2,1)S(1)}, bf16[8,16,640]{2,1,0:T(8,128)(2,1)S(1)}, u32[]{:S(2)}, u32[]{:S(2)}) collective-permute-start(bf16[8,16,640]{2,1,0:T(8,128)(2,1)S(1)} %attend.6), channel_id=1, source_target_pairs={{0,128},{64,192},{128,0},{192,64},{1,129},{65,193},{129,1},{193,65... | collective-permute-start | bytes 491528 | tf_op jit(solution)/shard_map/ppermute | solution.py:55
  83.2 5.7 %collective-permute-start.4 = (bf16[8,16,640]{2,1,0:T(8,128)(2,1)S(1)}, bf16[8,16,640]{2,1,0:T(8,128)(2,1)S(1)}, u32[]{:S(2)}, u32[]{:S(2)}) collective-permute-start(bf16[8,16,640]{2,1,0:T(8,128)(2,1)S(1)} %attend.5), channel_id=1, source_target_pairs={{0,192},{64,0},{128,64},{192,128},{1,193},{65,1},{129,65},{193,129... | collective-permute-start | bytes 491528 | tf_op jit(solution)/shard_map/ppermute | solution.py:55

commit v5 on v4

--- a/solution.py
+++ b/solution.py
@@ -64,7 +64,7 @@
             sent_ref[y * HN + h] = both[y * OWN : (y + 1) * OWN]
 
 
-def project_kernel(info_ref, got_ref, w0, w1, w2, w3, table_ref, k_ref, mix_ref):
+def project_kernel(info_ref, got_ref, w0, w1, w2, w3, table_ref, k_ref, o1, o2, o3, mix_ref):
     y = info_ref[2]
     total = None
     square = None
@@ -151,7 +151,7 @@
             values = jnp.concatenate([tail_values, first_lane(TAIL)], axis=1)
             scores = jnp.where(seen, product(queries, tail_keys), NEG_FILL)
         higher = jnp.maximum(best, jnp.max(scores, axis=1, keepdims=True))
-        weights = jnp.exp2(scores * SCALE2 - higher * SCALE2).astype(jnp.bfloat16)
+        weights = jnp.exp2((scores - higher) * SCALE2).astype(jnp.bfloat16)
         sums = sums * jnp.exp2((best - higher) * SCALE2) + jnp.dot(
             weights, values, preferred_element_type=jnp.float32
         )
@@ -168,7 +168,7 @@
     o_ref[:, :, FLAT:] = packed_levels(levels).reshape(ZN, OWN, HEAD_DIM)
 
 
-def merge_kernel(own_ref, one_ref, two_ref, three_ref, w1, w2, w3, o_ref):
+def merge_kernel(own_ref, one_ref, two_ref, three_ref, o_ref):
     refs = (own_ref, one_ref, two_ref, three_ref)
     levels = [levels_of(ref[:, :, FLAT:].reshape(SHARE, HEAD_DIM)) for ref in refs]
     most = levels[0]
@@ -233,6 +233,7 @@
         compiler_params=params(56),
         name="split",
     )(hidden, norm_gain[None, :])
+    w_outs = [along_y(w_out, shift) for shift in range(YN)]
     columns = [along_y(own_columns, shift) for shift in range(YN)]
     got = exchange(sent, ("y", "x", "core"))
     first_own = z * (OWN * YN) + y * OWN
@@ -240,12 +241,12 @@
     table = rotary_table(lax.dynamic_slice_in_dim(positions, first_own, OWN))
     mix = pl.pallas_call(
         project_kernel,
-        in_specs=[SMEM] + [VMEM] * 7,
+        in_specs=[SMEM] + [VMEM] * 10,
         out_specs=VMEM,
         out_shape=shape((ZN, OWN, WIDTH + HEAD_DIM), f32),
         compiler_params=params(16),
         name="project",
-    )(info, got, *columns, table, cache_keys)
+    )(info, got, *columns, table, cache_keys, *w_outs[1:])
     mix = exchange(mix, "z")
     queries, new_rows = pl.pallas_call(
         turn_kernel,
@@ -268,15 +269,14 @@
             name="attend",
         )(info, along_y(queries, shift), cache_keys, cache_values, new_rows)
         parts.append(along_y(part, -shift))
-    w_outs = [along_y(w_out, shift) for shift in range(YN)]
     part = pl.pallas_call(
         merge_kernel,
-        in_specs=[VMEM] * 7,
+        in_specs=[VMEM] * 4,
         out_specs=VMEM,
         out_shape=shape((ZN, OWN, FLAT + HEAD_DIM), bf16),
         compiler_params=params(),
         name="merge",
-    )(*parts, *w_outs[1:])
+    )(*parts)
     part = exchange(part, "z")
     rows = pl.pallas_call(
         join_kernel,

time: 134 us -> 137 us (1.022)
  waiting for transfers between devices: 7.2 us -> 12.2 us
    ppermute x12, waiting for transfers between devices: 0.03 us -> 12.2 us  [along_y(): return lax.ppermute(array, 'y', [(i, (i + shift) % YN) for i in range(YN)])]
    all_to_all x1, waiting for transfers between devices: 7.17 us -> 0.01 us  [exchange(): return lax.all_to_all(array, axes, 0, 0, tiled=True)]
    ppermute x12, starting transfers between devices: 17.9 us -> 13.8 us  [along_y(): return lax.ppermute(array, 'y', [(i, (i + shift) % YN) for i in range(YN)])]
    all_to_all x1, starting transfers between devices: 6.08 us -> 9.13 us  [exchange(): return lax.all_to_all(array, axes, 0, 0, tiled=True)]
  transfers between devices with their start and end apart: 13 -> 13, of which waited for: 1 -> 3; matrix products, arithmetic and copies ran while one was open for 1% -> 1% of each run, Pallas kernels for 14% -> 12%
where the time goes in v5:
time: 137 us; the launch traced here: 136 us
  blocking collectives  77 us (56%)
  starting transfers between devices  22.9 us (17%)
  Pallas kernels  20.1 us (15%)
  waiting for transfers between devices  12.2 us (9%)
  other arithmetic  1.66 us (1%)
  local copies, waits for them, and re-layouts  1.63 us (1%)
    all_to_all x5, blocking collectives, exchange(): return lax.all_to_all(array, axes, 0, 0, tiled=True)  77 us
    pallas_call x4, Pallas kernels, per_device(): pl.pallas_call(functools.partial(attend_kernel, shift), in_specs=[SMEM, V...  15.4 us
    ppermute x12, starting transfers between devices, along_y(): return lax.ppermute(array, 'y', [(i, (i + shift) % YN) for i in range(YN)])  13.8 us
    ppermute x12, waiting for transfers between devices, along_y(): return lax.ppermute(array, 'y', [(i, (i + shift) % YN) for i in range(YN)])  12.2 us
    all_to_all x1, starting transfers between devices, exchange(): return lax.all_to_all(array, axes, 0, 0, tiled=True)  9.13 us
  transfers between devices with their start and end apart: 13, of which 3 were waited for; matrix products, arithmetic and copies ran while one was open for 1% of the time, Pallas kernels for 12%

profile of v5, /device:TPU:1, one launch (start us, length us, event | category | flops | bytes accessed | tf_op | source)
XLA Modules:
  0.0 136.3 jit_solution(4610214129263306148)
XLA Ops:
  0.0 3.7 %collective-permute-start.4 = (bf16[512,128]{1,0:T(8,128)(2,1)}, bf16[512,128]{1,0:T(8,128)(2,1)S(1)}, u32[]{:S(2)}, u32[]{:S(2)}) collective-permute-start(bf16[512,128]{1,0:T(8,128)(2,1)} %w0.1), channel_id=1, source_target_pairs={{0,128},{64,192},{128,0},{192,64},{1,129},{65,193},{129,1},{193,65... | collective-permute-start | bytes 393224 | tf_op jit(solution)/shard_map/ppermute | solution.py:55
  3.7 0.4 collective-permute-start.3
  4.1 2.3 %collective-permute-start.5 = (bf16[512,128]{1,0:T(8,128)(2,1)}, bf16[512,128]{1,0:T(8,128)(2,1)S(1)}, u32[]{:S(2)}, u32[]{:S(2)}) collective-permute-start(bf16[512,128]{1,0:T(8,128)(2,1)} %w0.1), channel_id=1, source_target_pairs={{0,192},{64,0},{128,64},{192,128},{1,193},{65,1},{129,65},{193,129... | collective-permute-start | bytes 393224 | tf_op jit(solution)/shard_map/ppermute | solution.py:55
  6.5 0.1 collective-permute-start.2
  6.5 1.0 collective-permute-start.1
  7.5 1.4 %split.1 = bf16[32,16,256]{2,1,0:T(8,128)(2,1)} custom-call(bf16[64,128]{1,0:T(8,128)(2,1)} %hidden_ref.1, f32[1,128]{1,0:T(1,128)} %bitcast.6), custom_call_target="tpu_custom_call" | custom-call | tf_op jit(solution)/shard_map/split/pallas_call | solution.py:228
  8.9 9.1 %all-to-all-start = ((bf16[32,16,256]{2,1,0:T(8,128)(2,1)}), bf16[32,16,256]{2,1,0:T(8,128)(2,1)S(1)}, u32[]{:S(2)}, u32[]{:S(2)}) async-start(bf16[32,16,256]{2,1,0:T(8,128)(2,1)} %split.1), calls=%async_computation | async-start | bytes 524288 | tf_op jit(solution)/shard_map/all_to_all | solution.py:49
  18.1 0.8 dynamic-slice_convert_fusion
  18.9 0.1 multiply_cosine_fusion
  19.6 0.0 collective-permute-done.4.o2.w2
  19.6 1.5 %collective-permute-start = (bf16[128,768]{1,0:T(8,128)(2,1)S(1)}, bf16[128,768]{1,0:T(8,128)(2,1)S(1)}, u32[]{:S(2)}, u32[]{:S(2)}) collective-permute-start(bf16[128,768]{1,0:T(8,128)(2,1)S(1)} %constant_dynamic-slice_fusion.w0), channel_id=1, source_target_pairs={{0,64},{64,128},{128,192},{192,0},{1,65},{65,129},{129,193},{193,1... | collective-permute-start | bytes 589832 | tf_op jit(solution)/shard_map/ppermute | solution.py:55
  21.1 0.1 pad_add_fusion.info_ref
  21.2 0.1 pad_maximum_fusion.table_ref
  21.3 0.0 collective-permute-done.3.o1.w1
  21.3 0.0 collective-permute-done.5.o3.w3
  21.3 0.0 collective-permute-done.2.w3
  21.3 0.0 collective-permute-done.1.w2
  21.3 8.1 %collective-permute-done.w1 = bf16[128,768]{1,0:T(8,128)(2,1)S(1)} collective-permute-done((bf16[128,768]{1,0:T(8,128)(2,1)S(1)}, bf16[128,768]{1,0:T(8,128)(2,1)S(1)}, u32[]{:S(2)}, u32[]{:S(2)}) %collective-permute-start) | collective-permute-done | bytes 196640 | tf_op jit(solution)/shard_map/ppermute | solution.py:55
  29.4 0.7 copy-done.2
  30.1 0.9 copy-done.3
  31.0 1.5 %project.1 = f32[8,16,896]{2,1,0:T(8,128)S(1)} custom-call(s32[3]{0:T(128)S(1)} %pad_add_fusion.info_ref, bf16[32,16,256]{2,1,0:T(8,128)(2,1)S(1)} %all-to-all-done.got_ref, bf16[128,768]{1,0:T(8,128)(2,1)S(1)} %constant_dynamic-slice_fusion.w0, bf16[128,768]{1,0:T(8,128)(2,1)S(1)} %copy-done.3, bf16[128,768]{1,0:T(8,128)(2,1)} %collective-permute-done.1.w2, ...), custom_call_target="tpu_custom_call" | custom-call | tf_op jit(solution)/shard_map/project/pallas_call | solution.py:242
  32.5 22.3 %all_to_all.30.mix_ref = f32[8,16,896]{2,1,0:T(8,128)S(1)} all-to-all(f32[8,16,896]{2,1,0:T(8,128)S(1)} %project.1), channel_id=1, replica_groups=mesh['y'=4,'z'=8,'x'=4,'core'=2] {'z'}, dimensions={0} | all-to-all | bytes 917504 | tf_op jit(solution)/shard_map/all_to_all | solution.py:49
  54.8 0.2 turn.1
  55.0 10.7 %all_to_all.31.q_ref = bf16[8,16,512]{2,1,0:T(8,128)(2,1)S(1)} all-to-all(bf16[8,16,512]{2,1,0:T(8,128)(2,1)S(1)} %get-tuple-element.7), channel_id=1, replica_groups=mesh['y'=4,'z'=8,'x'=4,'core'=2] {'z'}, dimensions={0} | all-to-all | bytes 262144 | tf_op jit(solution)/shard_map/all_to_all | solution.py:49
  65.7 0.0 collective-permute-start.6
  65.7 2.7 %collective-permute-start.10 = (bf16[8,16,512]{2,1,0:T(8,128)(2,1)S(1)}, bf16[8,16,512]{2,1,0:T(8,128)(2,1)S(1)}, u32[]{:S(2)}, u32[]{:S(2)}) collective-permute-start(bf16[8,16,512]{2,1,0:T(8,128)(2,1)S(1)} %all_to_all.31.q_ref), channel_id=1, source_target_pairs={{0,192},{64,0},{128,64},{192,128},{1,193},{65,1},{129,65},{193,129... | collective-permute-start | bytes 393224 | tf_op jit(solution)/shard_map/ppermute | solution.py:55
  68.4 0.2 collective-permute-start.8
  68.6 2.1 %collective-permute-done.6.q_ref = bf16[8,16,512]{2,1,0:T(8,128)(2,1)S(1)} collective-permute-done((bf16[8,16,512]{2,1,0:T(8,128)(2,1)S(1)}, bf16[8,16,512]{2,1,0:T(8,128)(2,1)S(1)}, u32[]{:S(2)}, u32[]{:S(2)}) %collective-permute-start.6) | collective-permute-done | bytes 131104 | tf_op jit(solution)/shard_map/ppermute | solution.py:55
  70.7 3.9 %attend.5 = bf16[8,16,640]{2,1,0:T(8,128)(2,1)S(1)} custom-call(s32[3]{0:T(128)S(1)} %pad_add_fusion.info_ref, bf16[8,16,512]{2,1,0:T(8,128)(2,1)S(1)} %collective-permute-done.6.q_ref, bf16[4096,128]{1,0:T(8,128)(2,1)S(1)} %copy-done.1, bf16[4096,128]{1,0:T(8,128)(2,1)S(1)} %copy-done.5, bf16[16,256]{1,0:T(8,128)(2,1)S(1)} %get-tuple-element.8.new_ref), custom_call_target="tpu_custom_call" | custom-call | flops 4000000000 | tf_op jit(solution)/shard_map/attend/pallas_call | solution.py:262
  74.6 0.7 collective-permute-start.7
  75.3 0.0 collective-permute-done.8.q_ref
  75.3 3.9 %attend.6 = bf16[8,16,640]{2,1,0:T(8,128)(2,1)S(1)} custom-call(s32[3]{0:T(128)S(1)} %pad_add_fusion.info_ref, bf16[8,16,512]{2,1,0:T(8,128)(2,1)S(1)} %collective-permute-done.8.q_ref, bf16[4096,128]{1,0:T(8,128)(2,1)S(1)} %copy-done.1, bf16[4096,128]{1,0:T(8,128)(2,1)S(1)} %copy-done.5, bf16[16,256]{1,0:T(8,128)(2,1)S(1)} %get-tuple-element.8.new_ref), custom_call_target="tpu_custom_call" | custom-call | flops 4000000000 | tf_op jit(solution)/shard_map/attend/pallas_call | solution.py:262
  79.2 0.3 collective-permute-start.9
  79.4 0.0 collective-permute-done.10.q_ref
  79.5 3.9 %attend.7 = bf16[8,16,640]{2,1,0:T(8,128)(2,1)S(1)} custom-call(s32[3]{0:T(128)S(1)} %pad_add_fusion.info_ref, bf16[8,16,512]{2,1,0:T(8,128)(2,1)S(1)} %collective-permute-done.10.q_ref, bf16[4096,128]{1,0:T(8,128)(2,1)S(1)} %copy-done.1, bf16[4096,128]{1,0:T(8,128)(2,1)S(1)} %copy-done.5, bf16[16,256]{1,0:T(8,128)(2,1)S(1)} %get-tuple-element.8.new_ref), custom_call_target="tpu_custom_call" | custom-call | flops 4000000000 | tf_op jit(solution)/shard_map/attend/pallas_call | solution.py:262
  83.3 0.9 collective-permute-start.11
  84.2 3.9 %attend.4.own_ref = bf16[8,16,640]{2,1,0:T(8,128)(2,1)S(1)} custom-call(s32[3]{0:T(128)S(1)} %pad_add_fusion.info_ref, bf16[8,16,512]{2,1,0:T(8,128)(2,1)S(1)} %all_to_all.31.q_ref, bf16[4096,128]{1,0:T(8,128)(2,1)S(1)} %copy-done.1, bf16[4096,128]{1,0:T(8,128)(2,1)S(1)} %copy-done.5, bf16[16,256]{1,0:T(8,128)(2,1)S(1)} %get-tuple-element.8.new_ref), custom_call_target="tpu_custom_call" | custom-call | flops 4000000000 | tf_op jit(solution)/shard_map/attend/pallas_call | solution.py:262
  88.1 0.0 copy-start.4
  88.1 0.0 collective-permute-done.7.one_ref
  88.1 0.0 collective-permute-done.9.two_ref
  88.1 2.0 %collective-permute-done.11.three_ref = bf16[8,16,640]{2,1,0:T(8,128)(2,1)S(1)} collective-permute-done((bf16[8,16,640]{2,1,0:T(8,128)(2,1)S(1)}, bf16[8,16,640]{2,1,0:T(8,128)(2,1)S(1)}, u32[]{:S(2)}, u32[]{:S(2)}) %collective-permute-start.11) | collective-permute-done | bytes 163872 | tf_op jit(solution)/shard_map/ppermute | solution.py:55
  90.1 0.5 merge.1
  90.7 10.7 %all_to_all.32.back_ref = bf16[8,16,640]{2,1,0:T(8,128)(2,1)S(1)} all-to-all(bf16[8,16,640]{2,1,0:T(8,128)(2,1)S(1)} %merge.1), channel_id=1, replica_groups=mesh['y'=4,'z'=8,'x'=4,'core'=2] {'z'}, dimensions={0} | all-to-all | bytes 327680 | tf_op jit(solution)/shard_map/all_to_all | solution.py:49
  101.3 0.3 join.1
  101.6 10.3 %all_to_all.33.rows_ref = bf16[8,16,512]{2,1,0:T(8,128)(2,1)S(1)} all-to-all(bf16[8,16,512]{2,1,0:T(8,128)(2,1)S(1)} %join.1), channel_id=1, replica_groups=mesh['y'=4,'z'=8,'x'=4,'core'=2] {'z'}, dimensions={0} | all-to-all | bytes 262144 | tf_op jit(solution)/shard_map/all_to_all | solution.py:49
  111.9 0.8 finish.1
  112.7 23.0 %all_to_all.34 = f32[32,16,128]{2,1,0:T(8,128)S(1)} all-to-all(f32[32,16,128]{2,1,0:T(8,128)S(1)} %finish.1), channel_id=1, replica_groups=mesh['y'=4,'z'=8,'x'=4,'core'=2] {'y','x','core'}, dimensions={0} | all-to-all | bytes 524288 | tf_op jit(solution)/shard_map/all_to_all | solution.py:49
  135.7 0.6 bitcast_reduce_fusion
  (12 shorter events, 0.0 us)
Async XLA Ops:
  0.0 6.4 %copy-start = (bf16[128,6144]{1,0:T(8,128)(2,1)S(1)}, bf16[128,6144]{1,0:T(8,128)(2,1)}, u32[]{:S(2)}) copy-start(bf16[128,6144]{1,0:T(8,128)(2,1)} %param.10) | copy-start | bytes 4718596
  0.0 30.1 %copy-start.1 = (bf16[4096,128]{1,0:T(8,128)(2,1)S(1)}, bf16[4096,128]{1,0:T(8,128)(2,1)}, u32[]{:S(2)}) copy-start(bf16[4096,128]{1,0:T(8,128)(2,1)} %k_ref.9) | copy-start | bytes 3145732
  0.0 19.6 %collective-permute-start.4 = (bf16[512,128]{1,0:T(8,128)(2,1)}, bf16[512,128]{1,0:T(8,128)(2,1)S(1)}, u32[]{:S(2)}, u32[]{:S(2)}) collective-permute-start(bf16[512,128]{1,0:T(8,128)(2,1)} %w0.1), channel_id=1, source_target_pairs={{0,128},{64,192},{128,0},{192,64},{1,129},{65,193},{129,1},{193,65... | collective-permute-start | bytes 393224 | tf_op jit(solution)/shard_map/ppermute | solution.py:55
  3.7 17.5 %collective-permute-start.3 = (bf16[512,128]{1,0:T(8,128)(2,1)}, bf16[512,128]{1,0:T(8,128)(2,1)S(1)}, u32[]{:S(2)}, u32[]{:S(2)}) collective-permute-start(bf16[512,128]{1,0:T(8,128)(2,1)} %w0.1), channel_id=1, source_target_pairs={{0,64},{64,128},{128,192},{192,0},{1,65},{65,129},{129,193},{193,1... | collective-permute-start | bytes 393224 | tf_op jit(solution)/shard_map/ppermute | solution.py:55
  4.1 17.1 %collective-permute-start.5 = (bf16[512,128]{1,0:T(8,128)(2,1)}, bf16[512,128]{1,0:T(8,128)(2,1)S(1)}, u32[]{:S(2)}, u32[]{:S(2)}) collective-permute-start(bf16[512,128]{1,0:T(8,128)(2,1)} %w0.1), channel_id=1, source_target_pairs={{0,192},{64,0},{128,64},{192,128},{1,193},{65,1},{129,65},{193,129... | collective-permute-start | bytes 393224 | tf_op jit(solution)/shard_map/ppermute | solution.py:55
  6.5 14.8 %collective-permute-start.2 = (bf16[128,768]{1,0:T(8,128)(2,1)S(1)}, bf16[128,768]{1,0:T(8,128)(2,1)}, u32[]{:S(2)}, u32[]{:S(2)}) collective-permute-start(bf16[128,768]{1,0:T(8,128)(2,1)S(1)} %constant_dynamic-slice_fusion.w0), channel_id=1, source_target_pairs={{0,192},{64,0},{128,64},{192,128},{1,193},{65,1},{129,65},{193,129... | collective-permute-start | bytes 589832 | tf_op jit(solution)/shard_map/ppermute | solution.py:55
  6.5 14.7 %collective-permute-start.1 = (bf16[128,768]{1,0:T(8,128)(2,1)S(1)}, bf16[128,768]{1,0:T(8,128)(2,1)}, u32[]{:S(2)}, u32[]{:S(2)}) collective-permute-start(bf16[128,768]{1,0:T(8,128)(2,1)S(1)} %constant_dynamic-slice_fusion.w0), channel_id=1, source_target_pairs={{0,128},{64,192},{128,0},{192,64},{1,129},{65,193},{129,1},{193,65... | collective-permute-start | bytes 589832 | tf_op jit(solution)/shard_map/ppermute | solution.py:55
  8.9 21.2 %all-to-all-start = ((bf16[32,16,256]{2,1,0:T(8,128)(2,1)}), bf16[32,16,256]{2,1,0:T(8,128)(2,1)S(1)}, u32[]{:S(2)}, u32[]{:S(2)}) async-start(bf16[32,16,256]{2,1,0:T(8,128)(2,1)} %split.1), calls=%async_computation | async-start | bytes 524288 | tf_op jit(solution)/shard_map/all_to_all | solution.py:49
  19.6 9.8 %collective-permute-start = (bf16[128,768]{1,0:T(8,128)(2,1)S(1)}, bf16[128,768]{1,0:T(8,128)(2,1)S(1)}, u32[]{:S(2)}, u32[]{:S(2)}) collective-permute-start(bf16[128,768]{1,0:T(8,128)(2,1)S(1)} %constant_dynamic-slice_fusion.w0), channel_id=1, source_target_pairs={{0,64},{64,128},{128,192},{192,0},{1,65},{65,129},{129,193},{193,1... | collective-permute-start | bytes 589832 | tf_op jit(solution)/shard_map/ppermute | solution.py:55
  29.4 0.7 copy-start.2
  30.1 0.9 copy-start.3
  31.0 39.7 %copy-start.5 = (bf16[4096,128]{1,0:T(8,128)(2,1)S(1)}, bf16[4096,128]{1,0:T(8,128)(2,1)}, u32[]{:S(2)}) copy-start(bf16[4096,128]{1,0:T(8,128)(2,1)} %v_ref.7) | copy-start | bytes 3145732
  65.7 5.0 %collective-permute-start.6 = (bf16[8,16,512]{2,1,0:T(8,128)(2,1)S(1)}, bf16[8,16,512]{2,1,0:T(8,128)(2,1)S(1)}, u32[]{:S(2)}, u32[]{:S(2)}) collective-permute-start(bf16[8,16,512]{2,1,0:T(8,128)(2,1)S(1)} %all_to_all.31.q_ref), channel_id=1, source_target_pairs={{0,64},{64,128},{128,192},{192,0},{1,65},{65,129},{129,193},{193,1... | collective-permute-start | bytes 393224 | tf_op jit(solution)/shard_map/ppermute | solution.py:55
  65.7 13.7 %collective-permute-start.10 = (bf16[8,16,512]{2,1,0:T(8,128)(2,1)S(1)}, bf16[8,16,512]{2,1,0:T(8,128)(2,1)S(1)}, u32[]{:S(2)}, u32[]{:S(2)}) collective-permute-start(bf16[8,16,512]{2,1,0:T(8,128)(2,1)S(1)} %all_to_all.31.q_ref), channel_id=1, source_target_pairs={{0,192},{64,0},{128,64},{192,128},{1,193},{65,1},{129,65},{193,129... | collective-permute-start | bytes 393224 | tf_op jit(solution)/shard_map/ppermute | solution.py:55
  68.4 6.9 %collective-permute-start.8 = (bf16[8,16,512]{2,1,0:T(8,128)(2,1)S(1)}, bf16[8,16,512]{2,1,0:T(8,128)(2,1)S(1)}, u32[]{:S(2)}, u32[]{:S(2)}) collective-permute-start(bf16[8,16,512]{2,1,0:T(8,128)(2,1)S(1)} %all_to_all.31.q_ref), channel_id=1, source_target_pairs={{0,128},{64,192},{128,0},{192,64},{1,129},{65,193},{129,1},{193,65... | collective-permute-start | bytes 393224 | tf_op jit(solution)/shard_map/ppermute | solution.py:55
  74.6 13.5 %collective-permute-start.7 = (bf16[8,16,640]{2,1,0:T(8,128)(2,1)S(1)}, bf16[8,16,640]{2,1,0:T(8,128)(2,1)S(1)}, u32[]{:S(2)}, u32[]{:S(2)}) collective-permute-start(bf16[8,16,640]{2,1,0:T(8,128)(2,1)S(1)} %attend.5), channel_id=1, source_target_pairs={{0,192},{64,0},{128,64},{192,128},{1,193},{65,1},{129,65},{193,129... | collective-permute-start | bytes 491528 | tf_op jit(solution)/shard_map/ppermute | solution.py:55
  79.2 8.9 %collective-permute-start.9 = (bf16[8,16,640]{2,1,0:T(8,128)(2,1)S(1)}, bf16[8,16,640]{2,1,0:T(8,128)(2,1)S(1)}, u32[]{:S(2)}, u32[]{:S(2)}) collective-permute-start(bf16[8,16,640]{2,1,0:T(8,128)(2,1)S(1)} %attend.6), channel_id=1, source_target_pairs={{0,128},{64,192},{128,0},{192,64},{1,129},{65,193},{129,1},{193,65... | collective-permute-start | bytes 491528 | tf_op jit(solution)/shard_map/ppermute | solution.py:55
  83.3 6.8 %collective-permute-start.11 = (bf16[8,16,640]{2,1,0:T(8,128)(2,1)S(1)}, bf16[8,16,640]{2,1,0:T(8,128)(2,1)S(1)}, u32[]{:S(2)}, u32[]{:S(2)}) collective-permute-start(bf16[8,16,640]{2,1,0:T(8,128)(2,1)S(1)} %attend.7), channel_id=1, source_target_pairs={{0,64},{64,128},{128,192},{192,0},{1,65},{65,129},{129,193},{193,1... | collective-permute-start | bytes 491528 | tf_op jit(solution)/shard_map/ppermute | solution.py:55
  88.1 23.8 %copy-start.4 = (bf16[512,128]{1,0:T(8,128)(2,1)S(1)}, bf16[512,128]{1,0:T(8,128)(2,1)}, u32[]{:S(2)}) copy-start(bf16[512,128]{1,0:T(8,128)(2,1)} %w0.1) | copy-start | bytes 393220

commit v6 on v5

--- a/solution.py
+++ b/solution.py
@@ -64,7 +64,7 @@
             sent_ref[y * HN + h] = both[y * OWN : (y + 1) * OWN]
 
 
-def project_kernel(info_ref, got_ref, w0, w1, w2, w3, table_ref, k_ref, o1, o2, o3, mix_ref):
+def project_kernel(info_ref, got_ref, w0, w1, w2, w3, table_ref, k_ref, o1, o2, mix_ref):
     y = info_ref[2]
     total = None
     square = None
@@ -76,19 +76,25 @@
         own = jnp.sum(plain * plain, axis=1, keepdims=True)
         total = term if total is None else total + term
         square = own if square is None else square + own
-    mix_ref[:, :, :WIDTH] = total.reshape(ZN, OWN, WIDTH)
-    mix_ref[:, :, WIDTH:] = jnp.broadcast_to(square, (HN * OWN, HEAD_DIM)).reshape(ZN, OWN, HEAD_DIM)
+    for s in range(SLOTS):
+        part = total[:, s * HEAD_DIM : (s + 1) * HEAD_DIM]
+        mix_ref[:, s * OWN : (s + 1) * OWN] = part.reshape(ZN, OWN, HEAD_DIM)
+    wide = jnp.broadcast_to(square, (HN * OWN, HEAD_DIM)).reshape(ZN, OWN, HEAD_DIM)
+    lane = lax.broadcasted_iota(jnp.int32, (ZN, OWN // 2, HEAD_DIM), 2)
+    mix_ref[:, SLOTS * OWN :] = jnp.where(lane < HEAD_DIM // 2, wide[:, : OWN // 2], wide[:, OWN // 2 :])
 
 
 def turn_kernel(mix_ref, table_ref, queries_ref, new_ref):
     share = mix_ref[0]
     for z in range(1, ZN):
         share = share + mix_ref[z]
-    inv_rms = lax.rsqrt(share[:, WIDTH : WIDTH + 1] / D + 1e-05)
+    square = share[SLOTS * OWN :]
+    half = HEAD_DIM // 2
+    inv_rms = lax.rsqrt(jnp.concatenate([square[:, :1], square[:, half : half + 1]], axis=0) / D + 1e-05)
     cosine, sine = table_ref[:, :HEAD_DIM], table_ref[:, HEAD_DIM:]
     slots = []
     for s in range(SLOTS):
-        value = share[:, s * HEAD_DIM : (s + 1) * HEAD_DIM] * inv_rms
+        value = share[s * OWN : (s + 1) * OWN] * inv_rms
         if s <= GROUP:
             value = value * cosine + pltpu.roll(value, HEAD_DIM // 2, 1) * sine
         slots.append(value.astype(jnp.bfloat16))
@@ -168,7 +174,7 @@
     o_ref[:, :, FLAT:] = packed_levels(levels).reshape(ZN, OWN, HEAD_DIM)
 
 
-def merge_kernel(own_ref, one_ref, two_ref, three_ref, o_ref):
+def merge_kernel(own_ref, one_ref, two_ref, three_ref, held_ref, o_ref):
     refs = (own_ref, one_ref, two_ref, three_ref)
     levels = [levels_of(ref[:, :, FLAT:].reshape(SHARE, HEAD_DIM)) for ref in refs]
     most = levels[0]
@@ -241,12 +247,12 @@
     table = rotary_table(lax.dynamic_slice_in_dim(positions, first_own, OWN))
     mix = pl.pallas_call(
         project_kernel,
-        in_specs=[SMEM] + [VMEM] * 10,
-        out_specs=VMEM,
-        out_shape=shape((ZN, OWN, WIDTH + HEAD_DIM), f32),
+        in_specs=[SMEM] + [VMEM] * 9,
+        out_specs=VMEM,
+        out_shape=shape((ZN, SLOTS * OWN + OWN // 2, HEAD_DIM), f32),
         compiler_params=params(16),
         name="project",
-    )(info, got, *columns, table, cache_keys, *w_outs[1:])
+    )(info, got, *columns, table, cache_keys, w_outs[1], w_outs[3])
     mix = exchange(mix, "z")
     queries, new_rows = pl.pallas_call(
         turn_kernel,
@@ -271,12 +277,12 @@
         parts.append(along_y(part, -shift))
     part = pl.pallas_call(
         merge_kernel,
-        in_specs=[VMEM] * 4,
+        in_specs=[VMEM] * 5,
         out_specs=VMEM,
         out_shape=shape((ZN, OWN, FLAT + HEAD_DIM), bf16),
         compiler_params=params(),
         name="merge",
-    )(*parts)
+    )(*parts, w_outs[2])
     part = exchange(part, "z")
     rows = pl.pallas_call(
         join_kernel,

time: 137 us -> 136 us (level)
  waiting for transfers between devices: 12.2 us -> 8.57 us
  starting transfers between devices: 22.9 us -> 25.6 us
  blocking collectives: 77 us -> 75 us
    ppermute x12, waiting for transfers between devices: 12.2 us -> 2 us  [along_y(): return lax.ppermute(array, 'y', [(i, (i + shift) % YN) for i in range(YN)])]
    all_to_all x1, waiting for transfers between devices: 0.01 us -> 6.57 us  [exchange(): return lax.all_to_all(array, axes, 0, 0, tiled=True)]
    ppermute x12, starting transfers between devices: 13.8 us -> 19 us  [along_y(): return lax.ppermute(array, 'y', [(i, (i + shift) % YN) for i in range(YN)])]
    all_to_all x1, starting transfers between devices: 9.13 us -> 6.53 us  [exchange(): return lax.all_to_all(array, axes, 0, 0, tiled=True)]
    all_to_all x5, blocking collectives: 77 us -> 75 us  [exchange(): return lax.all_to_all(array, axes, 0, 0, tiled=True)]
  transfers between devices with their start and end apart: 13 -> 13, of which waited for: 3 -> 3; matrix products, arithmetic and copies ran while one was open for 1% -> 1% of each run, Pallas kernels for 12% -> 13%
where the time goes in v6:
time: 136 us; the launch traced here: 135 us
  blocking collectives  75 us (55%)
  starting transfers between devices  25.6 us (19%)
  Pallas kernels  20.9 us (15%)
  waiting for transfers between devices  8.57 us (6%)
  other arithmetic  2.24 us (2%)
  local copies, waits for them, and re-layouts  2.1 us (2%)
    all_to_all x5, blocking collectives, exchange(): return lax.all_to_all(array, axes, 0, 0, tiled=True)  75 us
    ppermute x12, starting transfers between devices, along_y(): return lax.ppermute(array, 'y', [(i, (i + shift) % YN) for i in range(YN)])  19 us
    pallas_call x4, Pallas kernels, per_device(): pl.pallas_call(functools.partial(attend_kernel, shift), in_specs=[SMEM, V...  16.2 us
    all_to_all x1, waiting for transfers between devices, exchange(): return lax.all_to_all(array, axes, 0, 0, tiled=True)  6.57 us
    all_to_all x1, starting transfers between devices, exchange(): return lax.all_to_all(array, axes, 0, 0, tiled=True)  6.53 us
  transfers between devices with their start and end apart: 13, of which 3 were waited for; matrix products, arithmetic and copies ran while one was open for 1% of the time, Pallas kernels for 13%

profile of v6, /device:TPU:1, one launch (start us, length us, event | category | flops | bytes accessed | tf_op | source)
XLA Modules:
  0.0 135.2 jit_solution(4810404597950083941)
XLA Ops:
  0.0 1.4 %copy-done = bf16[128,6144]{1,0:T(8,128)(2,1)S(1)} copy-done((bf16[128,6144]{1,0:T(8,128)(2,1)S(1)}, bf16[128,6144]{1,0:T(8,128)(2,1)}, u32[]{:S(2)}) %copy-start) | copy-done | bytes 1572888
  1.4 2.2 %collective-permute-start = (bf16[128,768]{1,0:T(8,128)(2,1)S(1)}, bf16[128,768]{1,0:T(8,128)(2,1)S(1)}, u32[]{:S(2)}, u32[]{:S(2)}) collective-permute-start(bf16[128,768]{1,0:T(8,128)(2,1)S(1)} %constant_dynamic-slice_fusion.w0), channel_id=1, source_target_pairs={{0,64},{64,128},{128,192},{192,0},{1,65},{65,129},{129,193},{193,1... | collective-permute-start | bytes 589832 | tf_op jit(solution)/shard_map/ppermute | solution.py:55
  3.6 2.6 %collective-permute-start.1 = (bf16[128,768]{1,0:T(8,128)(2,1)S(1)}, bf16[128,768]{1,0:T(8,128)(2,1)}, u32[]{:S(2)}, u32[]{:S(2)}) collective-permute-start(bf16[128,768]{1,0:T(8,128)(2,1)S(1)} %constant_dynamic-slice_fusion.w0), channel_id=1, source_target_pairs={{0,128},{64,192},{128,0},{192,64},{1,129},{65,193},{129,1},{193,65... | collective-permute-start | bytes 589832 | tf_op jit(solution)/shard_map/ppermute | solution.py:55
  6.3 1.1 collective-permute-start.2
  7.3 0.4 collective-permute-start.3
  7.7 2.3 %collective-permute-start.4 = (bf16[512,128]{1,0:T(8,128)(2,1)}, bf16[512,128]{1,0:T(8,128)(2,1)S(1)}, u32[]{:S(2)}, u32[]{:S(2)}) collective-permute-start(bf16[512,128]{1,0:T(8,128)(2,1)} %w0.1), channel_id=1, source_target_pairs={{0,192},{64,0},{128,64},{192,128},{1,193},{65,1},{129,65},{193,129... | collective-permute-start | bytes 393224 | tf_op jit(solution)/shard_map/ppermute | solution.py:55
  10.0 1.4 %split.1 = bf16[32,16,256]{2,1,0:T(8,128)(2,1)} custom-call(bf16[64,128]{1,0:T(8,128)(2,1)} %hidden_ref.1, f32[1,128]{1,0:T(1,128)} %bitcast.6), custom_call_target="tpu_custom_call" | custom-call | tf_op jit(solution)/shard_map/split/pallas_call | solution.py:234
  11.4 6.5 %all-to-all-start = ((bf16[32,16,256]{2,1,0:T(8,128)(2,1)}), bf16[32,16,256]{2,1,0:T(8,128)(2,1)S(1)}, u32[]{:S(2)}, u32[]{:S(2)}) async-start(bf16[32,16,256]{2,1,0:T(8,128)(2,1)} %split.1), calls=%async_computation | async-start | bytes 524288 | tf_op jit(solution)/shard_map/all_to_all | solution.py:49
  18.0 0.8 dynamic-slice_convert_fusion
  18.7 0.1 multiply_cosine_fusion
  19.5 0.7 pad_add_fusion.info_ref
  20.2 0.1 pad_maximum_fusion.table_ref
  20.3 0.0 collective-permute-done.3.o1.w1
  20.3 0.0 collective-permute-done.4.o2.w3
  20.3 0.0 collective-permute-done.w1
  20.3 0.0 collective-permute-done.1.w2
  20.3 0.0 collective-permute-done.2.w3
  20.3 6.6 %all-to-all-done.got_ref = bf16[32,16,256]{2,1,0:T(8,128)(2,1)S(1)} async-done(((bf16[32,16,256]{2,1,0:T(8,128)(2,1)}), bf16[32,16,256]{2,1,0:T(8,128)(2,1)S(1)}, u32[]{:S(2)}, u32[]{:S(2)}) %all-to-all-start) | async-done | bytes 262176 | tf_op jit(solution)/shard_map/all_to_all | solution.py:49
  26.9 0.7 copy-done.3
  27.5 1.5 %project.1 = f32[8,104,128]{2,1,0:T(8,128)S(1)} custom-call(s32[3]{0:T(128)S(1)} %copy-done.3, bf16[32,16,256]{2,1,0:T(8,128)(2,1)S(1)} %all-to-all-done.got_ref, bf16[128,768]{1,0:T(8,128)(2,1)S(1)} %constant_dynamic-slice_fusion.w0, bf16[128,768]{1,0:T(8,128)(2,1)S(1)} %collective-permute-done.w1, bf16[128,768]{1,0:T(8,128)(2,1)} %collective-permute-done.1.w2, ...), custom_call_target="tpu_custom_call" | custom-call | tf_op jit(solution)/shard_map/project/pallas_call | solution.py:248
  29.0 22.9 %all_to_all.30.mix_ref = f32[8,104,128]{2,1,0:T(8,128)S(1)} all-to-all(f32[8,104,128]{2,1,0:T(8,128)S(1)} %project.1), channel_id=1, replica_groups=mesh['y'=4,'z'=8,'x'=4,'core'=2] {'z'}, dimensions={0} | all-to-all | bytes 851968 | tf_op jit(solution)/shard_map/all_to_all | solution.py:49
  52.0 0.2 turn.1
  52.2 10.4 %all_to_all.31.q_ref = bf16[8,16,512]{2,1,0:T(8,128)(2,1)S(1)} all-to-all(bf16[8,16,512]{2,1,0:T(8,128)(2,1)S(1)} %get-tuple-element.7), channel_id=1, replica_groups=mesh['y'=4,'z'=8,'x'=4,'core'=2] {'z'}, dimensions={0} | all-to-all | bytes 262144 | tf_op jit(solution)/shard_map/all_to_all | solution.py:49
  62.6 2.0 %collective-permute-start.9 = (bf16[8,16,512]{2,1,0:T(8,128)(2,1)S(1)}, bf16[8,16,512]{2,1,0:T(8,128)(2,1)S(1)}, u32[]{:S(2)}, u32[]{:S(2)}) collective-permute-start(bf16[8,16,512]{2,1,0:T(8,128)(2,1)S(1)} %all_to_all.31.q_ref), channel_id=1, source_target_pairs={{0,192},{64,0},{128,64},{192,128},{1,193},{65,1},{129,65},{193,129... | collective-permute-start | bytes 393224 | tf_op jit(solution)/shard_map/ppermute | solution.py:55
  64.6 1.3 collective-permute-start.11
  65.8 1.7 %collective-permute-start.7 = (bf16[8,16,512]{2,1,0:T(8,128)(2,1)S(1)}, bf16[8,16,512]{2,1,0:T(8,128)(2,1)S(1)}, u32[]{:S(2)}, u32[]{:S(2)}) collective-permute-start(bf16[8,16,512]{2,1,0:T(8,128)(2,1)S(1)} %all_to_all.31.q_ref), channel_id=1, source_target_pairs={{0,128},{64,192},{128,0},{192,64},{1,129},{65,193},{129,1},{193,65... | collective-permute-start | bytes 393224 | tf_op jit(solution)/shard_map/ppermute | solution.py:55
  67.6 0.0 collective-permute-start.5
  67.6 0.8 collective-permute-done.9.q_ref
  68.4 4.0 %attend.7 = bf16[8,16,640]{2,1,0:T(8,128)(2,1)S(1)} custom-call(s32[3]{0:T(128)S(1)} %copy-done.4, bf16[8,16,512]{2,1,0:T(8,128)(2,1)S(1)} %collective-permute-done.9.q_ref, bf16[4096,128]{1,0:T(8,128)(2,1)S(1)} %copy-done.1, bf16[4096,128]{1,0:T(8,128)(2,1)S(1)} %copy-done.5, bf16[16,256]{1,0:T(8,128)(2,1)S(1)} %get-tuple-element.8.new_ref), custom_call_target="tpu_custom_call" | custom-call | flops 4000000000 | tf_op jit(solution)/shard_map/attend/pallas_call | solution.py:268
  72.4 0.4 collective-permute-start.10
  72.8 0.0 collective-permute-done.7.q_ref
  72.8 4.0 %attend.6 = bf16[8,16,640]{2,1,0:T(8,128)(2,1)S(1)} custom-call(s32[3]{0:T(128)S(1)} %copy-done.4, bf16[8,16,512]{2,1,0:T(8,128)(2,1)S(1)} %collective-permute-done.7.q_ref, bf16[4096,128]{1,0:T(8,128)(2,1)S(1)} %copy-done.1, bf16[4096,128]{1,0:T(8,128)(2,1)S(1)} %copy-done.5, bf16[16,256]{1,0:T(8,128)(2,1)S(1)} %get-tuple-element.8.new_ref), custom_call_target="tpu_custom_call" | custom-call | flops 4000000000 | tf_op jit(solution)/shard_map/attend/pallas_call | solution.py:268
  76.9 5.0 %collective-permute-start.8 = (bf16[8,16,640]{2,1,0:T(8,128)(2,1)S(1)}, bf16[8,16,640]{2,1,0:T(8,128)(2,1)S(1)}, u32[]{:S(2)}, u32[]{:S(2)}) collective-permute-start(bf16[8,16,640]{2,1,0:T(8,128)(2,1)S(1)} %attend.6), channel_id=1, source_target_pairs={{0,128},{64,192},{128,0},{192,64},{1,129},{65,193},{129,1},{193,65... | collective-permute-start | bytes 491528 | tf_op jit(solution)/shard_map/ppermute | solution.py:55
  81.9 0.0 collective-permute-done.5.q_ref
  81.9 4.0 %attend.5 = bf16[8,16,640]{2,1,0:T(8,128)(2,1)S(1)} custom-call(s32[3]{0:T(128)S(1)} %copy-done.4, bf16[8,16,512]{2,1,0:T(8,128)(2,1)S(1)} %collective-permute-done.5.q_ref, bf16[4096,128]{1,0:T(8,128)(2,1)S(1)} %copy-done.1, bf16[4096,128]{1,0:T(8,128)(2,1)S(1)} %copy-done.5, bf16[16,256]{1,0:T(8,128)(2,1)S(1)} %get-tuple-element.8.new_ref), custom_call_target="tpu_custom_call" | custom-call | flops 4000000000 | tf_op jit(solution)/shard_map/attend/pallas_call | solution.py:268
  86.0 0.1 collective-permute-start.6
  86.1 4.0 %attend.4.own_ref = bf16[8,16,640]{2,1,0:T(8,128)(2,1)S(1)} custom-call(s32[3]{0:T(128)S(1)} %copy-done.4, bf16[8,16,512]{2,1,0:T(8,128)(2,1)S(1)} %all_to_all.31.q_ref, bf16[4096,128]{1,0:T(8,128)(2,1)S(1)} %copy-done.1, bf16[4096,128]{1,0:T(8,128)(2,1)S(1)} %copy-done.5, bf16[16,256]{1,0:T(8,128)(2,1)S(1)} %get-tuple-element.8.new_ref), custom_call_target="tpu_custom_call" | custom-call | flops 4000000000 | tf_op jit(solution)/shard_map/attend/pallas_call | solution.py:268
  90.1 0.0 collective-permute-done.11.held_ref.w2
  90.1 0.0 collective-permute-done.10.three_ref
  90.1 0.0 collective-permute-done.8.two_ref
  90.1 1.2 collective-permute-done.6.one_ref
  91.3 0.5 merge.1
  91.8 10.7 %all_to_all.32.back_ref = bf16[8,16,640]{2,1,0:T(8,128)(2,1)S(1)} all-to-all(bf16[8,16,640]{2,1,0:T(8,128)(2,1)S(1)} %merge.1), channel_id=1, replica_groups=mesh['y'=4,'z'=8,'x'=4,'core'=2] {'z'}, dimensions={0} | all-to-all | bytes 327680 | tf_op jit(solution)/shard_map/all_to_all | solution.py:49
  102.5 0.3 join.1
  102.8 10.3 %all_to_all.33.rows_ref = bf16[8,16,512]{2,1,0:T(8,128)(2,1)S(1)} all-to-all(bf16[8,16,512]{2,1,0:T(8,128)(2,1)S(1)} %join.1), channel_id=1, replica_groups=mesh['y'=4,'z'=8,'x'=4,'core'=2] {'z'}, dimensions={0} | all-to-all | bytes 262144 | tf_op jit(solution)/shard_map/all_to_all | solution.py:49
  113.1 0.8 finish.1
  113.9 20.6 %all_to_all.34 = f32[32,16,128]{2,1,0:T(8,128)S(1)} all-to-all(f32[32,16,128]{2,1,0:T(8,128)S(1)} %finish.1), channel_id=1, replica_groups=mesh['y'=4,'z'=8,'x'=4,'core'=2] {'y','x','core'}, dimensions={0} | all-to-all | bytes 524288 | tf_op jit(solution)/shard_map/all_to_all | solution.py:49
  134.6 0.6 bitcast_reduce_fusion
  (12 shorter events, 0.0 us)
Async XLA Ops:
  0.0 1.4 %copy-start = (bf16[128,6144]{1,0:T(8,128)(2,1)S(1)}, bf16[128,6144]{1,0:T(8,128)(2,1)}, u32[]{:S(2)}) copy-start(bf16[128,6144]{1,0:T(8,128)(2,1)} %param.10) | copy-start | bytes 4718596
  0.0 26.9 %copy-start.1 = (bf16[4096,128]{1,0:T(8,128)(2,1)S(1)}, bf16[4096,128]{1,0:T(8,128)(2,1)}, u32[]{:S(2)}) copy-start(bf16[4096,128]{1,0:T(8,128)(2,1)} %k_ref.9) | copy-start | bytes 3145732
  1.4 18.8 %collective-permute-start = (bf16[128,768]{1,0:T(8,128)(2,1)S(1)}, bf16[128,768]{1,0:T(8,128)(2,1)S(1)}, u32[]{:S(2)}, u32[]{:S(2)}) collective-permute-start(bf16[128,768]{1,0:T(8,128)(2,1)S(1)} %constant_dynamic-slice_fusion.w0), channel_id=1, source_target_pairs={{0,64},{64,128},{128,192},{192,0},{1,65},{65,129},{129,193},{193,1... | collective-permute-start | bytes 589832 | tf_op jit(solution)/shard_map/ppermute | solution.py:55
  3.6 16.6 %collective-permute-start.1 = (bf16[128,768]{1,0:T(8,128)(2,1)S(1)}, bf16[128,768]{1,0:T(8,128)(2,1)}, u32[]{:S(2)}, u32[]{:S(2)}) collective-permute-start(bf16[128,768]{1,0:T(8,128)(2,1)S(1)} %constant_dynamic-slice_fusion.w0), channel_id=1, source_target_pairs={{0,128},{64,192},{128,0},{192,64},{1,129},{65,193},{129,1},{193,65... | collective-permute-start | bytes 589832 | tf_op jit(solution)/shard_map/ppermute | solution.py:55
  6.3 14.0 %collective-permute-start.2 = (bf16[128,768]{1,0:T(8,128)(2,1)S(1)}, bf16[128,768]{1,0:T(8,128)(2,1)}, u32[]{:S(2)}, u32[]{:S(2)}) collective-permute-start(bf16[128,768]{1,0:T(8,128)(2,1)S(1)} %constant_dynamic-slice_fusion.w0), channel_id=1, source_target_pairs={{0,192},{64,0},{128,64},{192,128},{1,193},{65,1},{129,65},{193,129... | collective-permute-start | bytes 589832 | tf_op jit(solution)/shard_map/ppermute | solution.py:55
  7.3 12.9 %collective-permute-start.3 = (bf16[512,128]{1,0:T(8,128)(2,1)}, bf16[512,128]{1,0:T(8,128)(2,1)S(1)}, u32[]{:S(2)}, u32[]{:S(2)}) collective-permute-start(bf16[512,128]{1,0:T(8,128)(2,1)} %w0.1), channel_id=1, source_target_pairs={{0,64},{64,128},{128,192},{192,0},{1,65},{65,129},{129,193},{193,1... | collective-permute-start | bytes 393224 | tf_op jit(solution)/shard_map/ppermute | solution.py:55
  7.7 12.5 %collective-permute-start.4 = (bf16[512,128]{1,0:T(8,128)(2,1)}, bf16[512,128]{1,0:T(8,128)(2,1)S(1)}, u32[]{:S(2)}, u32[]{:S(2)}) collective-permute-start(bf16[512,128]{1,0:T(8,128)(2,1)} %w0.1), channel_id=1, source_target_pairs={{0,192},{64,0},{128,64},{192,128},{1,193},{65,1},{129,65},{193,129... | collective-permute-start | bytes 393224 | tf_op jit(solution)/shard_map/ppermute | solution.py:55
  11.4 15.4 %all-to-all-start = ((bf16[32,16,256]{2,1,0:T(8,128)(2,1)}), bf16[32,16,256]{2,1,0:T(8,128)(2,1)S(1)}, u32[]{:S(2)}, u32[]{:S(2)}) async-start(bf16[32,16,256]{2,1,0:T(8,128)(2,1)} %split.1), calls=%async_computation | async-start | bytes 524288 | tf_op jit(solution)/shard_map/all_to_all | solution.py:49
  26.9 0.7 copy-start.3
  27.5 37.0 %copy-start.2 = (bf16[512,128]{1,0:T(8,128)(2,1)S(1)}, bf16[512,128]{1,0:T(8,128)(2,1)}, u32[]{:S(2)}) copy-start(bf16[512,128]{1,0:T(8,128)(2,1)} %w0.1) | copy-start | bytes 393220
  27.5 40.8 %copy-start.4 = (s32[3]{0:T(128)S(1)}, s32[3]{0:T(128)}, u32[]{:S(2)}) copy-start(s32[3]{0:T(128)} %pad_add_fusion.info_ref) | copy-start | bytes 40
  27.5 40.8 %copy-start.5 = (bf16[4096,128]{1,0:T(8,128)(2,1)S(1)}, bf16[4096,128]{1,0:T(8,128)(2,1)}, u32[]{:S(2)}) copy-start(bf16[4096,128]{1,0:T(8,128)(2,1)} %v_ref.7) | copy-start | bytes 3145732
  62.6 5.8 %collective-permute-start.9 = (bf16[8,16,512]{2,1,0:T(8,128)(2,1)S(1)}, bf16[8,16,512]{2,1,0:T(8,128)(2,1)S(1)}, u32[]{:S(2)}, u32[]{:S(2)}) collective-permute-start(bf16[8,16,512]{2,1,0:T(8,128)(2,1)S(1)} %all_to_all.31.q_ref), channel_id=1, source_target_pairs={{0,192},{64,0},{128,64},{192,128},{1,193},{65,1},{129,65},{193,129... | collective-permute-start | bytes 393224 | tf_op jit(solution)/shard_map/ppermute | solution.py:55
  64.6 25.5 %collective-permute-start.11 = (bf16[512,128]{1,0:T(8,128)(2,1)S(1)}, bf16[512,128]{1,0:T(8,128)(2,1)S(1)}, u32[]{:S(2)}, u32[]{:S(2)}) collective-permute-start(bf16[512,128]{1,0:T(8,128)(2,1)S(1)} %copy-done.2), channel_id=1, source_target_pairs={{0,128},{64,192},{128,0},{192,64},{1,129},{65,193},{129,1},{193,65... | collective-permute-start | bytes 393224 | tf_op jit(solution)/shard_map/ppermute | solution.py:55
  65.8 7.0 %collective-permute-start.7 = (bf16[8,16,512]{2,1,0:T(8,128)(2,1)S(1)}, bf16[8,16,512]{2,1,0:T(8,128)(2,1)S(1)}, u32[]{:S(2)}, u32[]{:S(2)}) collective-permute-start(bf16[8,16,512]{2,1,0:T(8,128)(2,1)S(1)} %all_to_all.31.q_ref), channel_id=1, source_target_pairs={{0,128},{64,192},{128,0},{192,64},{1,129},{65,193},{129,1},{193,65... | collective-permute-start | bytes 393224 | tf_op jit(solution)/shard_map/ppermute | solution.py:55
  67.6 14.4 %collective-permute-start.5 = (bf16[8,16,512]{2,1,0:T(8,128)(2,1)S(1)}, bf16[8,16,512]{2,1,0:T(8,128)(2,1)S(1)}, u32[]{:S(2)}, u32[]{:S(2)}) collective-permute-start(bf16[8,16,512]{2,1,0:T(8,128)(2,1)S(1)} %all_to_all.31.q_ref), channel_id=1, source_target_pairs={{0,64},{64,128},{128,192},{192,0},{1,65},{65,129},{129,193},{193,1... | collective-permute-start | bytes 393224 | tf_op jit(solution)/shard_map/ppermute | solution.py:55
  72.4 17.7 %collective-permute-start.10 = (bf16[8,16,640]{2,1,0:T(8,128)(2,1)S(1)}, bf16[8,16,640]{2,1,0:T(8,128)(2,1)S(1)}, u32[]{:S(2)}, u32[]{:S(2)}) collective-permute-start(bf16[8,16,640]{2,1,0:T(8,128)(2,1)S(1)} %attend.7), channel_id=1, source_target_pairs={{0,64},{64,128},{128,192},{192,0},{1,65},{65,129},{129,193},{193,1... | collective-permute-start | bytes 491528 | tf_op jit(solution)/shard_map/ppermute | solution.py:55
  76.9 13.3 %collective-permute-start.8 = (bf16[8,16,640]{2,1,0:T(8,128)(2,1)S(1)}, bf16[8,16,640]{2,1,0:T(8,128)(2,1)S(1)}, u32[]{:S(2)}, u32[]{:S(2)}) collective-permute-start(bf16[8,16,640]{2,1,0:T(8,128)(2,1)S(1)} %attend.6), channel_id=1, source_target_pairs={{0,128},{64,192},{128,0},{192,64},{1,129},{65,193},{129,1},{193,65... | collective-permute-start | bytes 491528 | tf_op jit(solution)/shard_map/ppermute | solution.py:55
  86.0 5.3 %collective-permute-start.6 = (bf16[8,16,640]{2,1,0:T(8,128)(2,1)S(1)}, bf16[8,16,640]{2,1,0:T(8,128)(2,1)S(1)}, u32[]{:S(2)}, u32[]{:S(2)}) collective-permute-start(bf16[8,16,640]{2,1,0:T(8,128)(2,1)S(1)} %attend.5), channel_id=1, source_target_pairs={{0,192},{64,0},{128,64},{192,128},{1,193},{65,1},{129,65},{193,129... | collective-permute-start | bytes 491528 | tf_op jit(solution)/shard_map/ppermute | solution.py:55

commit v7 on v6

--- a/solution.py
+++ b/solution.py
@@ -64,7 +64,7 @@
             sent_ref[y * HN + h] = both[y * OWN : (y + 1) * OWN]
 
 
-def project_kernel(info_ref, got_ref, w0, w1, w2, w3, table_ref, k_ref, o1, o2, mix_ref):
+def project_kernel(info_ref, got_ref, w0, w1, w2, w3, table_ref, k_ref, mix_ref):
     y = info_ref[2]
     total = None
     square = None
@@ -118,7 +118,11 @@
     return jnp.where(spot < GROUP, level, 0.0)
 
 
-def attend_kernel(shift, info_ref, q_ref, k_ref, v_ref, new_ref, o_ref):
+def attend_kernel(shift, info_ref, q_ref, k_ref, v_ref, new_ref, *refs):
+    o_ref = refs[-1]
+    if len(refs) > 1:
+        w_ref, passed_ref, o_ref = refs
+        passed_ref[...] = w_ref[...]
     count = info_ref[0]
     first_own = info_ref[1]
     source = lax.rem(info_ref[2] + YN - shift, YN)
@@ -174,7 +178,7 @@
     o_ref[:, :, FLAT:] = packed_levels(levels).reshape(ZN, OWN, HEAD_DIM)
 
 
-def merge_kernel(own_ref, one_ref, two_ref, three_ref, held_ref, o_ref):
+def merge_kernel(own_ref, one_ref, two_ref, three_ref, w1, w2, w3, o_ref):
     refs = (own_ref, one_ref, two_ref, three_ref)
     levels = [levels_of(ref[:, :, FLAT:].reshape(SHARE, HEAD_DIM)) for ref in refs]
     most = levels[0]
@@ -239,7 +243,6 @@
         compiler_params=params(56),
         name="split",
     )(hidden, norm_gain[None, :])
-    w_outs = [along_y(w_out, shift) for shift in range(YN)]
     columns = [along_y(own_columns, shift) for shift in range(YN)]
     got = exchange(sent, ("y", "x", "core"))
     first_own = z * (OWN * YN) + y * OWN
@@ -247,12 +250,12 @@
     table = rotary_table(lax.dynamic_slice_in_dim(positions, first_own, OWN))
     mix = pl.pallas_call(
         project_kernel,
-        in_specs=[SMEM] + [VMEM] * 9,
+        in_specs=[SMEM] + [VMEM] * 7,
         out_specs=VMEM,
         out_shape=shape((ZN, SLOTS * OWN + OWN // 2, HEAD_DIM), f32),
         compiler_params=params(16),
         name="project",
-    )(info, got, *columns, table, cache_keys, w_outs[1], w_outs[3])
+    )(info, got, *columns, table, cache_keys)
     mix = exchange(mix, "z")
     queries, new_rows = pl.pallas_call(
         turn_kernel,
@@ -265,24 +268,27 @@
     queries = exchange(queries, "z")
     parts = []
     for shift in range(YN):
-        part = pl.pallas_call(
+        extra = [w_out] if shift == 2 else []
+        *passed, part = pl.pallas_call(
             functools.partial(attend_kernel, shift),
-            in_specs=[SMEM, VMEM, VMEM, VMEM, VMEM],
-            out_specs=VMEM,
-            out_shape=shape((ZN, OWN, FLAT + HEAD_DIM), bf16),
+            in_specs=[SMEM, VMEM, VMEM, VMEM, VMEM] + [VMEM for _ in extra],
+            out_specs=[VMEM for _ in extra] + [VMEM],
+            out_shape=[shape(array.shape, bf16) for array in extra] + [shape((ZN, OWN, FLAT + HEAD_DIM), bf16)],
             compiler_params=params(24),
             cost_estimate=pl.CostEstimate(flops=4_000_000_000, bytes_accessed=0, transcendentals=0),
             name="attend",
-        )(info, along_y(queries, shift), cache_keys, cache_values, new_rows)
+        )(info, along_y(queries, shift), cache_keys, cache_values, new_rows, *extra)
+        if passed:
+            w_outs = [w_out] + [along_y(passed[0], step) for step in range(1, YN)]
         parts.append(along_y(part, -shift))
     part = pl.pallas_call(
         merge_kernel,
-        in_specs=[VMEM] * 5,
+        in_specs=[VMEM] * 7,
         out_specs=VMEM,
         out_shape=shape((ZN, OWN, FLAT + HEAD_DIM), bf16),
         compiler_params=params(),
         name="merge",
-    )(*parts, w_outs[2])
+    )(*parts, *w_outs[1:])
     part = exchange(part, "z")
     rows = pl.pallas_call(
         join_kernel,

time: 136 us -> 133 us (0.978)
  starting transfers between devices: 25.6 us -> 23.4 us
  waiting for transfers between devices: 8.57 us -> 10.1 us
    ppermute x12, starting transfers between devices: 19 us -> 15.8 us  [along_y(): return lax.ppermute(array, 'y', [(i, (i + shift) % YN) for i in range(YN)])]
    ppermute x12, waiting for transfers between devices: 2 us -> 3.71 us  [along_y(): return lax.ppermute(array, 'y', [(i, (i + shift) % YN) for i in range(YN)])]
  transfers between devices with their start and end apart: 13 -> 13, of which waited for: 3 -> 4; matrix products, arithmetic and copies ran while one was open for 1% -> 1% of each run, Pallas kernels for 13% -> 13%
where the time goes in v7:
time: 133 us; the launch traced here: 132 us
  blocking collectives  74.6 us (56%)
  starting transfers between devices  23.4 us (18%)
  Pallas kernels  20.1 us (15%)
  waiting for transfers between devices  10.1 us (8%)
  other arithmetic  1.66 us (1%)
  local copies, waits for them, and re-layouts  1.43 us (1%)
    all_to_all x5, blocking collectives, exchange(): return lax.all_to_all(array, axes, 0, 0, tiled=True)  74.6 us
    ppermute x12, starting transfers between devices, along_y(): return lax.ppermute(array, 'y', [(i, (i + shift) % YN) for i in range(YN)])  15.8 us
    pallas_call x4, Pallas kernels, per_device(): pl.pallas_call(functools.partial(attend_kernel, shift), in_specs=[SMEM, V...  15.4 us
    all_to_all x1, starting transfers between devices, exchange(): return lax.all_to_all(array, axes, 0, 0, tiled=True)  7.67 us
    all_to_all x1, waiting for transfers between devices, exchange(): return lax.all_to_all(array, axes, 0, 0, tiled=True)  6.42 us
    ppermute x12, waiting for transfers between devices, along_y(): return lax.ppermute(array, 'y', [(i, (i + shift) % YN) for i in range(YN)])  3.71 us
  transfers between devices with their start and end apart: 13, of which 4 were waited for; matrix products, arithmetic and copies ran while one was open for 1% of the time, Pallas kernels for 13%

profile of v7, /device:TPU:1, one launch (start us, length us, event | category | flops | bytes accessed | tf_op | source)
XLA Modules:
  0.0 132.2 jit_solution(7972363062880311578)
XLA Ops:
  0.0 1.4 %copy-done = bf16[128,6144]{1,0:T(8,128)(2,1)S(1)} copy-done((bf16[128,6144]{1,0:T(8,128)(2,1)S(1)}, bf16[128,6144]{1,0:T(8,128)(2,1)}, u32[]{:S(2)}) %copy-start) | copy-done | bytes 1572888
  1.4 3.6 %collective-permute-start.2 = (bf16[128,768]{1,0:T(8,128)(2,1)S(1)}, bf16[128,768]{1,0:T(8,128)(2,1)S(1)}, u32[]{:S(2)}, u32[]{:S(2)}) collective-permute-start(bf16[128,768]{1,0:T(8,128)(2,1)S(1)} %constant_dynamic-slice_fusion.w0), channel_id=1, source_target_pairs={{0,192},{64,0},{128,64},{192,128},{1,193},{65,1},{129,65},{193,129... | collective-permute-start | bytes 589832 | tf_op jit(solution)/shard_map/ppermute | solution.py:55
  5.1 0.3 collective-permute-start.1
  5.4 0.7 collective-permute-start
  6.1 1.4 %split.1 = bf16[32,16,256]{2,1,0:T(8,128)(2,1)} custom-call(bf16[64,128]{1,0:T(8,128)(2,1)} %hidden_ref.1, f32[1,128]{1,0:T(1,128)} %bitcast.6), custom_call_target="tpu_custom_call" | custom-call | tf_op jit(solution)/shard_map/split/pallas_call | solution.py:238
  7.6 7.7 %all-to-all-start = ((bf16[32,16,256]{2,1,0:T(8,128)(2,1)}), bf16[32,16,256]{2,1,0:T(8,128)(2,1)S(1)}, u32[]{:S(2)}, u32[]{:S(2)}) async-start(bf16[32,16,256]{2,1,0:T(8,128)(2,1)} %split.1), calls=%async_computation | async-start | bytes 524288 | tf_op jit(solution)/shard_map/all_to_all | solution.py:49
  15.3 0.8 dynamic-slice_convert_fusion
  16.0 0.1 multiply_cosine_fusion
  16.8 0.1 pad_add_fusion.info_ref
  16.9 0.1 pad_maximum_fusion.table_ref
  16.9 0.0 collective-permute-done.2.w3
  17.0 0.0 collective-permute-done.1.w2
  17.0 0.8 collective-permute-done.w1
  17.7 6.4 %all-to-all-done.got_ref = bf16[32,16,256]{2,1,0:T(8,128)(2,1)S(1)} async-done(((bf16[32,16,256]{2,1,0:T(8,128)(2,1)}), bf16[32,16,256]{2,1,0:T(8,128)(2,1)S(1)}, u32[]{:S(2)}, u32[]{:S(2)}) %all-to-all-start) | async-done | bytes 262176 | tf_op jit(solution)/shard_map/all_to_all | solution.py:49
  24.1 0.0 copy-done.1
  24.1 1.4 %project.1 = f32[8,104,128]{2,1,0:T(8,128)S(1)} custom-call(s32[3]{0:T(128)S(1)} %pad_add_fusion.info_ref, bf16[32,16,256]{2,1,0:T(8,128)(2,1)S(1)} %all-to-all-done.got_ref, bf16[128,768]{1,0:T(8,128)(2,1)S(1)} %constant_dynamic-slice_fusion.w0, bf16[128,768]{1,0:T(8,128)(2,1)} %collective-permute-done.w1, bf16[128,768]{1,0:T(8,128)(2,1)S(1)} %collective-permute-done.1.w2, ...), custom_call_target="tpu_custom_call" | custom-call | tf_op jit(solution)/shard_map/project/pallas_call | solution.py:251
  25.5 22.9 %all_to_all.30.mix_ref = f32[8,104,128]{2,1,0:T(8,128)S(1)} all-to-all(f32[8,104,128]{2,1,0:T(8,128)S(1)} %project.1), channel_id=1, replica_groups=mesh['y'=4,'z'=8,'x'=4,'core'=2] {'z'}, dimensions={0} | all-to-all | bytes 851968 | tf_op jit(solution)/shard_map/all_to_all | solution.py:49
  48.5 0.2 turn.1
  48.7 10.4 %all_to_all.31.q_ref = bf16[8,16,512]{2,1,0:T(8,128)(2,1)S(1)} all-to-all(bf16[8,16,512]{2,1,0:T(8,128)(2,1)S(1)} %get-tuple-element.9), channel_id=1, replica_groups=mesh['y'=4,'z'=8,'x'=4,'core'=2] {'z'}, dimensions={0} | all-to-all | bytes 262144 | tf_op jit(solution)/shard_map/all_to_all | solution.py:49
  59.1 2.3 %collective-permute-start.5 = (bf16[8,16,512]{2,1,0:T(8,128)(2,1)S(1)}, bf16[8,16,512]{2,1,0:T(8,128)(2,1)S(1)}, u32[]{:S(2)}, u32[]{:S(2)}) collective-permute-start(bf16[8,16,512]{2,1,0:T(8,128)(2,1)S(1)} %all_to_all.31.q_ref), channel_id=1, source_target_pairs={{0,128},{64,192},{128,0},{192,64},{1,129},{65,193},{129,1},{193,65... | collective-permute-start | bytes 393224 | tf_op jit(solution)/shard_map/ppermute | solution.py:55
  61.4 1.6 %collective-permute-start.7 = (bf16[8,16,512]{2,1,0:T(8,128)(2,1)S(1)}, bf16[8,16,512]{2,1,0:T(8,128)(2,1)S(1)}, u32[]{:S(2)}, u32[]{:S(2)}) collective-permute-start(bf16[8,16,512]{2,1,0:T(8,128)(2,1)S(1)} %all_to_all.31.q_ref), channel_id=1, source_target_pairs={{0,192},{64,0},{128,64},{192,128},{1,193},{65,1},{129,65},{193,129... | collective-permute-start | bytes 393224 | tf_op jit(solution)/shard_map/ppermute | solution.py:55
  63.0 0.0 collective-permute-start.3
  63.0 1.5 %collective-permute-done.5.q_ref = bf16[8,16,512]{2,1,0:T(8,128)(2,1)S(1)} collective-permute-done((bf16[8,16,512]{2,1,0:T(8,128)(2,1)S(1)}, bf16[8,16,512]{2,1,0:T(8,128)(2,1)S(1)}, u32[]{:S(2)}, u32[]{:S(2)}) %collective-permute-start.5) | collective-permute-done | bytes 131104 | tf_op jit(solution)/shard_map/ppermute | solution.py:55
  64.4 3.9 %attend.6 = (bf16[512,128]{1,0:T(8,128)(2,1)S(1)}, bf16[8,16,640]{2,1,0:T(8,128)(2,1)S(1)}) custom-call(s32[3]{0:T(128)S(1)} %pad_add_fusion.info_ref, bf16[8,16,512]{2,1,0:T(8,128)(2,1)S(1)} %collective-permute-done.5.q_ref, bf16[4096,128]{1,0:T(8,128)(2,1)S(1)} %copy-done.1, bf16[4096,128]{1,0:T(8,128)(2,1)S(1)} %copy-done.3, ...), custom_call_target="tpu_custom_call" | custom-call | flops 4000000000 | tf_op jit(solution)/shard_map/attend/pallas_call | solution.py:272
  68.3 2.0 %collective-permute-start.11 = (bf16[512,128]{1,0:T(8,128)(2,1)S(1)}, bf16[512,128]{1,0:T(8,128)(2,1)S(1)}, u32[]{:S(2)}, u32[]{:S(2)}) collective-permute-start(bf16[512,128]{1,0:T(8,128)(2,1)S(1)} %get-tuple-element.12), channel_id=1, source_target_pairs={{0,192},{64,0},{128,64},{192,128},{1,193},{65,1},{129,65},{193,129... | collective-permute-start | bytes 393224 | tf_op jit(solution)/shard_map/ppermute | solution.py:55
  70.4 1.4 %collective-permute-start.10 = (bf16[512,128]{1,0:T(8,128)(2,1)S(1)}, bf16[512,128]{1,0:T(8,128)(2,1)S(1)}, u32[]{:S(2)}, u32[]{:S(2)}) collective-permute-start(bf16[512,128]{1,0:T(8,128)(2,1)S(1)} %get-tuple-element.12), channel_id=1, source_target_pairs={{0,128},{64,192},{128,0},{192,64},{1,129},{65,193},{129,1},{193,65... | collective-permute-start | bytes 393224 | tf_op jit(solution)/shard_map/ppermute | solution.py:55
  71.7 0.0 collective-permute-start.9
  71.7 0.0 collective-permute-done.3.q_ref
  71.7 1.9 %collective-permute-start.6 = (bf16[8,16,640]{2,1,0:T(8,128)(2,1)S(1)}, bf16[8,16,640]{2,1,0:T(8,128)(2,1)S(1)}, u32[]{:S(2)}, u32[]{:S(2)}) collective-permute-start(bf16[8,16,640]{2,1,0:T(8,128)(2,1)S(1)} %get-tuple-element.11), channel_id=1, source_target_pairs={{0,128},{64,192},{128,0},{192,64},{1,129},{65,193},{129,1},{193,65... | collective-permute-start | bytes 491528 | tf_op jit(solution)/shard_map/ppermute | solution.py:55
  73.6 3.9 %attend.5 = bf16[8,16,640]{2,1,0:T(8,128)(2,1)S(1)} custom-call(s32[3]{0:T(128)S(1)} %pad_add_fusion.info_ref, bf16[8,16,512]{2,1,0:T(8,128)(2,1)S(1)} %collective-permute-done.3.q_ref, bf16[4096,128]{1,0:T(8,128)(2,1)S(1)} %copy-done.1, bf16[4096,128]{1,0:T(8,128)(2,1)S(1)} %copy-done.3, bf16[16,256]{1,0:T(8,128)(2,1)S(1)} %get-tuple-element.10.new_ref), custom_call_target="tpu_custom_call" | custom-call | flops 4000000000 | tf_op jit(solution)/shard_map/attend/pallas_call | solution.py:272
  77.5 0.0 collective-permute-done.7.q_ref
  77.5 1.8 %collective-permute-start.4 = (bf16[8,16,640]{2,1,0:T(8,128)(2,1)S(1)}, bf16[8,16,640]{2,1,0:T(8,128)(2,1)S(1)}, u32[]{:S(2)}, u32[]{:S(2)}) collective-permute-start(bf16[8,16,640]{2,1,0:T(8,128)(2,1)S(1)} %attend.5), channel_id=1, source_target_pairs={{0,192},{64,0},{128,64},{192,128},{1,193},{65,1},{129,65},{193,129... | collective-permute-start | bytes 491528 | tf_op jit(solution)/shard_map/ppermute | solution.py:55
  79.3 3.9 %attend.7 = bf16[8,16,640]{2,1,0:T(8,128)(2,1)S(1)} custom-call(s32[3]{0:T(128)S(1)} %pad_add_fusion.info_ref, bf16[8,16,512]{2,1,0:T(8,128)(2,1)S(1)} %collective-permute-done.7.q_ref, bf16[4096,128]{1,0:T(8,128)(2,1)S(1)} %copy-done.1, bf16[4096,128]{1,0:T(8,128)(2,1)S(1)} %copy-done.3, bf16[16,256]{1,0:T(8,128)(2,1)S(1)} %get-tuple-element.10.new_ref), custom_call_target="tpu_custom_call" | custom-call | flops 4000000000 | tf_op jit(solution)/shard_map/attend/pallas_call | solution.py:272
  83.2 0.0 collective-permute-done.11.w3
  83.2 0.1 collective-permute-start.8
  83.3 3.9 %attend.4.own_ref = bf16[8,16,640]{2,1,0:T(8,128)(2,1)S(1)} custom-call(s32[3]{0:T(128)S(1)} %pad_add_fusion.info_ref, bf16[8,16,512]{2,1,0:T(8,128)(2,1)S(1)} %all_to_all.31.q_ref, bf16[4096,128]{1,0:T(8,128)(2,1)S(1)} %copy-done.1, bf16[4096,128]{1,0:T(8,128)(2,1)S(1)} %copy-done.3, bf16[16,256]{1,0:T(8,128)(2,1)S(1)} %get-tuple-element.10.new_ref), custom_call_target="tpu_custom_call" | custom-call | flops 4000000000 | tf_op jit(solution)/shard_map/attend/pallas_call | solution.py:272
  87.2 0.0 collective-permute-done.10.w2
  87.2 0.0 collective-permute-done.9.w1
  87.2 0.0 collective-permute-done.6.two_ref
  87.2 0.0 collective-permute-done.4.one_ref
  87.2 1.5 %collective-permute-done.8.three_ref = bf16[8,16,640]{2,1,0:T(8,128)(2,1)S(1)} collective-permute-done((bf16[8,16,640]{2,1,0:T(8,128)(2,1)S(1)}, bf16[8,16,640]{2,1,0:T(8,128)(2,1)S(1)}, u32[]{:S(2)}, u32[]{:S(2)}) %collective-permute-start.8) | collective-permute-done | bytes 163872 | tf_op jit(solution)/shard_map/ppermute | solution.py:55
  88.7 0.5 merge.1
  89.2 10.7 %all_to_all.32.back_ref = bf16[8,16,640]{2,1,0:T(8,128)(2,1)S(1)} all-to-all(bf16[8,16,640]{2,1,0:T(8,128)(2,1)S(1)} %merge.1), channel_id=1, replica_groups=mesh['y'=4,'z'=8,'x'=4,'core'=2] {'z'}, dimensions={0} | all-to-all | bytes 327680 | tf_op jit(solution)/shard_map/all_to_all | solution.py:49
  99.9 0.3 join.1
  100.2 10.3 %all_to_all.33.rows_ref = bf16[8,16,512]{2,1,0:T(8,128)(2,1)S(1)} all-to-all(bf16[8,16,512]{2,1,0:T(8,128)(2,1)S(1)} %join.1), channel_id=1, replica_groups=mesh['y'=4,'z'=8,'x'=4,'core'=2] {'z'}, dimensions={0} | all-to-all | bytes 262144 | tf_op jit(solution)/shard_map/all_to_all | solution.py:49
  110.5 0.8 finish.1
  111.3 20.3 %all_to_all.34 = f32[32,16,128]{2,1,0:T(8,128)S(1)} all-to-all(f32[32,16,128]{2,1,0:T(8,128)S(1)} %finish.1), channel_id=1, replica_groups=mesh['y'=4,'z'=8,'x'=4,'core'=2] {'y','x','core'}, dimensions={0} | all-to-all | bytes 524288 | tf_op jit(solution)/shard_map/all_to_all | solution.py:49
  131.6 0.6 bitcast_reduce_fusion
  (8 shorter events, 0.0 us)
Async XLA Ops:
  0.0 1.4 %copy-start = (bf16[128,6144]{1,0:T(8,128)(2,1)S(1)}, bf16[128,6144]{1,0:T(8,128)(2,1)}, u32[]{:S(2)}) copy-start(bf16[128,6144]{1,0:T(8,128)(2,1)} %param.10) | copy-start | bytes 4718596
  0.0 24.1 %copy-start.1 = (bf16[4096,128]{1,0:T(8,128)(2,1)S(1)}, bf16[4096,128]{1,0:T(8,128)(2,1)}, u32[]{:S(2)}) copy-start(bf16[4096,128]{1,0:T(8,128)(2,1)} %k_ref.9) | copy-start | bytes 3145732
  1.4 15.5 %collective-permute-start.2 = (bf16[128,768]{1,0:T(8,128)(2,1)S(1)}, bf16[128,768]{1,0:T(8,128)(2,1)S(1)}, u32[]{:S(2)}, u32[]{:S(2)}) collective-permute-start(bf16[128,768]{1,0:T(8,128)(2,1)S(1)} %constant_dynamic-slice_fusion.w0), channel_id=1, source_target_pairs={{0,192},{64,0},{128,64},{192,128},{1,193},{65,1},{129,65},{193,129... | collective-permute-start | bytes 589832 | tf_op jit(solution)/shard_map/ppermute | solution.py:55
  5.1 11.9 %collective-permute-start.1 = (bf16[128,768]{1,0:T(8,128)(2,1)S(1)}, bf16[128,768]{1,0:T(8,128)(2,1)S(1)}, u32[]{:S(2)}, u32[]{:S(2)}) collective-permute-start(bf16[128,768]{1,0:T(8,128)(2,1)S(1)} %constant_dynamic-slice_fusion.w0), channel_id=1, source_target_pairs={{0,128},{64,192},{128,0},{192,64},{1,129},{65,193},{129,1},{193,65... | collective-permute-start | bytes 589832 | tf_op jit(solution)/shard_map/ppermute | solution.py:55
  5.4 12.3 %collective-permute-start = (bf16[128,768]{1,0:T(8,128)(2,1)S(1)}, bf16[128,768]{1,0:T(8,128)(2,1)}, u32[]{:S(2)}, u32[]{:S(2)}) collective-permute-start(bf16[128,768]{1,0:T(8,128)(2,1)S(1)} %constant_dynamic-slice_fusion.w0), channel_id=1, source_target_pairs={{0,64},{64,128},{128,192},{192,0},{1,65},{65,129},{129,193},{193,1... | collective-permute-start | bytes 589832 | tf_op jit(solution)/shard_map/ppermute | solution.py:55
  7.6 16.6 %all-to-all-start = ((bf16[32,16,256]{2,1,0:T(8,128)(2,1)}), bf16[32,16,256]{2,1,0:T(8,128)(2,1)S(1)}, u32[]{:S(2)}, u32[]{:S(2)}) async-start(bf16[32,16,256]{2,1,0:T(8,128)(2,1)} %split.1), calls=%async_computation | async-start | bytes 524288 | tf_op jit(solution)/shard_map/all_to_all | solution.py:49
  24.1 40.3 %copy-start.2 = (bf16[512,128]{1,0:T(8,128)(2,1)S(1)}, bf16[512,128]{1,0:T(8,128)(2,1)}, u32[]{:S(2)}) copy-start(bf16[512,128]{1,0:T(8,128)(2,1)} %w0.1) | copy-start | bytes 393220
  24.1 40.3 %copy-start.3 = (bf16[4096,128]{1,0:T(8,128)(2,1)S(1)}, bf16[4096,128]{1,0:T(8,128)(2,1)}, u32[]{:S(2)}) copy-start(bf16[4096,128]{1,0:T(8,128)(2,1)} %v_ref.7) | copy-start | bytes 3145732
  59.1 5.3 %collective-permute-start.5 = (bf16[8,16,512]{2,1,0:T(8,128)(2,1)S(1)}, bf16[8,16,512]{2,1,0:T(8,128)(2,1)S(1)}, u32[]{:S(2)}, u32[]{:S(2)}) collective-permute-start(bf16[8,16,512]{2,1,0:T(8,128)(2,1)S(1)} %all_to_all.31.q_ref), channel_id=1, source_target_pairs={{0,128},{64,192},{128,0},{192,64},{1,129},{65,193},{129,1},{193,65... | collective-permute-start | bytes 393224 | tf_op jit(solution)/shard_map/ppermute | solution.py:55
  61.4 16.1 %collective-permute-start.7 = (bf16[8,16,512]{2,1,0:T(8,128)(2,1)S(1)}, bf16[8,16,512]{2,1,0:T(8,128)(2,1)S(1)}, u32[]{:S(2)}, u32[]{:S(2)}) collective-permute-start(bf16[8,16,512]{2,1,0:T(8,128)(2,1)S(1)} %all_to_all.31.q_ref), channel_id=1, source_target_pairs={{0,192},{64,0},{128,64},{192,128},{1,193},{65,1},{129,65},{193,129... | collective-permute-start | bytes 393224 | tf_op jit(solution)/shard_map/ppermute | solution.py:55
  63.0 8.8 %collective-permute-start.3 = (bf16[8,16,512]{2,1,0:T(8,128)(2,1)S(1)}, bf16[8,16,512]{2,1,0:T(8,128)(2,1)S(1)}, u32[]{:S(2)}, u32[]{:S(2)}) collective-permute-start(bf16[8,16,512]{2,1,0:T(8,128)(2,1)S(1)} %all_to_all.31.q_ref), channel_id=1, source_target_pairs={{0,64},{64,128},{128,192},{192,0},{1,65},{65,129},{129,193},{193,1... | collective-permute-start | bytes 393224 | tf_op jit(solution)/shard_map/ppermute | solution.py:55
  68.3 14.9 %collective-permute-start.11 = (bf16[512,128]{1,0:T(8,128)(2,1)S(1)}, bf16[512,128]{1,0:T(8,128)(2,1)S(1)}, u32[]{:S(2)}, u32[]{:S(2)}) collective-permute-start(bf16[512,128]{1,0:T(8,128)(2,1)S(1)} %get-tuple-element.12), channel_id=1, source_target_pairs={{0,192},{64,0},{128,64},{192,128},{1,193},{65,1},{129,65},{193,129... | collective-permute-start | bytes 393224 | tf_op jit(solution)/shard_map/ppermute | solution.py:55
  70.4 16.8 %collective-permute-start.10 = (bf16[512,128]{1,0:T(8,128)(2,1)S(1)}, bf16[512,128]{1,0:T(8,128)(2,1)S(1)}, u32[]{:S(2)}, u32[]{:S(2)}) collective-permute-start(bf16[512,128]{1,0:T(8,128)(2,1)S(1)} %get-tuple-element.12), channel_id=1, source_target_pairs={{0,128},{64,192},{128,0},{192,64},{1,129},{65,193},{129,1},{193,65... | collective-permute-start | bytes 393224 | tf_op jit(solution)/shard_map/ppermute | solution.py:55
  71.7 15.5 %collective-permute-start.9 = (bf16[512,128]{1,0:T(8,128)(2,1)S(1)}, bf16[512,128]{1,0:T(8,128)(2,1)S(1)}, u32[]{:S(2)}, u32[]{:S(2)}) collective-permute-start(bf16[512,128]{1,0:T(8,128)(2,1)S(1)} %get-tuple-element.12), channel_id=1, source_target_pairs={{0,64},{64,128},{128,192},{192,0},{1,65},{65,129},{129,193},{193,1... | collective-permute-start | bytes 393224 | tf_op jit(solution)/shard_map/ppermute | solution.py:55
  71.7 15.5 %collective-permute-start.6 = (bf16[8,16,640]{2,1,0:T(8,128)(2,1)S(1)}, bf16[8,16,640]{2,1,0:T(8,128)(2,1)S(1)}, u32[]{:S(2)}, u32[]{:S(2)}) collective-permute-start(bf16[8,16,640]{2,1,0:T(8,128)(2,1)S(1)} %get-tuple-element.11), channel_id=1, source_target_pairs={{0,128},{64,192},{128,0},{192,64},{1,129},{65,193},{129,1},{193,65... | collective-permute-start | bytes 491528 | tf_op jit(solution)/shard_map/ppermute | solution.py:55
  77.5 9.7 %collective-permute-start.4 = (bf16[8,16,640]{2,1,0:T(8,128)(2,1)S(1)}, bf16[8,16,640]{2,1,0:T(8,128)(2,1)S(1)}, u32[]{:S(2)}, u32[]{:S(2)}) collective-permute-start(bf16[8,16,640]{2,1,0:T(8,128)(2,1)S(1)} %attend.5), channel_id=1, source_target_pairs={{0,192},{64,0},{128,64},{192,128},{1,193},{65,1},{129,65},{193,129... | collective-permute-start | bytes 491528 | tf_op jit(solution)/shard_map/ppermute | solution.py:55
  83.2 5.5 %collective-permute-start.8 = (bf16[8,16,640]{2,1,0:T(8,128)(2,1)S(1)}, bf16[8,16,640]{2,1,0:T(8,128)(2,1)S(1)}, u32[]{:S(2)}, u32[]{:S(2)}) collective-permute-start(bf16[8,16,640]{2,1,0:T(8,128)(2,1)S(1)} %attend.7), channel_id=1, source_target_pairs={{0,64},{64,128},{128,192},{192,0},{1,65},{65,129},{129,193},{193,1... | collective-permute-start | bytes 491528 | tf_op jit(solution)/shard_map/ppermute | solution.py:55

commit v8 on v7

--- a/solution.py
+++ b/solution.py
@@ -32,6 +32,7 @@
 TAIL = 128
 KEY_TILE = 512
 SHARE = OWN * ZN
+RESULT = FLAT + HEAD_DIM
 
 VMEM = pl.BlockSpec(memory_space=pltpu.VMEM)
 SMEM = pl.BlockSpec(memory_space=pltpu.SMEM)
@@ -121,8 +122,12 @@
 def attend_kernel(shift, info_ref, q_ref, k_ref, v_ref, new_ref, *refs):
     o_ref = refs[-1]
     if len(refs) > 1:
-        w_ref, passed_ref, o_ref = refs
-        passed_ref[...] = w_ref[...]
+        w_ref = refs[0]
+        for s in range(GROUP):
+            piece = w_ref[s * HEAD_DIM : (s + 1) * HEAD_DIM].reshape(ZN, OWN, HEAD_DIM)
+            o_ref[:, :, RESULT + s * HEAD_DIM : RESULT + (s + 1) * HEAD_DIM] = piece
+    if len(refs) > 2:
+        refs[1][...] = refs[0][...]
     count = info_ref[0]
     first_own = info_ref[1]
     source = lax.rem(info_ref[2] + YN - shift, YN)
@@ -151,7 +156,10 @@
     best = jnp.full((rows, 1), NEG_FILL, jnp.float32)
     sums = jnp.zeros((rows, 2 * HEAD_DIM), jnp.float32)
     for start in range(0, KEYS_DEV + TAIL, KEY_TILE):
-        if start < KEYS_DEV:
+        if start < KEYS_DEV // 2:
+            values = jnp.concatenate([v_ref[start : start + KEY_TILE, :], first_lane(KEY_TILE)], axis=1)
+            scores = product(queries, k_ref[start : start + KEY_TILE, :])
+        elif start < KEYS_DEV:
             index = lax.broadcasted_iota(jnp.int32, (KEY_TILE, HEAD_DIM), 0) + start
             hide = jnp.where((lane(KEY_TILE) == 0) & (index >= count), NEG_FILL, 0.0).astype(jnp.bfloat16)
             keys = jnp.concatenate([k_ref[start : start + KEY_TILE, :], hide], axis=1)
@@ -175,12 +183,12 @@
         here = slice(s * SHARE, (s + 1) * SHARE)
         o_ref[:, :, s * HEAD_DIM : (s + 1) * HEAD_DIM] = outs[here].reshape(ZN, OWN, HEAD_DIM)
         levels = jnp.where(spot == s, level[here], levels)
-    o_ref[:, :, FLAT:] = packed_levels(levels).reshape(ZN, OWN, HEAD_DIM)
-
-
-def merge_kernel(own_ref, one_ref, two_ref, three_ref, w1, w2, w3, o_ref):
+    o_ref[:, :, FLAT:RESULT] = packed_levels(levels).reshape(ZN, OWN, HEAD_DIM)
+
+
+def merge_kernel(own_ref, one_ref, two_ref, three_ref, held_ref, o_ref):
     refs = (own_ref, one_ref, two_ref, three_ref)
-    levels = [levels_of(ref[:, :, FLAT:].reshape(SHARE, HEAD_DIM)) for ref in refs]
+    levels = [levels_of(ref[:, :, FLAT:RESULT].reshape(SHARE, HEAD_DIM)) for ref in refs]
     most = levels[0]
     for level in levels[1:]:
         most = jnp.maximum(most, level)
@@ -214,11 +222,16 @@
         rows_ref[z] = attended
 
 
-def finish_kernel(info_ref, rows_ref, w0, w1, w2, w3, o_ref):
+def finish_kernel(info_ref, rows_ref, w0, three_ref, two_ref, w3, o_ref):
     rows = rows_ref[...].reshape(SHARE, FLAT)
-    for shift, w in enumerate((w0, w1, w2, w3)):
+
+    def carried(ref):
+        starts = range(RESULT, RESULT + FLAT, HEAD_DIM)
+        return jnp.concatenate([ref[:, :, n : n + HEAD_DIM].reshape(SHARE, HEAD_DIM) for n in starts], axis=0)
+
+    for shift, w in enumerate((w0[...], carried(three_ref), carried(two_ref), w3[...])):
         source = lax.rem(info_ref[2] + YN - shift, YN)
-        term = jnp.dot(rows, w[...], preferred_element_type=jnp.float32)
+        term = jnp.dot(rows, w, preferred_element_type=jnp.float32)
         o_ref[pl.ds(source * HN, HN)] = term.reshape(HN, OWN, HEAD_DIM)
 
 
@@ -268,27 +281,30 @@
     queries = exchange(queries, "z")
     parts = []
     for shift in range(YN):
-        extra = [w_out] if shift == 2 else []
+        carries = shift in (2, 3)
+        outs = [shape((ZN, OWN, RESULT + (FLAT if carries else 0)), bf16)]
+        if shift == 2:
+            outs.insert(0, shape(w_out.shape, bf16))
         *passed, part = pl.pallas_call(
             functools.partial(attend_kernel, shift),
-            in_specs=[SMEM, VMEM, VMEM, VMEM, VMEM] + [VMEM for _ in extra],
-            out_specs=[VMEM for _ in extra] + [VMEM],
-            out_shape=[shape(array.shape, bf16) for array in extra] + [shape((ZN, OWN, FLAT + HEAD_DIM), bf16)],
+            in_specs=[SMEM] + [VMEM] * (5 if carries else 4),
+            out_specs=[VMEM for _ in outs],
+            out_shape=outs,
             compiler_params=params(24),
             cost_estimate=pl.CostEstimate(flops=4_000_000_000, bytes_accessed=0, transcendentals=0),
             name="attend",
-        )(info, along_y(queries, shift), cache_keys, cache_values, new_rows, *extra)
+        )(info, along_y(queries, shift), cache_keys, cache_values, new_rows, *([w_out] if carries else []))
         if passed:
-            w_outs = [w_out] + [along_y(passed[0], step) for step in range(1, YN)]
+            last_columns = along_y(passed[0], 3)
         parts.append(along_y(part, -shift))
     part = pl.pallas_call(
         merge_kernel,
-        in_specs=[VMEM] * 7,
+        in_specs=[VMEM] * 5,
         out_specs=VMEM,
         out_shape=shape((ZN, OWN, FLAT + HEAD_DIM), bf16),
         compiler_params=params(),
         name="merge",
-    )(*parts, *w_outs[1:])
+    )(*parts, last_columns)
     part = exchange(part, "z")
     rows = pl.pallas_call(
         join_kernel,
@@ -306,7 +322,7 @@
         out_shape=shape((YN * HN, OWN, HEAD_DIM), f32),
         compiler_params=params(),
         name="finish",
-    )(info, rows, *w_outs)
+    )(info, rows, w_out, parts[3], parts[2], last_columns)
     result = exchange(result, ("y", "x", "core")).reshape(YN, HN, OWN, HEAD_DIM)
     return jnp.sum(result, axis=1).reshape(YN * OWN, HEAD_DIM).astype(bf16)
 

time: 133 us -> 131 us (0.985)
  waiting for transfers between devices: 10.1 us -> 14.1 us
  starting transfers between devices: 23.4 us -> 19.7 us
    ppermute x12 -> x10, waiting for transfers between devices: 3.71 us -> 7.71 us  [along_y(): return lax.ppermute(array, 'y', [(i, (i + shift) % YN) for i in range(YN)])]
    ppermute x12 -> x10, starting transfers between devices: 15.8 us -> 12.1 us  [along_y(): return lax.ppermute(array, 'y', [(i, (i + shift) % YN) for i in range(YN)])]
  transfers between devices with their start and end apart: 13 -> 11, of which waited for: 4 -> 4; matrix products, arithmetic and copies ran while one was open for 1% -> 1% of each run, Pallas kernels for 13% -> 12%
where the time goes in v8:
time: 131 us
  blocking collectives  73.4 us (56%)
  starting transfers between devices  19.7 us (15%)
  Pallas kernels  19.4 us (15%)
  waiting for transfers between devices  14.1 us (11%)
  other arithmetic  1.66 us (1%)
  local copies, waits for them, and re-layouts  1.43 us (1%)
    all_to_all x5, blocking collectives, exchange(): return lax.all_to_all(array, axes, 0, 0, tiled=True)  73.4 us
    pallas_call x4, Pallas kernels, per_device(): pl.pallas_call(functools.partial(attend_kernel, shift), in_specs=[SMEM] +...  14.7 us
    ppermute x10, starting transfers between devices, along_y(): return lax.ppermute(array, 'y', [(i, (i + shift) % YN) for i in range(YN)])  12.1 us
    ppermute x10, waiting for transfers between devices, along_y(): return lax.ppermute(array, 'y', [(i, (i + shift) % YN) for i in range(YN)])  7.71 us
    all_to_all x1, starting transfers between devices, exchange(): return lax.all_to_all(array, axes, 0, 0, tiled=True)  7.67 us
    all_to_all x1, waiting for transfers between devices, exchange(): return lax.all_to_all(array, axes, 0, 0, tiled=True)  6.41 us
  transfers between devices with their start and end apart: 11, of which 4 were waited for; matrix products, arithmetic and copies ran while one was open for 1% of the time, Pallas kernels for 12%

profile of v8, /device:TPU:1, one launch (start us, length us, event | category | flops | bytes accessed | tf_op | source)
XLA Modules:
  0.0 130.5 jit_solution(7068738869706051532)
XLA Ops:
  0.0 0.0 copy-start
  0.0 0.0 copy-start.1
  0.0 1.4 %copy-done = bf16[128,6144]{1,0:T(8,128)(2,1)S(1)} copy-done((bf16[128,6144]{1,0:T(8,128)(2,1)S(1)}, bf16[128,6144]{1,0:T(8,128)(2,1)}, u32[]{:S(2)}) %copy-start) | copy-done | bytes 1572888
  1.4 3.6 %collective-permute-start.2 = (bf16[128,768]{1,0:T(8,128)(2,1)S(1)}, bf16[128,768]{1,0:T(8,128)(2,1)S(1)}, u32[]{:S(2)}, u32[]{:S(2)}) collective-permute-start(bf16[128,768]{1,0:T(8,128)(2,1)S(1)} %constant_dynamic-slice_fusion.w0), channel_id=1, source_target_pairs={{0,192},{64,0},{128,64},{192,128},{1,193},{65,1},{129,65},{193,129... | collective-permute-start | bytes 589832 | tf_op jit(solution)/shard_map/ppermute | solution.py:56
  5.1 0.3 collective-permute-start.1
  5.4 0.7 collective-permute-start
  6.1 1.4 %split.1 = bf16[32,16,256]{2,1,0:T(8,128)(2,1)} custom-call(bf16[64,128]{1,0:T(8,128)(2,1)} %hidden_ref.1, f32[1,128]{1,0:T(1,128)} %bitcast.6), custom_call_target="tpu_custom_call" | custom-call | tf_op jit(solution)/shard_map/split/pallas_call | solution.py:251
  7.5 7.7 %all-to-all-start = ((bf16[32,16,256]{2,1,0:T(8,128)(2,1)}), bf16[32,16,256]{2,1,0:T(8,128)(2,1)S(1)}, u32[]{:S(2)}, u32[]{:S(2)}) async-start(bf16[32,16,256]{2,1,0:T(8,128)(2,1)} %split.1), calls=%async_computation | async-start | bytes 524288 | tf_op jit(solution)/shard_map/all_to_all | solution.py:50
  15.2 0.8 dynamic-slice_convert_fusion
  16.0 0.1 multiply_cosine_fusion
  16.8 0.1 pad_add_fusion.info_ref
  16.9 0.1 pad_maximum_fusion.table_ref
  16.9 0.0 collective-permute-done.2.w3
  16.9 0.0 collective-permute-done.1.w2
  16.9 0.8 collective-permute-done.w1
  17.7 6.4 %all-to-all-done.got_ref = bf16[32,16,256]{2,1,0:T(8,128)(2,1)S(1)} async-done(((bf16[32,16,256]{2,1,0:T(8,128)(2,1)}), bf16[32,16,256]{2,1,0:T(8,128)(2,1)S(1)}, u32[]{:S(2)}, u32[]{:S(2)}) %all-to-all-start) | async-done | bytes 262176 | tf_op jit(solution)/shard_map/all_to_all | solution.py:50
  24.1 0.0 copy-done.1
  24.1 1.4 %project.1 = f32[8,104,128]{2,1,0:T(8,128)S(1)} custom-call(s32[3]{0:T(128)S(1)} %pad_add_fusion.info_ref, bf16[32,16,256]{2,1,0:T(8,128)(2,1)S(1)} %all-to-all-done.got_ref, bf16[128,768]{1,0:T(8,128)(2,1)S(1)} %constant_dynamic-slice_fusion.w0, bf16[128,768]{1,0:T(8,128)(2,1)} %collective-permute-done.w1, bf16[128,768]{1,0:T(8,128)(2,1)S(1)} %collective-permute-done.1.w2, ...), custom_call_target="tpu_custom_call" | custom-call | tf_op jit(solution)/shard_map/project/pallas_call | solution.py:264
  25.5 23.0 %all_to_all.30.mix_ref = f32[8,104,128]{2,1,0:T(8,128)S(1)} all-to-all(f32[8,104,128]{2,1,0:T(8,128)S(1)} %project.1), channel_id=1, replica_groups=mesh['y'=4,'z'=8,'x'=4,'core'=2] {'z'}, dimensions={0} | all-to-all | bytes 851968 | tf_op jit(solution)/shard_map/all_to_all | solution.py:50
  48.5 0.2 turn.1
  48.7 10.4 %all_to_all.31.q_ref = bf16[8,16,512]{2,1,0:T(8,128)(2,1)S(1)} all-to-all(bf16[8,16,512]{2,1,0:T(8,128)(2,1)S(1)} %get-tuple-element.9), channel_id=1, replica_groups=mesh['y'=4,'z'=8,'x'=4,'core'=2] {'z'}, dimensions={0} | all-to-all | bytes 262144 | tf_op jit(solution)/shard_map/all_to_all | solution.py:50
  59.1 1.4 %collective-permute-start.3 = (bf16[8,16,512]{2,1,0:T(8,128)(2,1)S(1)}, bf16[8,16,512]{2,1,0:T(8,128)(2,1)S(1)}, u32[]{:S(2)}, u32[]{:S(2)}) collective-permute-start(bf16[8,16,512]{2,1,0:T(8,128)(2,1)S(1)} %all_to_all.31.q_ref), channel_id=1, source_target_pairs={{0,64},{64,128},{128,192},{192,0},{1,65},{65,129},{129,193},{193,1... | collective-permute-start | bytes 393224 | tf_op jit(solution)/shard_map/ppermute | solution.py:56
  60.5 1.2 collective-permute-start.7
  61.8 1.0 collective-permute-start.5
  62.8 1.3 collective-permute-done.3.q_ref
  64.1 0.0 copy-done.3
  64.1 3.7 %attend.5 = bf16[8,16,640]{2,1,0:T(8,128)(2,1)S(1)} custom-call(s32[3]{0:T(128)S(1)} %pad_add_fusion.info_ref, bf16[8,16,512]{2,1,0:T(8,128)(2,1)S(1)} %collective-permute-done.3.q_ref, bf16[4096,128]{1,0:T(8,128)(2,1)S(1)} %copy-done.1, bf16[4096,128]{1,0:T(8,128)(2,1)S(1)} %copy-done.3, bf16[16,256]{1,0:T(8,128)(2,1)S(1)} %get-tuple-element.10.new_ref), custom_call_target="tpu_custom_call" | custom-call | flops 4000000000 | tf_op jit(solution)/shard_map/attend/pallas_call | solution.py:288
  67.8 1.0 collective-permute-start.4
  68.9 0.0 collective-permute-done.5.q_ref
  68.9 0.0 copy-done.2
  68.9 3.7 %attend.6 = (bf16[512,128]{1,0:T(8,128)(2,1)S(1)}, bf16[8,16,1152]{2,1,0:T(8,128)(2,1)S(1)}) custom-call(s32[3]{0:T(128)S(1)} %pad_add_fusion.info_ref, bf16[8,16,512]{2,1,0:T(8,128)(2,1)S(1)} %collective-permute-done.5.q_ref, bf16[4096,128]{1,0:T(8,128)(2,1)S(1)} %copy-done.1, bf16[4096,128]{1,0:T(8,128)(2,1)S(1)} %copy-done.3, ...), custom_call_target="tpu_custom_call" | custom-call | flops 4000000000 | tf_op jit(solution)/shard_map/attend/pallas_call | solution.py:288
  72.6 0.6 collective-permute-start.9
  73.2 1.9 %collective-permute-start.6 = (bf16[8,16,1152]{2,1,0:T(8,128)(2,1)S(1)}, bf16[8,16,1152]{2,1,0:T(8,128)(2,1)S(1)}, u32[]{:S(2)}, u32[]{:S(2)}) collective-permute-start(bf16[8,16,1152]{2,1,0:T(8,128)(2,1)S(1)} %get-tuple-element.11), channel_id=1, source_target_pairs={{0,128},{64,192},{128,0},{192,64},{1,129},{65,193},{129,1},{193,65... | collective-permute-start | bytes 884744 | tf_op jit(solution)/shard_map/ppermute | solution.py:56
  75.1 0.0 collective-permute-done.7.q_ref
  75.1 3.7 %attend.7 = bf16[8,16,1152]{2,1,0:T(8,128)(2,1)S(1)} custom-call(s32[3]{0:T(128)S(1)} %pad_add_fusion.info_ref, bf16[8,16,512]{2,1,0:T(8,128)(2,1)S(1)} %collective-permute-done.7.q_ref, bf16[4096,128]{1,0:T(8,128)(2,1)S(1)} %copy-done.1, bf16[4096,128]{1,0:T(8,128)(2,1)S(1)} %copy-done.3, bf16[16,256]{1,0:T(8,128)(2,1)S(1)} %get-tuple-element.10.new_ref, ...), custom_call_target="tpu_custom_call" | custom-call | flops 4000000000 | tf_op jit(solution)/shard_map/attend/pallas_call | solution.py:288
  78.8 0.1 collective-permute-start.8
  78.9 3.7 %attend.4.own_ref = bf16[8,16,640]{2,1,0:T(8,128)(2,1)S(1)} custom-call(s32[3]{0:T(128)S(1)} %pad_add_fusion.info_ref, bf16[8,16,512]{2,1,0:T(8,128)(2,1)S(1)} %all_to_all.31.q_ref, bf16[4096,128]{1,0:T(8,128)(2,1)S(1)} %copy-done.1, bf16[4096,128]{1,0:T(8,128)(2,1)S(1)} %copy-done.3, bf16[16,256]{1,0:T(8,128)(2,1)S(1)} %get-tuple-element.10.new_ref), custom_call_target="tpu_custom_call" | custom-call | flops 4000000000 | tf_op jit(solution)/shard_map/attend/pallas_call | solution.py:288
  82.6 0.0 collective-permute-done.9.held_ref.w3
  82.6 0.0 collective-permute-done.4.one_ref
  82.6 0.0 collective-permute-done.6.two_ref
  82.6 5.6 %collective-permute-done.8.three_ref = bf16[8,16,1152]{2,1,0:T(8,128)(2,1)S(1)} collective-permute-done((bf16[8,16,1152]{2,1,0:T(8,128)(2,1)S(1)}, bf16[8,16,1152]{2,1,0:T(8,128)(2,1)S(1)}, u32[]{:S(2)}, u32[]{:S(2)}) %collective-permute-start.8) | collective-permute-done | bytes 294944 | tf_op jit(solution)/shard_map/ppermute | solution.py:56
  88.3 0.5 merge.1
  88.8 10.7 %all_to_all.32.back_ref = bf16[8,16,640]{2,1,0:T(8,128)(2,1)S(1)} all-to-all(bf16[8,16,640]{2,1,0:T(8,128)(2,1)S(1)} %merge.1), channel_id=1, replica_groups=mesh['y'=4,'z'=8,'x'=4,'core'=2] {'z'}, dimensions={0} | all-to-all | bytes 327680 | tf_op jit(solution)/shard_map/all_to_all | solution.py:50
  99.5 0.3 join.1
  99.7 10.3 %all_to_all.33.rows_ref = bf16[8,16,512]{2,1,0:T(8,128)(2,1)S(1)} all-to-all(bf16[8,16,512]{2,1,0:T(8,128)(2,1)S(1)} %join.1), channel_id=1, replica_groups=mesh['y'=4,'z'=8,'x'=4,'core'=2] {'z'}, dimensions={0} | all-to-all | bytes 262144 | tf_op jit(solution)/shard_map/all_to_all | solution.py:50
  110.0 0.8 finish.1
  110.9 19.0 %all_to_all.34 = f32[32,16,128]{2,1,0:T(8,128)S(1)} all-to-all(f32[32,16,128]{2,1,0:T(8,128)S(1)} %finish.1), channel_id=1, replica_groups=mesh['y'=4,'z'=8,'x'=4,'core'=2] {'y','x','core'}, dimensions={0} | all-to-all | bytes 524288 | tf_op jit(solution)/shard_map/all_to_all | solution.py:50
  129.9 0.6 bitcast_reduce_fusion
  (4 shorter events, 0.0 us)
Async XLA Ops:
  0.0 1.4 %copy-start = (bf16[128,6144]{1,0:T(8,128)(2,1)S(1)}, bf16[128,6144]{1,0:T(8,128)(2,1)}, u32[]{:S(2)}) copy-start(bf16[128,6144]{1,0:T(8,128)(2,1)} %param.10) | copy-start | bytes 4718596
  0.0 24.1 %copy-start.1 = (bf16[4096,128]{1,0:T(8,128)(2,1)S(1)}, bf16[4096,128]{1,0:T(8,128)(2,1)}, u32[]{:S(2)}) copy-start(bf16[4096,128]{1,0:T(8,128)(2,1)} %k_ref.9) | copy-start | bytes 3145732
  1.4 15.5 %collective-permute-start.2 = (bf16[128,768]{1,0:T(8,128)(2,1)S(1)}, bf16[128,768]{1,0:T(8,128)(2,1)S(1)}, u32[]{:S(2)}, u32[]{:S(2)}) collective-permute-start(bf16[128,768]{1,0:T(8,128)(2,1)S(1)} %constant_dynamic-slice_fusion.w0), channel_id=1, source_target_pairs={{0,192},{64,0},{128,64},{192,128},{1,193},{65,1},{129,65},{193,129... | collective-permute-start | bytes 589832 | tf_op jit(solution)/shard_map/ppermute | solution.py:56
  5.1 11.9 %collective-permute-start.1 = (bf16[128,768]{1,0:T(8,128)(2,1)S(1)}, bf16[128,768]{1,0:T(8,128)(2,1)S(1)}, u32[]{:S(2)}, u32[]{:S(2)}) collective-permute-start(bf16[128,768]{1,0:T(8,128)(2,1)S(1)} %constant_dynamic-slice_fusion.w0), channel_id=1, source_target_pairs={{0,128},{64,192},{128,0},{192,64},{1,129},{65,193},{129,1},{193,65... | collective-permute-start | bytes 589832 | tf_op jit(solution)/shard_map/ppermute | solution.py:56
  5.4 12.3 %collective-permute-start = (bf16[128,768]{1,0:T(8,128)(2,1)S(1)}, bf16[128,768]{1,0:T(8,128)(2,1)}, u32[]{:S(2)}, u32[]{:S(2)}) collective-permute-start(bf16[128,768]{1,0:T(8,128)(2,1)S(1)} %constant_dynamic-slice_fusion.w0), channel_id=1, source_target_pairs={{0,64},{64,128},{128,192},{192,0},{1,65},{65,129},{129,193},{193,1... | collective-permute-start | bytes 589832 | tf_op jit(solution)/shard_map/ppermute | solution.py:56
  7.5 16.6 %all-to-all-start = ((bf16[32,16,256]{2,1,0:T(8,128)(2,1)}), bf16[32,16,256]{2,1,0:T(8,128)(2,1)S(1)}, u32[]{:S(2)}, u32[]{:S(2)}) async-start(bf16[32,16,256]{2,1,0:T(8,128)(2,1)} %split.1), calls=%async_computation | async-start | bytes 524288 | tf_op jit(solution)/shard_map/all_to_all | solution.py:50
  24.1 40.0 %copy-start.3 = (bf16[4096,128]{1,0:T(8,128)(2,1)S(1)}, bf16[4096,128]{1,0:T(8,128)(2,1)}, u32[]{:S(2)}) copy-start(bf16[4096,128]{1,0:T(8,128)(2,1)} %v_ref.7) | copy-start | bytes 3145732
  59.1 5.0 %collective-permute-start.3 = (bf16[8,16,512]{2,1,0:T(8,128)(2,1)S(1)}, bf16[8,16,512]{2,1,0:T(8,128)(2,1)S(1)}, u32[]{:S(2)}, u32[]{:S(2)}) collective-permute-start(bf16[8,16,512]{2,1,0:T(8,128)(2,1)S(1)} %all_to_all.31.q_ref), channel_id=1, source_target_pairs={{0,64},{64,128},{128,192},{192,0},{1,65},{65,129},{129,193},{193,1... | collective-permute-start | bytes 393224 | tf_op jit(solution)/shard_map/ppermute | solution.py:56
  60.5 14.6 %collective-permute-start.7 = (bf16[8,16,512]{2,1,0:T(8,128)(2,1)S(1)}, bf16[8,16,512]{2,1,0:T(8,128)(2,1)S(1)}, u32[]{:S(2)}, u32[]{:S(2)}) collective-permute-start(bf16[8,16,512]{2,1,0:T(8,128)(2,1)S(1)} %all_to_all.31.q_ref), channel_id=1, source_target_pairs={{0,192},{64,0},{128,64},{192,128},{1,193},{65,1},{129,65},{193,129... | collective-permute-start | bytes 393224 | tf_op jit(solution)/shard_map/ppermute | solution.py:56
  61.8 7.1 %collective-permute-start.5 = (bf16[8,16,512]{2,1,0:T(8,128)(2,1)S(1)}, bf16[8,16,512]{2,1,0:T(8,128)(2,1)S(1)}, u32[]{:S(2)}, u32[]{:S(2)}) collective-permute-start(bf16[8,16,512]{2,1,0:T(8,128)(2,1)S(1)} %all_to_all.31.q_ref), channel_id=1, source_target_pairs={{0,128},{64,192},{128,0},{192,64},{1,129},{65,193},{129,1},{193,65... | collective-permute-start | bytes 393224 | tf_op jit(solution)/shard_map/ppermute | solution.py:56
  64.1 4.7 %copy-start.2 = (bf16[512,128]{1,0:T(8,128)(2,1)S(1)}, bf16[512,128]{1,0:T(8,128)(2,1)}, u32[]{:S(2)}) copy-start(bf16[512,128]{1,0:T(8,128)(2,1)} %w0.1) | copy-start | bytes 393220
  67.8 14.8 %collective-permute-start.4 = (bf16[8,16,640]{2,1,0:T(8,128)(2,1)S(1)}, bf16[8,16,640]{2,1,0:T(8,128)(2,1)S(1)}, u32[]{:S(2)}, u32[]{:S(2)}) collective-permute-start(bf16[8,16,640]{2,1,0:T(8,128)(2,1)S(1)} %attend.5), channel_id=1, source_target_pairs={{0,192},{64,0},{128,64},{192,128},{1,193},{65,1},{129,65},{193,129... | collective-permute-start | bytes 491528 | tf_op jit(solution)/shard_map/ppermute | solution.py:56
  72.6 10.1 %collective-permute-start.9 = (bf16[512,128]{1,0:T(8,128)(2,1)S(1)}, bf16[512,128]{1,0:T(8,128)(2,1)S(1)}, u32[]{:S(2)}, u32[]{:S(2)}) collective-permute-start(bf16[512,128]{1,0:T(8,128)(2,1)S(1)} %get-tuple-element.12), channel_id=1, source_target_pairs={{0,192},{64,0},{128,64},{192,128},{1,193},{65,1},{129,65},{193,129... | collective-permute-start | bytes 393224 | tf_op jit(solution)/shard_map/ppermute | solution.py:56
  73.2 9.4 %collective-permute-start.6 = (bf16[8,16,1152]{2,1,0:T(8,128)(2,1)S(1)}, bf16[8,16,1152]{2,1,0:T(8,128)(2,1)S(1)}, u32[]{:S(2)}, u32[]{:S(2)}) collective-permute-start(bf16[8,16,1152]{2,1,0:T(8,128)(2,1)S(1)} %get-tuple-element.11), channel_id=1, source_target_pairs={{0,128},{64,192},{128,0},{192,64},{1,129},{65,193},{129,1},{193,65... | collective-permute-start | bytes 884744 | tf_op jit(solution)/shard_map/ppermute | solution.py:56
  78.8 9.4 %collective-permute-start.8 = (bf16[8,16,1152]{2,1,0:T(8,128)(2,1)S(1)}, bf16[8,16,1152]{2,1,0:T(8,128)(2,1)S(1)}, u32[]{:S(2)}, u32[]{:S(2)}) collective-permute-start(bf16[8,16,1152]{2,1,0:T(8,128)(2,1)S(1)} %attend.7), channel_id=1, source_target_pairs={{0,64},{64,128},{128,192},{192,0},{1,65},{65,129},{129,193},{193,1... | collective-permute-start | bytes 884744 | tf_op jit(solution)/shard_map/ppermute | solution.py:56

commit v9 on v8

--- a/solution.py
+++ b/solution.py
@@ -121,7 +121,7 @@
 
 def attend_kernel(shift, info_ref, q_ref, k_ref, v_ref, new_ref, *refs):
     o_ref = refs[-1]
-    if len(refs) > 1:
+    if len(refs) > 2:
         w_ref = refs[0]
         for s in range(GROUP):
             piece = w_ref[s * HEAD_DIM : (s + 1) * HEAD_DIM].reshape(ZN, OWN, HEAD_DIM)
@@ -279,24 +279,26 @@
         name="turn",
     )(mix, table)
     queries = exchange(queries, "z")
-    parts = []
-    for shift in range(YN):
+    parts, handed = {}, [w_out]
+    for shift in (2, 3, 1, 0):
         carries = shift in (2, 3)
         outs = [shape((ZN, OWN, RESULT + (FLAT if carries else 0)), bf16)]
-        if shift == 2:
+        if carries:
             outs.insert(0, shape(w_out.shape, bf16))
+        extra = handed[-1:] if shift else [last_columns]
         *passed, part = pl.pallas_call(
             functools.partial(attend_kernel, shift),
-            in_specs=[SMEM] + [VMEM] * (5 if carries else 4),
+            in_specs=[SMEM] + [VMEM] * (4 + len(extra)),
             out_specs=[VMEM for _ in outs],
             out_shape=outs,
             compiler_params=params(24),
-            cost_estimate=pl.CostEstimate(flops=4_000_000_000, bytes_accessed=0, transcendentals=0),
+            cost_estimate=pl.CostEstimate(flops=1000000000, bytes_accessed=0, transcendentals=0),
             name="attend",
-        )(info, along_y(queries, shift), cache_keys, cache_values, new_rows, *([w_out] if carries else []))
-        if passed:
+        )(info, along_y(queries, shift), cache_keys, cache_values, new_rows, *extra)
+        handed.extend(passed)
+        if shift == 2:
             last_columns = along_y(passed[0], 3)
-        parts.append(along_y(part, -shift))
+        parts[shift] = along_y(part, -shift)
     part = pl.pallas_call(
         merge_kernel,
         in_specs=[VMEM] * 5,
@@ -304,7 +306,7 @@
         out_shape=shape((ZN, OWN, FLAT + HEAD_DIM), bf16),
         compiler_params=params(),
         name="merge",
-    )(*parts, last_columns)
+    )(*[parts[shift] for shift in range(YN)], last_columns)
     part = exchange(part, "z")
     rows = pl.pallas_call(
         join_kernel,

time: 131 us -> 132 us (level)
  waiting for transfers between devices: 14.1 us -> 11.5 us
  blocking collectives: 73.4 us -> 75.2 us
  starting transfers between devices: 19.7 us -> 21.4 us
    ppermute x10, waiting for transfers between devices: 7.71 us -> 5.07 us  [along_y(): return lax.ppermute(array, 'y', [(i, (i + shift) % YN) for i in range(YN)])]
    all_to_all x5, blocking collectives: 73.4 us -> 75.2 us  [exchange(): return lax.all_to_all(array, axes, 0, 0, tiled=True)]
    ppermute x10, starting transfers between devices: 12.1 us -> 13.7 us  [along_y(): return lax.ppermute(array, 'y', [(i, (i + shift) % YN) for i in range(YN)])]
  transfers between devices with their start and end apart: 11 -> 11, of which waited for: 4 -> 5; matrix products, arithmetic and copies ran while one was open for 1% -> 1% of each run, Pallas kernels for 12% -> 12%
where the time goes in v9:
time: 132 us; the launch traced here: 131 us
  blocking collectives  75.2 us (57%)
  starting transfers between devices  21.4 us (16%)
  Pallas kernels  19.5 us (15%)
  waiting for transfers between devices  11.5 us (9%)
  other arithmetic  1.66 us (1%)
  local copies, waits for them, and re-layouts  1.43 us (1%)
    all_to_all x5, blocking collectives, exchange(): return lax.all_to_all(array, axes, 0, 0, tiled=True)  75.2 us
    pallas_call x4, Pallas kernels, per_device(): pl.pallas_call(functools.partial(attend_kernel, shift), in_specs=[SMEM] +...  14.8 us
    ppermute x10, starting transfers between devices, along_y(): return lax.ppermute(array, 'y', [(i, (i + shift) % YN) for i in range(YN)])  13.7 us
    all_to_all x1, starting transfers between devices, exchange(): return lax.all_to_all(array, axes, 0, 0, tiled=True)  7.67 us
    all_to_all x1, waiting for transfers between devices, exchange(): return lax.all_to_all(array, axes, 0, 0, tiled=True)  6.4 us
    ppermute x10, waiting for transfers between devices, along_y(): return lax.ppermute(array, 'y', [(i, (i + shift) % YN) for i in range(YN)])  5.07 us
  transfers between devices with their start and end apart: 11, of which 5 were waited for; matrix products, arithmetic and copies ran while one was open for 1% of the time, Pallas kernels for 12%

profile of v9, /device:TPU:1, one launch (start us, length us, event | category | flops | bytes accessed | tf_op | source)
XLA Modules:
  0.0 131.3 jit_solution(339886952534158640)
XLA Ops:
  0.0 0.0 copy-start
  0.0 0.0 copy-start.1
  0.0 1.4 %copy-done = bf16[128,6144]{1,0:T(8,128)(2,1)S(1)} copy-done((bf16[128,6144]{1,0:T(8,128)(2,1)S(1)}, bf16[128,6144]{1,0:T(8,128)(2,1)}, u32[]{:S(2)}) %copy-start) | copy-done | bytes 1572888
  1.4 3.6 %collective-permute-start.2 = (bf16[128,768]{1,0:T(8,128)(2,1)S(1)}, bf16[128,768]{1,0:T(8,128)(2,1)S(1)}, u32[]{:S(2)}, u32[]{:S(2)}) collective-permute-start(bf16[128,768]{1,0:T(8,128)(2,1)S(1)} %constant_dynamic-slice_fusion.w0), channel_id=1, source_target_pairs={{0,192},{64,0},{128,64},{192,128},{1,193},{65,1},{129,65},{193,129... | collective-permute-start | bytes 589832 | tf_op jit(solution)/shard_map/ppermute | solution.py:56
  5.1 0.3 collective-permute-start.1
  5.4 0.7 collective-permute-start
  6.1 1.4 %split.1 = bf16[32,16,256]{2,1,0:T(8,128)(2,1)} custom-call(bf16[64,128]{1,0:T(8,128)(2,1)} %hidden_ref.1, f32[1,128]{1,0:T(1,128)} %bitcast.6), custom_call_target="tpu_custom_call" | custom-call | tf_op jit(solution)/shard_map/split/pallas_call | solution.py:251
  7.5 7.7 %all-to-all-start = ((bf16[32,16,256]{2,1,0:T(8,128)(2,1)}), bf16[32,16,256]{2,1,0:T(8,128)(2,1)S(1)}, u32[]{:S(2)}, u32[]{:S(2)}) async-start(bf16[32,16,256]{2,1,0:T(8,128)(2,1)} %split.1), calls=%async_computation | async-start | bytes 524288 | tf_op jit(solution)/shard_map/all_to_all | solution.py:50
  15.2 0.8 dynamic-slice_convert_fusion
  16.0 0.1 multiply_cosine_fusion
  16.8 0.1 pad_add_fusion.info_ref
  16.9 0.1 pad_maximum_fusion.table_ref
  16.9 0.0 collective-permute-done.2.w3
  16.9 0.0 collective-permute-done.1.w2
  16.9 0.8 collective-permute-done.w1
  17.7 6.4 %all-to-all-done.got_ref = bf16[32,16,256]{2,1,0:T(8,128)(2,1)S(1)} async-done(((bf16[32,16,256]{2,1,0:T(8,128)(2,1)}), bf16[32,16,256]{2,1,0:T(8,128)(2,1)S(1)}, u32[]{:S(2)}, u32[]{:S(2)}) %all-to-all-start) | async-done | bytes 262176 | tf_op jit(solution)/shard_map/all_to_all | solution.py:50
  24.1 0.0 copy-done.1
  24.1 1.4 %project.1 = f32[8,104,128]{2,1,0:T(8,128)S(1)} custom-call(s32[3]{0:T(128)S(1)} %pad_add_fusion.info_ref, bf16[32,16,256]{2,1,0:T(8,128)(2,1)S(1)} %all-to-all-done.got_ref, bf16[128,768]{1,0:T(8,128)(2,1)S(1)} %constant_dynamic-slice_fusion.w0, bf16[128,768]{1,0:T(8,128)(2,1)} %collective-permute-done.w1, bf16[128,768]{1,0:T(8,128)(2,1)S(1)} %collective-permute-done.1.w2, ...), custom_call_target="tpu_custom_call" | custom-call | tf_op jit(solution)/shard_map/project/pallas_call | solution.py:264
  25.5 22.9 %all_to_all.30.mix_ref = f32[8,104,128]{2,1,0:T(8,128)S(1)} all-to-all(f32[8,104,128]{2,1,0:T(8,128)S(1)} %project.1), channel_id=1, replica_groups=mesh['y'=4,'z'=8,'x'=4,'core'=2] {'z'}, dimensions={0} | all-to-all | bytes 851968 | tf_op jit(solution)/shard_map/all_to_all | solution.py:50
  48.5 0.2 turn.1
  48.7 10.4 %all_to_all.31.q_ref = bf16[8,16,512]{2,1,0:T(8,128)(2,1)S(1)} all-to-all(bf16[8,16,512]{2,1,0:T(8,128)(2,1)S(1)} %get-tuple-element.11), channel_id=1, replica_groups=mesh['y'=4,'z'=8,'x'=4,'core'=2] {'z'}, dimensions={0} | all-to-all | bytes 262144 | tf_op jit(solution)/shard_map/all_to_all | solution.py:50
  59.1 2.3 %collective-permute-start.3 = (bf16[8,16,512]{2,1,0:T(8,128)(2,1)S(1)}, bf16[8,16,512]{2,1,0:T(8,128)(2,1)S(1)}, u32[]{:S(2)}, u32[]{:S(2)}) collective-permute-start(bf16[8,16,512]{2,1,0:T(8,128)(2,1)S(1)} %all_to_all.31.q_ref), channel_id=1, source_target_pairs={{0,128},{64,192},{128,0},{192,64},{1,129},{65,193},{129,1},{193,65... | collective-permute-start | bytes 393224 | tf_op jit(solution)/shard_map/ppermute | solution.py:56
  61.4 1.6 %collective-permute-start.6 = (bf16[8,16,512]{2,1,0:T(8,128)(2,1)S(1)}, bf16[8,16,512]{2,1,0:T(8,128)(2,1)S(1)}, u32[]{:S(2)}, u32[]{:S(2)}) collective-permute-start(bf16[8,16,512]{2,1,0:T(8,128)(2,1)S(1)} %all_to_all.31.q_ref), channel_id=1, source_target_pairs={{0,192},{64,0},{128,64},{192,128},{1,193},{65,1},{129,65},{193,129... | collective-permute-start | bytes 393224 | tf_op jit(solution)/shard_map/ppermute | solution.py:56
  62.9 0.0 collective-permute-start.5
  63.0 1.5 %collective-permute-done.3.q_ref = bf16[8,16,512]{2,1,0:T(8,128)(2,1)S(1)} collective-permute-done((bf16[8,16,512]{2,1,0:T(8,128)(2,1)S(1)}, bf16[8,16,512]{2,1,0:T(8,128)(2,1)S(1)}, u32[]{:S(2)}, u32[]{:S(2)}) %collective-permute-start.3) | collective-permute-done | bytes 131104 | tf_op jit(solution)/shard_map/ppermute | solution.py:56
  64.4 0.0 copy-done.2
  64.4 0.0 copy-done.3
  64.4 3.7 %attend.4 = (bf16[512,128]{1,0:T(8,128)(2,1)S(1)}, bf16[8,16,1152]{2,1,0:T(8,128)(2,1)S(1)}) custom-call(s32[3]{0:T(128)S(1)} %pad_add_fusion.info_ref, bf16[8,16,512]{2,1,0:T(8,128)(2,1)S(1)} %collective-permute-done.3.q_ref, bf16[4096,128]{1,0:T(8,128)(2,1)S(1)} %copy-done.1, bf16[4096,128]{1,0:T(8,128)(2,1)S(1)} %copy-done.3, ...), custom_call_target="tpu_custom_call" | custom-call | flops 1000000000 | tf_op jit(solution)/shard_map/attend/pallas_call | solution.py:289
  68.1 0.0 collective-permute-done.6.q_ref
  68.1 3.7 %attend.6 = (bf16[512,128]{1,0:T(8,128)(2,1)S(1)}, bf16[8,16,1152]{2,1,0:T(8,128)(2,1)S(1)}) custom-call(s32[3]{0:T(128)S(1)} %pad_add_fusion.info_ref, bf16[8,16,512]{2,1,0:T(8,128)(2,1)S(1)} %collective-permute-done.6.q_ref, bf16[4096,128]{1,0:T(8,128)(2,1)S(1)} %copy-done.1, bf16[4096,128]{1,0:T(8,128)(2,1)S(1)} %copy-done.3, ...), custom_call_target="tpu_custom_call" | custom-call | flops 1000000000 | tf_op jit(solution)/shard_map/attend/pallas_call | solution.py:289
  71.9 1.8 %collective-permute-start.9 = (bf16[8,16,1152]{2,1,0:T(8,128)(2,1)S(1)}, bf16[8,16,1152]{2,1,0:T(8,128)(2,1)S(1)}, u32[]{:S(2)}, u32[]{:S(2)}) collective-permute-start(bf16[8,16,1152]{2,1,0:T(8,128)(2,1)S(1)} %get-tuple-element.16), channel_id=1, source_target_pairs={{0,64},{64,128},{128,192},{192,0},{1,65},{65,129},{129,193},{193,1... | collective-permute-start | bytes 884744 | tf_op jit(solution)/shard_map/ppermute | solution.py:56
  73.7 1.6 %collective-permute-start.8 = (bf16[8,16,1152]{2,1,0:T(8,128)(2,1)S(1)}, bf16[8,16,1152]{2,1,0:T(8,128)(2,1)S(1)}, u32[]{:S(2)}, u32[]{:S(2)}) collective-permute-start(bf16[8,16,1152]{2,1,0:T(8,128)(2,1)S(1)} %get-tuple-element.15), channel_id=1, source_target_pairs={{0,128},{64,192},{128,0},{192,64},{1,129},{65,193},{129,1},{193,65... | collective-permute-start | bytes 884744 | tf_op jit(solution)/shard_map/ppermute | solution.py:56
  75.3 1.3 collective-permute-start.4
  76.5 0.0 collective-permute-done.5.q_ref
  76.5 3.7 %attend.7 = bf16[8,16,640]{2,1,0:T(8,128)(2,1)S(1)} custom-call(s32[3]{0:T(128)S(1)} %pad_add_fusion.info_ref, bf16[8,16,512]{2,1,0:T(8,128)(2,1)S(1)} %collective-permute-done.5.q_ref, bf16[4096,128]{1,0:T(8,128)(2,1)S(1)} %copy-done.1, bf16[4096,128]{1,0:T(8,128)(2,1)S(1)} %copy-done.3, bf16[16,256]{1,0:T(8,128)(2,1)S(1)} %get-tuple-element.12.new_ref, ...), custom_call_target="tpu_custom_call" | custom-call | flops 1000000000 | tf_op jit(solution)/shard_map/attend/pallas_call | solution.py:289
  80.2 0.5 collective-permute-start.7
  80.7 0.5 collective-permute-done.4.refs_0_.held_ref.w3
  81.2 3.7 %attend.5.own_ref = bf16[8,16,640]{2,1,0:T(8,128)(2,1)S(1)} custom-call(s32[3]{0:T(128)S(1)} %pad_add_fusion.info_ref, bf16[8,16,512]{2,1,0:T(8,128)(2,1)S(1)} %all_to_all.31.q_ref, bf16[4096,128]{1,0:T(8,128)(2,1)S(1)} %copy-done.1, bf16[4096,128]{1,0:T(8,128)(2,1)S(1)} %copy-done.3, bf16[16,256]{1,0:T(8,128)(2,1)S(1)} %get-tuple-element.12.new_ref, ...), custom_call_target="tpu_custom_call" | custom-call | flops 1000000000 | tf_op jit(solution)/shard_map/attend/pallas_call | solution.py:289
  84.9 2.3 %collective-permute-done.7.one_ref = bf16[8,16,640]{2,1,0:T(8,128)(2,1)S(1)} collective-permute-done((bf16[8,16,640]{2,1,0:T(8,128)(2,1)S(1)}, bf16[8,16,640]{2,1,0:T(8,128)(2,1)S(1)}, u32[]{:S(2)}, u32[]{:S(2)}) %collective-permute-start.7) | collective-permute-done | bytes 163872 | tf_op jit(solution)/shard_map/ppermute | solution.py:56
  87.2 0.0 collective-permute-done.9.three_ref
  87.2 0.0 collective-permute-done.8.two_ref
  87.2 0.6 merge.1
  87.8 10.7 %all_to_all.32.back_ref = bf16[8,16,640]{2,1,0:T(8,128)(2,1)S(1)} all-to-all(bf16[8,16,640]{2,1,0:T(8,128)(2,1)S(1)} %merge.1), channel_id=1, replica_groups=mesh['y'=4,'z'=8,'x'=4,'core'=2] {'z'}, dimensions={0} | all-to-all | bytes 327680 | tf_op jit(solution)/shard_map/all_to_all | solution.py:50
  98.4 0.3 join.1
  98.7 10.3 %all_to_all.33.rows_ref = bf16[8,16,512]{2,1,0:T(8,128)(2,1)S(1)} all-to-all(bf16[8,16,512]{2,1,0:T(8,128)(2,1)S(1)} %join.1), channel_id=1, replica_groups=mesh['y'=4,'z'=8,'x'=4,'core'=2] {'z'}, dimensions={0} | all-to-all | bytes 262144 | tf_op jit(solution)/shard_map/all_to_all | solution.py:50
  109.0 0.8 finish.1
  109.8 20.9 %all_to_all.34 = f32[32,16,128]{2,1,0:T(8,128)S(1)} all-to-all(f32[32,16,128]{2,1,0:T(8,128)S(1)} %finish.1), channel_id=1, replica_groups=mesh['y'=4,'z'=8,'x'=4,'core'=2] {'y','x','core'}, dimensions={0} | all-to-all | bytes 524288 | tf_op jit(solution)/shard_map/all_to_all | solution.py:50
  130.7 0.6 bitcast_reduce_fusion
  (4 shorter events, 0.0 us)
Async XLA Ops:
  0.0 1.4 %copy-start = (bf16[128,6144]{1,0:T(8,128)(2,1)S(1)}, bf16[128,6144]{1,0:T(8,128)(2,1)}, u32[]{:S(2)}) copy-start(bf16[128,6144]{1,0:T(8,128)(2,1)} %param.10) | copy-start | bytes 4718596
  0.0 24.1 %copy-start.1 = (bf16[4096,128]{1,0:T(8,128)(2,1)S(1)}, bf16[4096,128]{1,0:T(8,128)(2,1)}, u32[]{:S(2)}) copy-start(bf16[4096,128]{1,0:T(8,128)(2,1)} %k_ref.9) | copy-start | bytes 3145732
  1.4 15.5 %collective-permute-start.2 = (bf16[128,768]{1,0:T(8,128)(2,1)S(1)}, bf16[128,768]{1,0:T(8,128)(2,1)S(1)}, u32[]{:S(2)}, u32[]{:S(2)}) collective-permute-start(bf16[128,768]{1,0:T(8,128)(2,1)S(1)} %constant_dynamic-slice_fusion.w0), channel_id=1, source_target_pairs={{0,192},{64,0},{128,64},{192,128},{1,193},{65,1},{129,65},{193,129... | collective-permute-start | bytes 589832 | tf_op jit(solution)/shard_map/ppermute | solution.py:56
  5.1 11.9 %collective-permute-start.1 = (bf16[128,768]{1,0:T(8,128)(2,1)S(1)}, bf16[128,768]{1,0:T(8,128)(2,1)S(1)}, u32[]{:S(2)}, u32[]{:S(2)}) collective-permute-start(bf16[128,768]{1,0:T(8,128)(2,1)S(1)} %constant_dynamic-slice_fusion.w0), channel_id=1, source_target_pairs={{0,128},{64,192},{128,0},{192,64},{1,129},{65,193},{129,1},{193,65... | collective-permute-start | bytes 589832 | tf_op jit(solution)/shard_map/ppermute | solution.py:56
  5.4 12.3 %collective-permute-start = (bf16[128,768]{1,0:T(8,128)(2,1)S(1)}, bf16[128,768]{1,0:T(8,128)(2,1)}, u32[]{:S(2)}, u32[]{:S(2)}) collective-permute-start(bf16[128,768]{1,0:T(8,128)(2,1)S(1)} %constant_dynamic-slice_fusion.w0), channel_id=1, source_target_pairs={{0,64},{64,128},{128,192},{192,0},{1,65},{65,129},{129,193},{193,1... | collective-permute-start | bytes 589832 | tf_op jit(solution)/shard_map/ppermute | solution.py:56
  7.5 16.6 %all-to-all-start = ((bf16[32,16,256]{2,1,0:T(8,128)(2,1)}), bf16[32,16,256]{2,1,0:T(8,128)(2,1)S(1)}, u32[]{:S(2)}, u32[]{:S(2)}) async-start(bf16[32,16,256]{2,1,0:T(8,128)(2,1)} %split.1), calls=%async_computation | async-start | bytes 524288 | tf_op jit(solution)/shard_map/all_to_all | solution.py:50
  24.1 40.3 %copy-start.2 = (bf16[512,128]{1,0:T(8,128)(2,1)S(1)}, bf16[512,128]{1,0:T(8,128)(2,1)}, u32[]{:S(2)}) copy-start(bf16[512,128]{1,0:T(8,128)(2,1)} %w0.1) | copy-start | bytes 393220
  24.1 40.3 %copy-start.3 = (bf16[4096,128]{1,0:T(8,128)(2,1)S(1)}, bf16[4096,128]{1,0:T(8,128)(2,1)}, u32[]{:S(2)}) copy-start(bf16[4096,128]{1,0:T(8,128)(2,1)} %v_ref.7) | copy-start | bytes 3145732
  59.1 5.3 %collective-permute-start.3 = (bf16[8,16,512]{2,1,0:T(8,128)(2,1)S(1)}, bf16[8,16,512]{2,1,0:T(8,128)(2,1)S(1)}, u32[]{:S(2)}, u32[]{:S(2)}) collective-permute-start(bf16[8,16,512]{2,1,0:T(8,128)(2,1)S(1)} %all_to_all.31.q_ref), channel_id=1, source_target_pairs={{0,128},{64,192},{128,0},{192,64},{1,129},{65,193},{129,1},{193,65... | collective-permute-start | bytes 393224 | tf_op jit(solution)/shard_map/ppermute | solution.py:56
  61.4 6.8 %collective-permute-start.6 = (bf16[8,16,512]{2,1,0:T(8,128)(2,1)S(1)}, bf16[8,16,512]{2,1,0:T(8,128)(2,1)S(1)}, u32[]{:S(2)}, u32[]{:S(2)}) collective-permute-start(bf16[8,16,512]{2,1,0:T(8,128)(2,1)S(1)} %all_to_all.31.q_ref), channel_id=1, source_target_pairs={{0,192},{64,0},{128,64},{192,128},{1,193},{65,1},{129,65},{193,129... | collective-permute-start | bytes 393224 | tf_op jit(solution)/shard_map/ppermute | solution.py:56
  62.9 13.6 %collective-permute-start.5 = (bf16[8,16,512]{2,1,0:T(8,128)(2,1)S(1)}, bf16[8,16,512]{2,1,0:T(8,128)(2,1)S(1)}, u32[]{:S(2)}, u32[]{:S(2)}) collective-permute-start(bf16[8,16,512]{2,1,0:T(8,128)(2,1)S(1)} %all_to_all.31.q_ref), channel_id=1, source_target_pairs={{0,64},{64,128},{128,192},{192,0},{1,65},{65,129},{129,193},{193,1... | collective-permute-start | bytes 393224 | tf_op jit(solution)/shard_map/ppermute | solution.py:56
  71.9 15.4 %collective-permute-start.9 = (bf16[8,16,1152]{2,1,0:T(8,128)(2,1)S(1)}, bf16[8,16,1152]{2,1,0:T(8,128)(2,1)S(1)}, u32[]{:S(2)}, u32[]{:S(2)}) collective-permute-start(bf16[8,16,1152]{2,1,0:T(8,128)(2,1)S(1)} %get-tuple-element.16), channel_id=1, source_target_pairs={{0,64},{64,128},{128,192},{192,0},{1,65},{65,129},{129,193},{193,1... | collective-permute-start | bytes 884744 | tf_op jit(solution)/shard_map/ppermute | solution.py:56
  73.7 13.5 %collective-permute-start.8 = (bf16[8,16,1152]{2,1,0:T(8,128)(2,1)S(1)}, bf16[8,16,1152]{2,1,0:T(8,128)(2,1)S(1)}, u32[]{:S(2)}, u32[]{:S(2)}) collective-permute-start(bf16[8,16,1152]{2,1,0:T(8,128)(2,1)S(1)} %get-tuple-element.15), channel_id=1, source_target_pairs={{0,128},{64,192},{128,0},{192,64},{1,129},{65,193},{129,1},{193,65... | collective-permute-start | bytes 884744 | tf_op jit(solution)/shard_map/ppermute | solution.py:56
  75.3 5.9 %collective-permute-start.4 = (bf16[512,128]{1,0:T(8,128)(2,1)S(1)}, bf16[512,128]{1,0:T(8,128)(2,1)S(1)}, u32[]{:S(2)}, u32[]{:S(2)}) collective-permute-start(bf16[512,128]{1,0:T(8,128)(2,1)S(1)} %get-tuple-element.13.refs_0_), channel_id=1, source_target_pairs={{0,192},{64,0},{128,64},{192,128},{1,193},{65,1},{129,65},{193,129... | collective-permute-start | bytes 393224 | tf_op jit(solution)/shard_map/ppermute | solution.py:56
  80.2 7.0 %collective-permute-start.7 = (bf16[8,16,640]{2,1,0:T(8,128)(2,1)S(1)}, bf16[8,16,640]{2,1,0:T(8,128)(2,1)S(1)}, u32[]{:S(2)}, u32[]{:S(2)}) collective-permute-start(bf16[8,16,640]{2,1,0:T(8,128)(2,1)S(1)} %attend.7), channel_id=1, source_target_pairs={{0,192},{64,0},{128,64},{192,128},{1,193},{65,1},{129,65},{193,129... | collective-permute-start | bytes 491528 | tf_op jit(solution)/shard_map/ppermute | solution.py:56
